TPU v7x, 32 devices: a whole 2x2x4 slice. The times are simulated.
32 devices in a mesh: groups: 2 (over y), pair: 4 (over z), aux: 2 (over x), occ: 2 (over core).
Axes of the slice: x: 2, y: 2, z: 4, core: 2. Of those that a mesh axis runs over, the one named last changes fastest.
Arguments:
- three_index: bfloat16 [48, 20480, 256], P(('groups', 'pair', 'occ'), 'aux'), parts along dimension 0, may hold values from -1.25 to 1.25
- pair_orbs: int32 [128, 2], P('groups'), parts along dimension 0, may hold values from 0 to 23, as said below
- live_pairs: int32 [16], P('groups'), parts along dimension 0, may hold values from 1 to 8, as said below
- domains: int32 [48, 256], P('groups'), parts along dimension 0, may hold values from 0 to 1791, as said below
- coupled: int32 [128, 4], P(('groups', 'pair', 'occ')), parts along dimension 0, may hold values from 0 to 63, as said below
- fock_coupling_weight: float32 [128, 4], P(('groups', 'pair', 'occ')), parts along dimension 0, may hold values from -4 to 4
- occ_energy: float32 [48], P('groups'), parts along dimension 0, may hold values from -1.2 to -0.3
- virt_energy: float32 [3584], P('groups'), parts along dimension 0, may hold values from 0.4 to 4
Outputs:
- amplitudes: bfloat16 [128, 256, 256], P(('groups', 'pair', 'occ')), parts along dimension 0
There are 2 independent parts, one for each index of `groups`. A program takes and returns all parts, laid end to end along the dimension named above; each array names one. Nothing has to cross between parts.
Inputs may be any that keep to these rules, and one draw needn't show every extreme that they name: pair_orbs[s, 0] is an orbital of owner s // 8 (orbitals o * 3 to o * 3 + 2 belong to owner o); pair_orbs[s, 1] differs from it and belongs to the same owner or to one of the two owners beside it; pairs may repeat. The live slots of an owner are its first live_pairs[o] slots; some owner has all 8 slots live. `domains`: each row holds 256 distinct virtual indices. `coupled`: each entry is a live slot of the same owner or of one of the two owners beside it.
All inputs are finite; a program needn't handle non-finite values.
Results may differ from a plain program's by a relative error of at most 0.0045.
Values may be sent and summed in bfloat16 or wider, within the bound.
No kernel may reach another device: no remote copies, remote signals or barrier semaphores. Data moves between devices by JAX's collectives and lax.ppermute only.
A program may use at most 192 MiB of HBM per device.

v0:
```python
import jax
import jax.numpy as jnp
from jax import lax
from jax.sharding import PartitionSpec as P

ITERS = 2


def extended_2(cells, sides, width):
    for axis, dim in sides:
        count = lax.axis_size(axis)
        ends = count - 1
        head = lax.slice_in_dim(cells, 0, width, axis=dim)
        tail = lax.slice_in_dim(cells, cells.shape[dim] - width, cells.shape[dim], axis=dim)
        cells = jnp.concatenate(
            [
                lax.ppermute(tail, axis, [(i, (i + 1) % count) for i in range(ends)]),
                cells,
                lax.ppermute(head, axis, [((i + 1) % count, i) for i in range(ends)]),
            ],
            axis=dim,
        )
    return cells


def energy_gaps(row_orbitals, col_orbs, domains, occ_energy, virt_energy):
    row_energy = virt_energy[domains[row_orbitals]]
    col_energy = virt_energy[domains[col_orbs]]
    return (
        row_energy[:, :, None]
        + col_energy[:, None, :]
        - occ_energy[row_orbitals][:, None, None]
        - occ_energy[col_orbs][:, None, None]
    )


def neighbour_view(rounded):
    return extended_2(rounded, ((("pair", "occ"), 0),), rounded.shape[0])


def on_device(
    three_index,
    pair_orbs,
    live_pairs,
    domains,
    coupled,
    fock_coupling_weight,
    occ_energy,
    virt_energy,
):
    orb_dev = three_index.shape[0]
    slots_dev = coupled.shape[0]
    dom_width = three_index.shape[2]
    owner_id = lax.axis_index(("pair", "occ"))
    owner_base = owner_id * slots_dev
    first_orb = (owner_id - 1) * orb_dev
    first_slot = (owner_id - 1) * slots_dev
    live_count = live_pairs[owner_id]
    blocks = extended_2(three_index, ((("pair", "occ"), 0),), orb_dev)
    owner_slots = owner_base + jnp.arange(slots_dev, dtype=jnp.int32)
    left_local = pair_orbs[owner_slots, 0] - first_orb
    right_local = pair_orbs[owner_slots, 1] - first_orb

    def integral(position):

        def compute():
            left_block = lax.dynamic_index_in_dim(blocks, left_local[position], 0, keepdims=False)
            right_block = lax.dynamic_index_in_dim(blocks, right_local[position], 0, keepdims=False)
            return lax.dot_general(
                left_block,
                right_block,
                (((0,), (0,)), ((), ())),
                preferred_element_type=jnp.float32,
            )

        def skip():
            return jnp.zeros((dom_width, dom_width), jnp.float32)

        return lax.cond(position < live_count, compute, skip)

    partials = lax.map(integral, jnp.arange(slots_dev, dtype=jnp.int32))
    integrals = lax.psum(partials, "aux")
    own_local = jnp.arange(slots_dev, dtype=jnp.int32)
    slot_indices = owner_base + own_local
    live_mask = (own_local < live_count).astype(jnp.float32)[:, None, None]
    row_orbitals = pair_orbs[slot_indices, 0]
    col_orbs = pair_orbs[slot_indices, 1]
    row_dom = domains[row_orbitals]
    col_dom = domains[col_orbs]
    sources = coupled[own_local]
    source_rows = domains[pair_orbs[sources, 0]]
    source_cols = domains[pair_orbs[sources, 1]]
    row_match = (row_dom[:, None, :, None] == source_rows[:, :, None, :]).astype(jnp.bfloat16)
    col_match = (source_cols[:, :, :, None] == col_dom[:, None, None, :]).astype(jnp.bfloat16)
    weights = fock_coupling_weight[own_local]
    source_local = sources - first_slot
    denominators = energy_gaps(row_orbitals, col_orbs, domains, occ_energy, virt_energy)
    amplitudes = -integrals / denominators
    for sweep in range(ITERS):
        rounded = amplitudes.astype(jnp.bfloat16)
        extended = neighbour_view(rounded)
        picked = extended[source_local]
        selected = jnp.einsum(
            "snac,sncd->snad", row_match, picked, preferred_element_type=jnp.float32
        ).astype(jnp.bfloat16)
        products = jnp.einsum(
            "snad,sndb->snab", selected, col_match, preferred_element_type=jnp.float32
        )
        coupling = jnp.sum(weights[:, :, None, None] * products, axis=1)
        amplitudes = live_mask * (coupling - integrals) / denominators
    return amplitudes.astype(jnp.bfloat16)


def solution(mesh):
    return jax.shard_map(
        on_device,
        mesh=mesh,
        in_specs=(
            P(("groups", "pair", "occ"), "aux", None),
            P("groups", None),
            P("groups"),
            P("groups", None),
            P(("groups", "pair", "occ"), None),
            P(("groups", "pair", "occ"), None),
            P("groups"),
            P("groups"),
        ),
        out_specs=P(("groups", "pair", "occ"), None, None),
        check_vma=False,
    )
```

profile of v0, /device:TPU:1, one launch (start us, length us, event | category | flops | bytes accessed | tf_op | source)
XLA Modules:
  0.0 476.1 jit_solution(11908281129953937022)
XLA Ops:
  6.5 4.7 collective-permute-start
  11.3 5.2 %collective-permute-start.1 = (bf16[3,10240,256]{2,1,0:T(8,128)(2,1)}, bf16[3,10240,256]{2,1,0:T(8,128)(2,1)}, u32[]{:S(2)}, u32[]{:S(2)}) collective-permute-start(bf16[3,10240,256]{2,1,0:T(8,128)(2,1)} %param.12), channel_id=1, source_target_pairs={{1,0},{4,1},{5,4},{8,5},{9,8},{12,9},{13,12},{3,2},{6,3},{7,6},{10... | collective-permute-start | bytes 47185928 | tf_op jit(solution)/shard_map/ppermute | solution.py:19
  20.5 160.1 %collective-permute-done = bf16[3,10240,256]{2,1,0:T(8,128)(2,1)} collective-permute-done((bf16[3,10240,256]{2,1,0:T(8,128)(2,1)}, bf16[3,10240,256]{2,1,0:T(8,128)(2,1)}, u32[]{:S(2)}, u32[]{:S(2)}) %collective-permute-start) | collective-permute-done | bytes 15728672 | tf_op jit(solution)/shard_map/ppermute | solution.py:17
  185.0 31.7 %pad_maximum_fusion = bf16[9,10240,256]{2,1,0:T(8,128)(2,1)} fusion(bf16[3,10240,256]{2,1,0:T(8,128)(2,1)} %collective-permute-done.1, bf16[3,10240,256]{2,1,0:T(8,128)(2,1)} %param.12, bf16[3,10240,256]{2,1,0:T(8,128)(2,1)} %collective-permute-done), kind=kLoop, calls=%fused_computation.24 | loop fusion | flops 47185920 | bytes 94371840 | tf_op jit(solution)/shard_map/concatenate | solution.py:15
  216.8 95.6 %while.10 = (s32[]{:T(128)}, f32[8,256,256]{2,1,0:T(8,128)}, s32[8]{0:T(128)S(1)}, s32[]{:T(128)}, s32[8]{0:T(128)S(1)}, /*index=5*/bf16[9,10240,256]{2,1,0:T(8,128)(2,1)}, s32[8]{0:T(128)S(1)}, s32[]{:T(128)}) while((s32[]{:T(128)}, f32[8,256,256]{2,1,0:T(8,128)}, s32[8]{0:T(128)S(1)}, s32[]{:T(128)}, s32[8]{0:T(128)S(1)}, ...), condition=%wide.region_3.4_spmd, body=%wide.region_0.3_spmd.sunk | while | flops 1342177280 | bytes 11272989 | solution.py:81
  218.8 12.2 %conditional.2 = (f32[1,256,256]{2,1,0:T(8,128)S(1)}) conditional(s32[]{:T(128)} %convert_element_type.46, () %tuple.31, (s32[]{:T(128)}, s32[8]{0:T(128)S(1)}, bf16[9,10240,256]{2,1,0:T(8,128)(2,1)}, s32[8]{0:T(128)S(1)}) %tuple.32), branch_computations={%region_1.1_spmd, %region_2.2_spmd} | conditional | flops 1342177280 | bytes 10748046 | solution.py:79
  225.4 5.6 %fusion.5 = f32[1,256,256]{2,1,0:T(8,128)S(1)} fusion(bf16[9,10240,256]{2,1,0:T(8,128)(2,1)} %get-tuple-element.45, s32[]{:T(128)S(6)} %select_n.104, s32[]{:T(128)S(6)} %select_n.103), kind=kOutput, calls=%fused_computation.21 | convolution fusion | flops 1342177280 | bytes 10747912 | tf_op jit(solution)/shard_map/while/body/eval_jaxpr/cond/branch_1_fun/dot_general | solution.py:69
  233.8 12.2 %conditional.2 = (f32[1,256,256]{2,1,0:T(8,128)S(1)}) conditional(s32[]{:T(128)} %convert_element_type.46, () %tuple.31, (s32[]{:T(128)}, s32[8]{0:T(128)S(1)}, bf16[9,10240,256]{2,1,0:T(8,128)(2,1)}, s32[8]{0:T(128)S(1)}) %tuple.32), branch_computations={%region_1.1_spmd, %region_2.2_spmd} | conditional | flops 1342177280 | bytes 10748046 | solution.py:79
  240.4 5.6 %fusion.5 = f32[1,256,256]{2,1,0:T(8,128)S(1)} fusion(bf16[9,10240,256]{2,1,0:T(8,128)(2,1)} %get-tuple-element.45, s32[]{:T(128)S(6)} %select_n.104, s32[]{:T(128)S(6)} %select_n.103), kind=kOutput, calls=%fused_computation.21 | convolution fusion | flops 1342177280 | bytes 10747912 | tf_op jit(solution)/shard_map/while/body/eval_jaxpr/cond/branch_1_fun/dot_general | solution.py:69
  248.8 12.2 %conditional.2 = (f32[1,256,256]{2,1,0:T(8,128)S(1)}) conditional(s32[]{:T(128)} %convert_element_type.46, () %tuple.31, (s32[]{:T(128)}, s32[8]{0:T(128)S(1)}, bf16[9,10240,256]{2,1,0:T(8,128)(2,1)}, s32[8]{0:T(128)S(1)}) %tuple.32), branch_computations={%region_1.1_spmd, %region_2.2_spmd} | conditional | flops 1342177280 | bytes 10748046 | solution.py:79
  255.4 5.6 %fusion.5 = f32[1,256,256]{2,1,0:T(8,128)S(1)} fusion(bf16[9,10240,256]{2,1,0:T(8,128)(2,1)} %get-tuple-element.45, s32[]{:T(128)S(6)} %select_n.104, s32[]{:T(128)S(6)} %select_n.103), kind=kOutput, calls=%fused_computation.21 | convolution fusion | flops 1342177280 | bytes 10747912 | tf_op jit(solution)/shard_map/while/body/eval_jaxpr/cond/branch_1_fun/dot_general | solution.py:69
  263.8 12.2 %conditional.2 = (f32[1,256,256]{2,1,0:T(8,128)S(1)}) conditional(s32[]{:T(128)} %convert_element_type.46, () %tuple.31, (s32[]{:T(128)}, s32[8]{0:T(128)S(1)}, bf16[9,10240,256]{2,1,0:T(8,128)(2,1)}, s32[8]{0:T(128)S(1)}) %tuple.32), branch_computations={%region_1.1_spmd, %region_2.2_spmd} | conditional | flops 1342177280 | bytes 10748046 | solution.py:79
  270.4 5.6 %fusion.5 = f32[1,256,256]{2,1,0:T(8,128)S(1)} fusion(bf16[9,10240,256]{2,1,0:T(8,128)(2,1)} %get-tuple-element.45, s32[]{:T(128)S(6)} %select_n.104, s32[]{:T(128)S(6)} %select_n.103), kind=kOutput, calls=%fused_computation.21 | convolution fusion | flops 1342177280 | bytes 10747912 | tf_op jit(solution)/shard_map/while/body/eval_jaxpr/cond/branch_1_fun/dot_general | solution.py:69
  278.8 12.2 %conditional.2 = (f32[1,256,256]{2,1,0:T(8,128)S(1)}) conditional(s32[]{:T(128)} %convert_element_type.46, () %tuple.31, (s32[]{:T(128)}, s32[8]{0:T(128)S(1)}, bf16[9,10240,256]{2,1,0:T(8,128)(2,1)}, s32[8]{0:T(128)S(1)}) %tuple.32), branch_computations={%region_1.1_spmd, %region_2.2_spmd} | conditional | flops 1342177280 | bytes 10748046 | solution.py:79
  285.4 5.6 %fusion.5 = f32[1,256,256]{2,1,0:T(8,128)S(1)} fusion(bf16[9,10240,256]{2,1,0:T(8,128)(2,1)} %get-tuple-element.45, s32[]{:T(128)S(6)} %select_n.104, s32[]{:T(128)S(6)} %select_n.103), kind=kOutput, calls=%fused_computation.21 | convolution fusion | flops 1342177280 | bytes 10747912 | tf_op jit(solution)/shard_map/while/body/eval_jaxpr/cond/branch_1_fun/dot_general | solution.py:69
  293.8 12.2 %conditional.2 = (f32[1,256,256]{2,1,0:T(8,128)S(1)}) conditional(s32[]{:T(128)} %convert_element_type.46, () %tuple.31, (s32[]{:T(128)}, s32[8]{0:T(128)S(1)}, bf16[9,10240,256]{2,1,0:T(8,128)(2,1)}, s32[8]{0:T(128)S(1)}) %tuple.32), branch_computations={%region_1.1_spmd, %region_2.2_spmd} | conditional | flops 1342177280 | bytes 10748046 | solution.py:79
  300.4 5.6 %fusion.5 = f32[1,256,256]{2,1,0:T(8,128)S(1)} fusion(bf16[9,10240,256]{2,1,0:T(8,128)(2,1)} %get-tuple-element.45, s32[]{:T(128)S(6)} %select_n.104, s32[]{:T(128)S(6)} %select_n.103), kind=kOutput, calls=%fused_computation.21 | convolution fusion | flops 1342177280 | bytes 10747912 | tf_op jit(solution)/shard_map/while/body/eval_jaxpr/cond/branch_1_fun/dot_general | solution.py:69
  315.0 11.8 %gather_fusion.7 = f32[2048]{0:T(1024)S(1)} fusion(f32[1792]{0:T(1024)S(1)} %copy-done.2, s32[2048]{0:T(1024)S(1)} %broadcast_clamp_fusion.1), kind=kCustom, calls=%fused_computation.7 | custom fusion | bytes 24576 | tf_op jit(solution)/shard_map/gather | solution.py:27
  326.8 11.8 %gather_fusion.9 = f32[2048]{0:T(1024)S(1)} fusion(f32[1792]{0:T(1024)S(1)} %copy-done.2, s32[2048]{0:T(1024)S(1)} %broadcast_clamp_fusion), kind=kCustom, calls=%fused_computation.9 | custom fusion | bytes 24576 | tf_op jit(solution)/shard_map/gather | solution.py:28
  339.4 58.7 %all-reduce.6.cloned.1.call-done = f32[8,256,256]{2,1,0:T(8,128)} async-done(((f32[8,256,256]{2,1,0:T(8,128)}), f32[8,256,256]{2,1,0:T(8,128)}) %all-reduce.6.cloned.1.call-update) | async-done | bytes 2097168 | tf_op jit(solution)/shard_map/psum | solution.py:82
  424.9 7.0 %multiply_reduce_fusion.1 = f32[8,256,256]{2,1,0:T(8,128)} fusion(f32[8,4]{1,0:T(8,128)S(1)} %gather_fusion, s32[8,256]{1,0:T(8,128)S(1)} %gather_fusion.8, s32[8,4,256]{2,1,0:T(4,128)S(1)} %reshape.242, bf16[8,4,256,256]{3,2,1,0:T(8,128)(2,1)} %bitcast.64, s32[8,4,256]{2,1,0:T(4,128)S(1)} %reshape.174, s32[8,256]{1,0:T(8,128)S(1)} %gather_fusion.2), kind=kOutput, calls=%fused_computation.34 | convolution fusion | flops 2157445120 | bytes 6373504 | tf_op jit(solution)/shard_map/snad,sndb->snab/dot_general | solution.py:106
  438.9 9.1 %collective-permute-done.4 = bf16[8,256,256]{2,1,0:T(8,128)(2,1)S(1)} collective-permute-done((bf16[8,256,256]{2,1,0:T(8,128)(2,1)S(1)}, bf16[8,256,256]{2,1,0:T(8,128)(2,1)S(1)}, u32[]{:S(2)}, u32[]{:S(2)}) %collective-permute-start.4) | collective-permute-done | bytes 1048608 | tf_op jit(solution)/shard_map/ppermute | solution.py:17
  454.3 4.6 gather_fusion.15
  459.0 6.8 %multiply_reduce_fusion = f32[8,256,256]{2,1,0:T(8,128)} fusion(f32[8,4]{1,0:T(8,128)S(1)} %gather_fusion, s32[8,256]{1,0:T(8,128)S(1)} %gather_fusion.8, s32[8,4,256]{2,1,0:T(4,128)S(1)} %reshape.242, bf16[8,4,256,256]{3,2,1,0:T(8,128)(2,1)} %bitcast.63, s32[8,4,256]{2,1,0:T(4,128)S(1)} %reshape.174, s32[8,256]{1,0:T(8,128)S(1)} %gather_fusion.2), kind=kOutput, calls=%fused_computation.33 | convolution fusion | flops 2157445120 | bytes 6373504 | tf_op jit(solution)/shard_map/snad,sndb->snab/dot_general | solution.py:106
  (124 shorter events, 73.4 us)
Async XLA Ops:
  6.5 305.9 %copy-start = (s32[24,256]{1,0:T(8,128)S(1)}, s32[24,256]{1,0:T(8,128)}, u32[]{:S(2)}) copy-start(s32[24,256]{1,0:T(8,128)} %param.15) | copy-start | bytes 73732
  6.5 391.5 %all-reduce.6.cloned.1.call-start = ((), (), s32[]{:S(2)}) async-start(), calls=%async_computation | async-start | bytes 4194304 | tf_op jit(solution)/shard_map/psum | solution.py:82
  6.5 174.1 %collective-permute-start = (bf16[3,10240,256]{2,1,0:T(8,128)(2,1)}, bf16[3,10240,256]{2,1,0:T(8,128)(2,1)}, u32[]{:S(2)}, u32[]{:S(2)}) collective-permute-start(bf16[3,10240,256]{2,1,0:T(8,128)(2,1)} %param.12), channel_id=1, source_target_pairs={{0,1},{1,4},{4,5},{5,8},{8,9},{9,12},{12,13},{2,3},{3,6},{6,7},{7,... | collective-permute-start | bytes 47185928 | tf_op jit(solution)/shard_map/ppermute | solution.py:17
  11.3 173.7 %collective-permute-start.1 = (bf16[3,10240,256]{2,1,0:T(8,128)(2,1)}, bf16[3,10240,256]{2,1,0:T(8,128)(2,1)}, u32[]{:S(2)}, u32[]{:S(2)}) collective-permute-start(bf16[3,10240,256]{2,1,0:T(8,128)(2,1)} %param.12), channel_id=1, source_target_pairs={{1,0},{4,1},{5,4},{8,5},{9,8},{12,9},{13,12},{3,2},{6,3},{7,6},{10... | collective-permute-start | bytes 47185928 | tf_op jit(solution)/shard_map/ppermute | solution.py:19
  216.8 96.9 %copy-start.3 = (f32[24]{0:T(128)S(1)}, f32[24]{0:T(128)}, u32[]{:S(2)}) copy-start(f32[24]{0:T(128)} %param.18) | copy-start | bytes 292
  312.4 2.6 copy-start.2
  326.8 11.8 %copy-start.7 = (s32[8,4]{0,1:T(4,128)S(1)}, s32[8,4]{0,1:T(4,128)}, u32[]{:S(2)}) copy-start(s32[8,4]{0,1:T(4,128)} %param.16) | copy-start | bytes 388
  338.6 67.6 %copy-start.1 = (s32[64,2]{0,1:T(2,128)S(1)}, s32[64,2]{0,1:T(2,128)}, u32[]{:S(2)}) copy-start(s32[64,2]{0,1:T(2,128)} %param.13) | copy-start | bytes 1540
  400.2 8.6 %copy-start.5 = (bf16[8,256,256]{2,1,0:T(8,128)(2,1)}, bf16[8,256,256]{2,1,0:T(8,128)(2,1)S(1)}, u32[]{:S(2)}) copy-start(bf16[8,256,256]{2,1,0:T(8,128)(2,1)S(1)} %divide_convert_fusion.2) | copy-start | bytes 3145732
  400.2 15.4 %collective-permute-start.2 = (bf16[8,256,256]{2,1,0:T(8,128)(2,1)S(1)}, bf16[8,256,256]{2,1,0:T(8,128)(2,1)S(1)}, u32[]{:S(2)}, u32[]{:S(2)}) collective-permute-start(bf16[8,256,256]{2,1,0:T(8,128)(2,1)S(1)} %divide_convert_fusion.2), channel_id=1, source_target_pairs={{0,1},{1,4},{4,5},{5,8},{8,9},{9,12},{12,13},{2,3},{3,6},{6,7},{7,... | collective-permute-start | bytes 3145736 | tf_op jit(solution)/shard_map/ppermute | solution.py:17
  403.9 16.2 %collective-permute-start.3 = (bf16[8,256,256]{2,1,0:T(8,128)(2,1)S(1)}, bf16[8,256,256]{2,1,0:T(8,128)(2,1)}, u32[]{:S(2)}, u32[]{:S(2)}) collective-permute-start(bf16[8,256,256]{2,1,0:T(8,128)(2,1)S(1)} %divide_convert_fusion.2), channel_id=1, source_target_pairs={{1,0},{4,1},{5,4},{8,5},{9,8},{12,9},{13,12},{3,2},{6,3},{7,6},{10... | collective-permute-start | bytes 3145736 | tf_op jit(solution)/shard_map/ppermute | solution.py:19
  406.9 2.9 copy-start.8
  415.6 1.0 copy-start.6
  424.9 7.0 %copy-start.4 = (f32[8,256,256]{2,1,0:T(8,128)S(1)}, f32[8,256,256]{2,1,0:T(8,128)}, u32[]{:S(2)}) copy-start(f32[8,256,256]{2,1,0:T(8,128)} %all-reduce.6.cloned.1.call-done) | copy-start | bytes 6291460
  434.4 13.7 %collective-permute-start.4 = (bf16[8,256,256]{2,1,0:T(8,128)(2,1)S(1)}, bf16[8,256,256]{2,1,0:T(8,128)(2,1)S(1)}, u32[]{:S(2)}, u32[]{:S(2)}) collective-permute-start(bf16[8,256,256]{2,1,0:T(8,128)(2,1)S(1)} %divide_convert_fusion.1), channel_id=1, source_target_pairs={{0,1},{1,4},{4,5},{5,8},{8,9},{9,12},{12,13},{2,3},{3,6},{6,7},{7,... | collective-permute-start | bytes 3145736 | tf_op jit(solution)/shard_map/ppermute | solution.py:17
  436.3 16.1 %collective-permute-start.5 = (bf16[8,256,256]{2,1,0:T(8,128)(2,1)S(1)}, bf16[8,256,256]{2,1,0:T(8,128)(2,1)S(1)}, u32[]{:S(2)}, u32[]{:S(2)}) collective-permute-start(bf16[8,256,256]{2,1,0:T(8,128)(2,1)S(1)} %divide_convert_fusion.1), channel_id=1, source_target_pairs={{1,0},{4,1},{5,4},{8,5},{9,8},{12,9},{13,12},{3,2},{6,3},{7,6},{10... | collective-permute-start | bytes 3145736 | tf_op jit(solution)/shard_map/ppermute | solution.py:19
Sparse Core Ops, SparseCore 0:
  312.5 85.4 all-reduce.5
where the time goes:
time: 471 us; the launch traced here: 476 us
  waiting for transfers between devices  245 us (52%)
  local copies, waits for them, and re-layouts  61.9 us (13%)
  matrix products  47.5 us (10%)
  other arithmetic  44.5 us (9%)
  loops' own time  43.8 us (9%)
  starting transfers between devices  20.1 us (4%)
  between operations  13.8 us (3%)
    ppermute x3, waiting for transfers between devices, extended_2(): lax.ppermute(tail, axis, [(i, (i + 1) % count) for i in range(ends)])  174 us
    psum x1, waiting for transfers between devices, on_device(): integrals = lax.psum(partials, 'aux')  58.7 us
    concatenate x3, other arithmetic, extended_2(): jnp.concatenate([lax.ppermute(tail, axis, [(i, (i + 1) % count) for i in...  35.7 us
    dot_general x6, matrix products, compute(): lax.dot_general(left_block, right_block, (((0,), (0,)), ((), ())), prefer...  33.7 us
    another operation x8, loops' own time, integral(): return lax.cond(position < live_count, compute, skip)  32.7 us
    dot_general x2, matrix products, on_device(): jnp.einsum('snad,sndb->snab', selected, col_match, preferred_element_type...  13.8 us
    gather x3, local copies, waits for them, and re-layouts, energy_gaps(): col_energy = virt_energy[domains[col_orbs]]  12.3 us
    ppermute x3, waiting for transfers between devices, extended_2(): lax.ppermute(head, axis, [((i + 1) % count, i) for i in range(ends)])  12.3 us
  transfers between devices with their start and end apart: 7, of which 7 were waited for; matrix products, arithmetic and copies ran while one was open for 8% of the time, Pallas kernels for 0%

commit v1 on v0

v1 whole, which is shorter than its diff:
```python
import functools

import jax
import jax.numpy as jnp
from jax import lax
from jax.experimental import pallas as pl
from jax.experimental.pallas import tpu as pltpu
from jax.sharding import PartitionSpec as P

ITERS = 2
LINE = ("pair", "occ")
VMEM = 56 * 1024 * 1024
F32 = jnp.float32
BF16 = jnp.bfloat16
ROWS = (((0,), (0,)), ((), ()))


def chip_mate(value):
    return lax.ppermute(value, "occ", [(0, 1), (1, 0)])


def line_mate(value):
    pairs = []
    for chip in range(lax.axis_size("pair") - 1):
        left, right = 2 * chip + 1, 2 * chip + 2
        pairs += [(left, right), (right, left)]
    return lax.ppermute(value, LINE, pairs)


def aux_sum(value):
    count = lax.axis_size("aux")
    step = 1
    while step < count:
        other = lax.ppermute(value, "aux", [(i, i ^ step) for i in range(count)])
        value = (value.astype(F32) + other.astype(F32)).astype(BF16)
        step *= 2
    return value


def tile_rows(rows):
    for tile in (1280, 1024, 640, 512, 256, 128):
        if rows % tile == 0:
            return tile
    return rows


def own_kernel(block_ref, out_ref, total_ref):
    step = pl.program_id(0)

    @pl.when(step == 0)
    def _():
        total_ref[...] = jnp.zeros_like(total_ref)

    count = block_ref.shape[0]
    at = 0
    for left in range(count):
        for right in range(left + 1, count):
            total_ref[at] += lax.dot_general(block_ref[left], block_ref[right], ROWS, preferred_element_type=F32)
            at += 1

    @pl.when(step == pl.num_programs(0) - 1)
    def _():
        out_ref[...] = total_ref[...].astype(out_ref.dtype)


def own_products(blocks):
    count, rows, width = blocks.shape
    tile = tile_rows(rows)
    combos = count * (count - 1) // 2
    return pl.pallas_call(
        own_kernel,
        grid=(rows // tile,),
        in_specs=[pl.BlockSpec((count, tile, width), lambda t: (0, t, 0))],
        out_specs=pl.BlockSpec((combos, width, width), lambda t: (0, 0, 0)),
        out_shape=jax.ShapeDtypeStruct((combos, width, width), BF16),
        scratch_shapes=[pltpu.VMEM((combos, width, width), F32)],
        compiler_params=pltpu.CompilerParams(vmem_limit_bytes=VMEM),
        cost_estimate=pl.CostEstimate(
            flops=2 * combos * rows * width * width, bytes_accessed=2 * count * rows * width, transcendentals=0
        ),
        name="own_products",
    )(blocks)


def mate_kernel(half_ref, block_ref, mate_ref, out_ref, total_ref):
    step = pl.program_id(0)

    @pl.when(step == 0)
    def _():
        total_ref[...] = jnp.zeros_like(total_ref)

    mate = mate_ref[...]
    for orb in range(block_ref.shape[0]):
        total_ref[orb] += lax.dot_general(mate, block_ref[orb], ROWS, preferred_element_type=F32)

    @pl.when(step == pl.num_programs(0) - 1)
    def _():
        out_ref[...] = total_ref[...].astype(out_ref.dtype)


def mate_products(half, blocks, mate):
    count, _, width = blocks.shape
    rows, cols = mate.shape
    tile = tile_rows(rows)
    steps = rows // tile
    return pl.pallas_call(
        mate_kernel,
        grid_spec=pltpu.PrefetchScalarGridSpec(
            num_scalar_prefetch=1,
            grid=(steps,),
            in_specs=[
                pl.BlockSpec((count, tile, width), lambda t, half: (0, half[0] * steps + t, 0)),
                pl.BlockSpec((tile, cols), lambda t, half: (t, 0)),
            ],
            out_specs=pl.BlockSpec((count, cols, width), lambda t, half: (0, 0, 0)),
            scratch_shapes=[pltpu.VMEM((count, cols, width), F32)],
        ),
        out_shape=jax.ShapeDtypeStruct((count, cols, width), BF16),
        compiler_params=pltpu.CompilerParams(vmem_limit_bytes=VMEM),
        cost_estimate=pl.CostEstimate(
            flops=2 * count * rows * cols * width,
            bytes_accessed=2 * rows * (count * width + cols),
            transcendentals=0,
        ),
        name="mate_products",
    )(half, blocks, mate)


def pick(refs, which, index, into_ref):
    for at, ref in enumerate(refs):

        @pl.when(which == at)
        def _(ref=ref):
            into_ref[...] = ref[index].astype(into_ref.dtype)


def start_kernel(count, kind_ref, row_ref, col_ref, *refs):
    own_ref = refs[0]
    sent = {1: refs[1 : 1 + count], 2: refs[1 + 2 * count : 1 + 3 * count]}
    got = {1: refs[1 + count : 1 + 2 * count], 2: refs[1 + 3 * count : 1 + 4 * count]}
    inverse_ref, base_ref, rounded_ref, direct_ref, turned_ref = refs[1 + 4 * count :]
    slot = pl.program_id(0)
    kind, row, col = kind_ref[slot], row_ref[slot], col_ref[slot]

    @pl.when(kind == 0)
    def _():
        low, high = jnp.minimum(row, col), jnp.maximum(row, col)
        at = low * count - low * (low + 1) // 2 + high - low - 1
        value = own_ref[at].astype(F32)

        @pl.when(row < col)
        def _():
            direct_ref[...] = value
            turned_ref[...] = jnp.zeros_like(turned_ref)

        @pl.when(row > col)
        def _():
            direct_ref[...] = jnp.zeros_like(direct_ref)
            turned_ref[...] = value

    for which in (1, 2):

        @pl.when(kind == which)
        def _(which=which):
            pick(got[which], row, col, direct_ref)
            pick(sent[which], col, row, turned_ref)

    integral = direct_ref[...] + turned_ref[...].T
    base = -integral * inverse_ref[0]
    base_ref[0] = base
    rounded_ref[0] = base.astype(BF16)


def start_amplitudes(kind, row, col, own, chip_sent, chip_got, line_sent, line_got, inverse):
    slots, width, _ = inverse.shape
    count = len(chip_sent)
    tables = [own, *chip_sent, *chip_got, *line_sent, *line_got]
    whole = [pl.BlockSpec(t.shape, lambda s, *_: (0, 0, 0)) for t in tables]
    per_slot = pl.BlockSpec((1, width, width), lambda s, *_: (s, 0, 0))
    return pl.pallas_call(
        functools.partial(start_kernel, count),
        grid_spec=pltpu.PrefetchScalarGridSpec(
            num_scalar_prefetch=3,
            grid=(slots,),
            in_specs=[*whole, per_slot],
            out_specs=[per_slot, per_slot],
            scratch_shapes=[pltpu.VMEM((width, width), F32), pltpu.VMEM((width, width), F32)],
        ),
        out_shape=[
            jax.ShapeDtypeStruct((slots, width, width), F32),
            jax.ShapeDtypeStruct((slots, width, width), BF16),
        ],
        compiler_params=pltpu.CompilerParams(vmem_limit_bytes=VMEM),
        cost_estimate=pl.CostEstimate(flops=8 * slots * width * width, bytes_accessed=12 * 1024 * 1024, transcendentals=0),
        name="start_amplitudes",
    )(kind, row, col, *tables, inverse)


def sweep_kernel(kind_ref, source_ref, weight_ref, own_ref, chip_ref, line_ref, rows_ref, cols_ref, base_ref, inverse_ref, out_ref, picked_ref):
    slot = pl.program_id(0)
    total = None
    for n in range(rows_ref.shape[1]):
        pick((own_ref, chip_ref, line_ref), kind_ref[slot, n], source_ref[slot, n], picked_ref.at[n])
        selected = jnp.dot(rows_ref[0, n], picked_ref[n], preferred_element_type=F32).astype(BF16)
        term = weight_ref[slot, n] * jnp.dot(selected, cols_ref[0, n], preferred_element_type=F32)
        total = term if total is None else total + term
    out_ref[0] = (base_ref[0] + total * inverse_ref[0]).astype(out_ref.dtype)


def sweep_amplitudes(kind, source, weights, own, chip, line, row_match, col_match, base, inverse):
    slots, width, _ = own.shape
    neighbours = kind.shape[1]
    whole = pl.BlockSpec(own.shape, lambda s, *_: (0, 0, 0))
    match = pl.BlockSpec((1, neighbours, width, width), lambda s, *_: (s, 0, 0, 0))
    per_slot = pl.BlockSpec((1, width, width), lambda s, *_: (s, 0, 0))
    return pl.pallas_call(
        sweep_kernel,
        grid_spec=pltpu.PrefetchScalarGridSpec(
            num_scalar_prefetch=2,
            grid=(slots,),
            in_specs=[pl.BlockSpec(memory_space=pltpu.SMEM), whole, whole, whole, match, match, per_slot, per_slot],
            out_specs=per_slot,
            scratch_shapes=[pltpu.VMEM((neighbours, width, width), BF16)],
        ),
        out_shape=jax.ShapeDtypeStruct((slots, width, width), BF16),
        compiler_params=pltpu.CompilerParams(vmem_limit_bytes=VMEM),
        cost_estimate=pl.CostEstimate(
            flops=4 * slots * neighbours * width**3, bytes_accessed=16 * 1024 * 1024, transcendentals=0
        ),
        name="sweep_amplitudes",
    )(kind, source, weights, own, chip, line, row_match, col_match, base, inverse)


def on_device(three_index, pair_orbs, live_pairs, domains, coupled, fock_coupling_weight, occ_energy, virt_energy):
    count, naux, width = three_index.shape
    slots = coupled.shape[0]
    half_rows = naux // 2
    owner = lax.axis_index(LINE)
    parity = lax.axis_index("occ")
    chip_owner = owner + 1 - 2 * parity
    half = jnp.reshape(parity, (1,)).astype(jnp.int32)

    halves = three_index.reshape(count, 2, half_rows, width)
    sends = [lax.dynamic_index_in_dim(halves[j], 1 - parity, 0, keepdims=False) for j in range(count)]
    from_line = [line_mate(s) for s in sends]
    from_chip = [chip_mate(s) for s in sends]

    own = aux_sum(own_products(three_index))
    chip_sent = [aux_sum(mate_products(half, three_index, m)) for m in from_chip]
    chip_got = [chip_mate(v) for v in chip_sent]
    line_sent = [aux_sum(mate_products(half, three_index, m)) for m in from_line]
    line_got = [line_mate(v) for v in line_sent]

    local = jnp.arange(slots, dtype=jnp.int32)
    pairs = lax.dynamic_slice_in_dim(pair_orbs, owner * slots, slots, 0)
    live = (local < live_pairs[owner]).astype(F32)[:, None, None]
    rows, cols = pairs[:, 0], pairs[:, 1]

    def kind_of(other):
        return jnp.where(other == owner, 0, jnp.where(other == chip_owner, 1, 2)).astype(jnp.int32)

    energies = virt_energy[domains]
    gaps = (
        energies[rows][:, :, None]
        + energies[cols][:, None, :]
        - occ_energy[rows][:, None, None]
        - occ_energy[cols][:, None, None]
    )
    inverse = live / gaps
    source_rows = domains[pair_orbs[coupled, 0]]
    source_cols = domains[pair_orbs[coupled, 1]]
    row_match = (domains[rows][:, None, :, None] == source_rows[:, :, None, :]).astype(BF16)
    col_match = (source_cols[:, :, :, None] == domains[cols][:, None, None, :]).astype(BF16)

    base, rounded = start_amplitudes(
        kind_of(cols // count), rows % count, cols % count, own, chip_sent, chip_got, line_sent, line_got, inverse
    )
    kind, source = kind_of(coupled // slots), coupled % slots
    for sweep in range(ITERS):
        rounded = sweep_amplitudes(
            kind, source, fock_coupling_weight, rounded, chip_mate(rounded), line_mate(rounded),
            row_match, col_match, base, inverse,
        )
    return rounded


def solution(mesh):
    return jax.shard_map(
        on_device,
        mesh=mesh,
        in_specs=(
            P(("groups", "pair", "occ"), "aux", None),
            P("groups", None),
            P("groups"),
            P("groups", None),
            P(("groups", "pair", "occ"), None),
            P(("groups", "pair", "occ"), None),
            P("groups"),
            P("groups"),
        ),
        out_specs=P(("groups", "pair", "occ"), None, None),
        check_vma=False,
    )
```

time: 471 us -> 245 us (0.52); the launches traced: 476 us -> 244 us
  waiting for transfers between devices: 245 us -> 41.8 us
  Pallas kernels: 0 us -> 91.5 us
  matrix products: 47.5 us -> 0 us
  loops' own time: 43.8 us -> 0 us
  other arithmetic: 44.5 us -> 10.7 us
  starting transfers between devices: 20.1 us -> 35.3 us
  between operations: 13.8 us -> 0.54 us
    ppermute x6 -> x23, waiting for transfers between devices: 186 us -> 41.8 us  [the longest x8 22.2 us: line_mate(): return lax.ppermute(value, LINE, pairs)]
    pallas_call x0 -> x10, Pallas kernels: none -> 91.5 us  [the longest x6 39.9 us: mate_products(): pl.pallas_call(mate_kernel, grid_spec=pltpu.PrefetchScalarGridSpec(num_sc...]
    psum x1 -> x0, waiting for transfers between devices: 58.7 us -> none  [on_device(): integrals = lax.psum(partials, 'aux')]
    dot_general x8 -> x0, matrix products: 47.5 us -> none  [the longest x6 33.7 us: compute(): lax.dot_general(left_block, right_block, (((0,), (0,)), ((), ())), prefer...]
    another operation x9 -> x0, loops' own time: 43.8 us -> none  [the longest x8 32.7 us: integral(): return lax.cond(position < live_count, compute, skip)]
    concatenate x5 -> x1, other arithmetic: 35.7 us -> 0.61 us  [on_device(): source_cols = domains[pair_orbs[coupled, 1]]]
    ppermute x6 -> x23, starting transfers between devices: 20.1 us -> 35.3 us  [the longest x8 28.8 us: line_mate(): return lax.ppermute(value, LINE, pairs)]
    dynamic_slice x21 -> x2, local copies, waits for them, and re-layouts: 13.5 us -> 0.67 us  [the longest x1 0.59 us: on_device(): live = (local < live_pairs[owner]).astype(F32)[:, None, None]]
  transfers between devices with their start and end apart: 7 -> 23, of which waited for: 7 -> 7; matrix products, arithmetic and copies ran while one was open for 8% -> 23% of each run, Pallas kernels for 0% -> 21%
where the time goes in v1:
time: 245 us; the launch traced here: 244 us
  Pallas kernels  91.5 us (37%)
  local copies, waits for them, and re-layouts  64.6 us (26%)
  waiting for transfers between devices  41.8 us (17%)
  starting transfers between devices  35.3 us (14%)
  other arithmetic  10.7 us (4%)
    pallas_call x6, Pallas kernels, mate_products(): pl.pallas_call(mate_kernel, grid_spec=pltpu.PrefetchScalarGridSpec(num_sc...  39.9 us
    gather x2, local copies, waits for them, and re-layouts, on_device(): energies = virt_energy[domains]  34.3 us
    pallas_call x2, Pallas kernels, sweep_amplitudes(): pl.pallas_call(sweep_kernel, grid_spec=pltpu.PrefetchScalarGridSpec(num_s...  31.7 us
    ppermute x8, starting transfers between devices, line_mate(): return lax.ppermute(value, LINE, pairs)  28.8 us
    ppermute x8, waiting for transfers between devices, line_mate(): return lax.ppermute(value, LINE, pairs)  22.2 us
    ppermute x7, waiting for transfers between devices, aux_sum(): other = lax.ppermute(value, 'aux', [(i, i ^ step) for i in range(count)])  19.6 us
    slice x1, local copies, waits for them, and re-layouts, on_device(): halves[j]  12 us
    pallas_call x1, Pallas kernels, own_products(): pl.pallas_call(own_kernel, grid=(rows // tile,), in_specs=[pl.BlockSpec((...  11.1 us
  transfers between devices with their start and end apart: 23, of which 7 were waited for; matrix products, arithmetic and copies ran while one was open for 23% of the time, Pallas kernels for 21%

profile of v1, /device:TPU:1, one launch (start us, length us, event | category | flops | bytes accessed | tf_op | source)
XLA Modules:
  0.0 244.4 jit_solution(4230977064559450828)
XLA Ops:
  0.0 12.0 %fusion.8 = (bf16[1,10240,256]{2,1,0:T(8,128)(2,1)}, bf16[1,10240,256]{2,1,0:T(8,128)(2,1)}, bf16[1,10240,256]{2,1,0:T(8,128)(2,1)}) fusion(bf16[3,10240,256]{2,1,0:T(8,128)(2,1)} %block_ref.13), kind=kLoop, calls=%fused_computation.58 | loop fusion | bytes 31457280 | tf_op jit(solution)/shard_map/slice | solution.py:244
  12.0 3.6 %dynamic-slice_bitcast_fusion.2 = bf16[5120,256]{1,0:T(8,128)(2,1)} fusion(bf16[2,5120,256]{2,1,0:T(8,128)(2,1)} %bitcast.41, s32[]{:T(128)S(6)} %select_n.104), kind=kLoop, calls=%fused_computation.15 | loop fusion | bytes 5242884 | tf_op jit(solution)/shard_map/jit(dynamic_index_in_dim)/squeeze | solution.py:244
  19.8 4.6 %collective-permute-start.10 = (bf16[5120,256]{1,0:T(8,128)(2,1)}, bf16[5120,256]{1,0:T(8,128)(2,1)}, u32[]{:S(2)}, u32[]{:S(2)}) collective-permute-start(bf16[5120,256]{1,0:T(8,128)(2,1)} %dynamic-slice_bitcast_fusion.2), channel_id=1, source_target_pairs={{1,4},{4,1},{5,8},{8,5},{9,12},{12,9},{3,6},{6,3},{7,10},{10,7},{1... | collective-permute-start | bytes 7864328 | tf_op jit(solution)/shard_map/ppermute | solution.py:27
  27.7 3.6 %collective-permute-start.14 = (bf16[5120,256]{1,0:T(8,128)(2,1)S(1)}, bf16[5120,256]{1,0:T(8,128)(2,1)}, u32[]{:S(2)}, u32[]{:S(2)}) collective-permute-start(bf16[5120,256]{1,0:T(8,128)(2,1)S(1)} %dynamic-slice_bitcast_fusion), channel_id=1, source_target_pairs={{1,4},{4,1},{5,8},{8,5},{9,12},{12,9},{3,6},{6,3},{7,10},{10,7},{1... | collective-permute-start | bytes 7864328 | tf_op jit(solution)/shard_map/ppermute | solution.py:27
  31.4 34.3 %gather_fusion = f32[6144]{0:T(1024)S(1)} fusion(f32[1792]{0:T(1024)S(1)} %copy-done, s32[6144]{0:T(1024)S(1)} %broadcast_clamp_fusion), kind=kCustom, calls=%fused_computation | custom fusion | bytes 73728 | tf_op jit(solution)/shard_map/gather | solution.py:262
  71.7 11.1 %own_products.1 = bf16[3,256,256]{2,1,0:T(8,128)(2,1)} custom-call(bf16[3,10240,256]{2,1,0:T(8,128)(2,1)} %block_ref.13), custom_call_target="tpu_custom_call" | custom-call | flops 4026531840 | bytes 15728640 | tf_op jit(solution)/shard_map/own_products/pallas_call | solution.py:70
  82.8 6.7 %mate_products.6 = bf16[3,256,256]{2,1,0:T(8,128)(2,1)} custom-call(s32[1]{0:T(128)} %bitcast.4.half_ref, bf16[3,10240,256]{2,1,0:T(8,128)(2,1)} %block_ref.13, bf16[5120,256]{1,0:T(8,128)(2,1)} %collective-permute-done.1.mate_ref), custom_call_target="tpu_custom_call" | custom-call | flops 2013265920 | bytes 10485760 | tf_op jit(solution)/shard_map/mate_products/pallas_call | solution.py:106
  90.8 6.6 %mate_products.7 = bf16[3,256,256]{2,1,0:T(8,128)(2,1)} custom-call(s32[1]{0:T(128)} %bitcast.4.half_ref, bf16[3,10240,256]{2,1,0:T(8,128)(2,1)} %block_ref.13, bf16[5120,256]{1,0:T(8,128)(2,1)} %collective-permute-done.3.mate_ref), custom_call_target="tpu_custom_call" | custom-call | flops 2013265920 | bytes 10485760 | tf_op jit(solution)/shard_map/mate_products/pallas_call | solution.py:106
  97.7 6.6 %mate_products.8 = bf16[3,256,256]{2,1,0:T(8,128)(2,1)} custom-call(s32[1]{0:T(128)} %bitcast.4.half_ref, bf16[3,10240,256]{2,1,0:T(8,128)(2,1)} %block_ref.13, bf16[5120,256]{1,0:T(8,128)(2,1)} %collective-permute-done.5.mate_ref), custom_call_target="tpu_custom_call" | custom-call | flops 2013265920 | bytes 10485760 | tf_op jit(solution)/shard_map/mate_products/pallas_call | solution.py:106
  105.6 6.6 %mate_products.9 = bf16[3,256,256]{2,1,0:T(8,128)(2,1)} custom-call(s32[1]{0:T(128)} %bitcast.4.half_ref, bf16[3,10240,256]{2,1,0:T(8,128)(2,1)} %block_ref.13, bf16[5120,256]{1,0:T(8,128)(2,1)} %collective-permute-done.10.mate_ref), custom_call_target="tpu_custom_call" | custom-call | flops 2013265920 | bytes 10485760 | tf_op jit(solution)/shard_map/mate_products/pallas_call | solution.py:106
  112.6 6.7 %mate_products.10 = bf16[3,256,256]{2,1,0:T(8,128)(2,1)} custom-call(s32[1]{0:T(128)} %bitcast.4.half_ref, bf16[3,10240,256]{2,1,0:T(8,128)(2,1)} %block_ref.13, bf16[5120,256]{1,0:T(8,128)(2,1)} %collective-permute-done.12.mate_ref), custom_call_target="tpu_custom_call" | custom-call | flops 2013265920 | bytes 10485760 | tf_op jit(solution)/shard_map/mate_products/pallas_call | solution.py:106
  120.5 6.6 %mate_products.11 = bf16[3,256,256]{2,1,0:T(8,128)(2,1)} custom-call(s32[1]{0:T(128)} %bitcast.4.half_ref, bf16[3,10240,256]{2,1,0:T(8,128)(2,1)} %block_ref.13, bf16[5120,256]{1,0:T(8,128)(2,1)} %collective-permute-done.14.mate_ref), custom_call_target="tpu_custom_call" | custom-call | flops 2013265920 | bytes 10485760 | tf_op jit(solution)/shard_map/mate_products/pallas_call | solution.py:106
  129.2 4.6 %collective-permute-done.11 = bf16[3,256,256]{2,1,0:T(8,128)(2,1)S(1)} collective-permute-done((bf16[3,256,256]{2,1,0:T(8,128)(2,1)S(1)}, bf16[3,256,256]{2,1,0:T(8,128)(2,1)S(1)}, u32[]{:S(2)}, u32[]{:S(2)}) %collective-permute-start.11) | collective-permute-done | bytes 393248 | tf_op jit(solution)/shard_map/ppermute | solution.py:34
  133.9 8.3 %collective-permute-done.13 = bf16[3,256,256]{2,1,0:T(8,128)(2,1)S(1)} collective-permute-done((bf16[3,256,256]{2,1,0:T(8,128)(2,1)S(1)}, bf16[3,256,256]{2,1,0:T(8,128)(2,1)S(1)}, u32[]{:S(2)}, u32[]{:S(2)}) %collective-permute-start.13) | collective-permute-done | bytes 393248 | tf_op jit(solution)/shard_map/ppermute | solution.py:34
  142.4 6.6 %collective-permute-done.15 = bf16[3,256,256]{2,1,0:T(8,128)(2,1)S(1)} collective-permute-done((bf16[3,256,256]{2,1,0:T(8,128)(2,1)}, bf16[3,256,256]{2,1,0:T(8,128)(2,1)S(1)}, u32[]{:S(2)}, u32[]{:S(2)}) %collective-permute-start.15) | collective-permute-done | bytes 393248 | tf_op jit(solution)/shard_map/ppermute | solution.py:34
  149.0 5.2 %collective-permute-start.16 = (bf16[3,256,256]{2,1,0:T(8,128)(2,1)S(1)}, bf16[3,256,256]{2,1,0:T(8,128)(2,1)S(1)}, u32[]{:S(2)}, u32[]{:S(2)}) collective-permute-start(bf16[3,256,256]{2,1,0:T(8,128)(2,1)S(1)} %add_convert_fusion.2.refs_7_), channel_id=1, source_target_pairs={{1,4},{4,1},{5,8},{8,5},{9,12},{12,9},{3,6},{6,3},{7,10},{10,7},{1... | collective-permute-start | bytes 1179656 | tf_op jit(solution)/shard_map/ppermute | solution.py:27
  156.3 3.6 %collective-permute-start.18 = (bf16[3,256,256]{2,1,0:T(8,128)(2,1)S(1)}, bf16[3,256,256]{2,1,0:T(8,128)(2,1)S(1)}, u32[]{:S(2)}, u32[]{:S(2)}) collective-permute-start(bf16[3,256,256]{2,1,0:T(8,128)(2,1)S(1)} %add_convert_fusion.refs_9_), channel_id=1, source_target_pairs={{1,4},{4,1},{5,8},{8,5},{9,12},{12,9},{3,6},{6,3},{7,10},{10,7},{1... | collective-permute-start | bytes 1179656 | tf_op jit(solution)/shard_map/ppermute | solution.py:27
  163.8 4.2 %collective-permute-done.18.refs_12_ = bf16[3,256,256]{2,1,0:T(8,128)(2,1)S(1)} collective-permute-done((bf16[3,256,256]{2,1,0:T(8,128)(2,1)S(1)}, bf16[3,256,256]{2,1,0:T(8,128)(2,1)S(1)}, u32[]{:S(2)}, u32[]{:S(2)}) %collective-permute-start.18) | collective-permute-done | bytes 393248 | tf_op jit(solution)/shard_map/ppermute | solution.py:27
  168.8 8.8 %start_amplitudes.1 = (f32[8,256,256]{2,1,0:T(8,128)}, bf16[8,256,256]{2,1,0:T(8,128)(2,1)}) custom-call(s32[8]{0:T(128)} %get-tuple-element.19.kind_ref, s32[8]{0:T(128)} %get-tuple-element.20.row_ref, s32[8]{0:T(128)} %get-tuple-element.18.col_ref, bf16[3,256,256]{2,1,0:T(8,128)(2,1)} %add_convert_fusion.6.refs_0_, bf16[3,256,256]{2,1,0:T(8,128)(2,1)} %copy-done.8, ...), custom_call_target="tpu_custom_call" | custom-call | flops 4194304 | bytes 12582912 | tf_op jit(solution)/shard_map/start_amplitudes/pallas_call | solution.py:180
  177.6 3.9 %collective-permute-start.20 = (bf16[8,256,256]{2,1,0:T(8,128)(2,1)}, bf16[8,256,256]{2,1,0:T(8,128)(2,1)S(1)}, u32[]{:S(2)}, u32[]{:S(2)}) collective-permute-start(bf16[8,256,256]{2,1,0:T(8,128)(2,1)} %get-tuple-element.7.own_ref), channel_id=1, source_target_pairs={{1,4},{4,1},{5,8},{8,5},{9,12},{12,9},{3,6},{6,3},{7,10},{10,7},{1... | collective-permute-start | bytes 3145736 | tf_op jit(solution)/shard_map/ppermute | solution.py:27
  195.0 15.8 %sweep_amplitudes.2.own_ref = bf16[8,256,256]{2,1,0:T(8,128)(2,1)} custom-call(s32[8,4]{1,0:T(8,128)} %get-tuple-element.15.kind_ref, s32[8,4]{1,0:T(8,128)} %get-tuple-element.14.source_ref, f32[8,4]{1,0:T(8,128)} %copy.24.weight_ref, bf16[8,256,256]{2,1,0:T(8,128)(2,1)} %get-tuple-element.7.own_ref, bf16[8,256,256]{2,1,0:T(8,128)(2,1)} %copy-done.20, ...), custom_call_target="tpu_custom_call" | custom-call | flops 2147483648 | bytes 16777216 | tf_op jit(solution)/shard_map/sweep_amplitudes/pallas_call | solution.py:216
  210.8 4.0 %collective-permute-start.22 = (bf16[8,256,256]{2,1,0:T(8,128)(2,1)}, bf16[8,256,256]{2,1,0:T(8,128)(2,1)S(1)}, u32[]{:S(2)}, u32[]{:S(2)}) collective-permute-start(bf16[8,256,256]{2,1,0:T(8,128)(2,1)} %sweep_amplitudes.2.own_ref), channel_id=1, source_target_pairs={{1,4},{4,1},{5,8},{8,5},{9,12},{12,9},{3,6},{6,3},{7,10},{10,7},{1... | collective-permute-start | bytes 3145736 | tf_op jit(solution)/shard_map/ppermute | solution.py:27
  214.9 12.7 %collective-permute-done.22.line_ref = bf16[8,256,256]{2,1,0:T(8,128)(2,1)S(1)} collective-permute-done((bf16[8,256,256]{2,1,0:T(8,128)(2,1)}, bf16[8,256,256]{2,1,0:T(8,128)(2,1)S(1)}, u32[]{:S(2)}, u32[]{:S(2)}) %collective-permute-start.22) | collective-permute-done | bytes 1048608 | tf_op jit(solution)/shard_map/ppermute | solution.py:27
  228.5 15.9 %sweep_amplitudes.3 = bf16[8,256,256]{2,1,0:T(8,128)(2,1)} custom-call(s32[8,4]{1,0:T(8,128)} %get-tuple-element.15.kind_ref, s32[8,4]{1,0:T(8,128)} %get-tuple-element.14.source_ref, f32[8,4]{1,0:T(8,128)} %copy.24.weight_ref, bf16[8,256,256]{2,1,0:T(8,128)(2,1)} %sweep_amplitudes.2.own_ref, bf16[8,256,256]{2,1,0:T(8,128)(2,1)} %copy-done.22, ...), custom_call_target="tpu_custom_call" | custom-call | flops 2147483648 | bytes 16777216 | tf_op jit(solution)/shard_map/sweep_amplitudes/pallas_call | solution.py:216
  (148 shorter events, 41.1 us)
Async XLA Ops:
  15.6 12.1 %collective-permute-start.1 = (bf16[5120,256]{1,0:T(8,128)(2,1)}, bf16[5120,256]{1,0:T(8,128)(2,1)}, u32[]{:S(2)}, u32[]{:S(2)}) collective-permute-start(bf16[5120,256]{1,0:T(8,128)(2,1)} %dynamic-slice_bitcast_fusion.2), channel_id=1, source_target_pairs={{0,1},{1,0},{2,3},{3,2},{4,5},{5,4},{6,7},{7,6},{8,9},{9,8},{10,11... | collective-permute-start | bytes 7864328 | tf_op jit(solution)/shard_map/ppermute | solution.py:19
  17.7 71.8 %collective-permute-start.3 = (bf16[5120,256]{1,0:T(8,128)(2,1)}, bf16[5120,256]{1,0:T(8,128)(2,1)}, u32[]{:S(2)}, u32[]{:S(2)}) collective-permute-start(bf16[5120,256]{1,0:T(8,128)(2,1)} %dynamic-slice_bitcast_fusion.1), channel_id=1, source_target_pairs={{0,1},{1,0},{2,3},{3,2},{4,5},{5,4},{6,7},{7,6},{8,9},{9,8},{10,11... | collective-permute-start | bytes 7864328 | tf_op jit(solution)/shard_map/ppermute | solution.py:19
  19.6 77.8 %collective-permute-start.5 = (bf16[5120,256]{1,0:T(8,128)(2,1)S(1)}, bf16[5120,256]{1,0:T(8,128)(2,1)}, u32[]{:S(2)}, u32[]{:S(2)}) collective-permute-start(bf16[5120,256]{1,0:T(8,128)(2,1)S(1)} %dynamic-slice_bitcast_fusion), channel_id=1, source_target_pairs={{0,1},{1,0},{2,3},{3,2},{4,5},{5,4},{6,7},{7,6},{8,9},{9,8},{10,11... | collective-permute-start | bytes 7864328 | tf_op jit(solution)/shard_map/ppermute | solution.py:19
  19.8 84.6 %collective-permute-start.10 = (bf16[5120,256]{1,0:T(8,128)(2,1)}, bf16[5120,256]{1,0:T(8,128)(2,1)}, u32[]{:S(2)}, u32[]{:S(2)}) collective-permute-start(bf16[5120,256]{1,0:T(8,128)(2,1)} %dynamic-slice_bitcast_fusion.2), channel_id=1, source_target_pairs={{1,4},{4,1},{5,8},{8,5},{9,12},{12,9},{3,6},{6,3},{7,10},{10,7},{1... | collective-permute-start | bytes 7864328 | tf_op jit(solution)/shard_map/ppermute | solution.py:27
  24.4 87.9 %collective-permute-start.12 = (bf16[5120,256]{1,0:T(8,128)(2,1)}, bf16[5120,256]{1,0:T(8,128)(2,1)}, u32[]{:S(2)}, u32[]{:S(2)}) collective-permute-start(bf16[5120,256]{1,0:T(8,128)(2,1)} %dynamic-slice_bitcast_fusion.1), channel_id=1, source_target_pairs={{1,4},{4,1},{5,8},{8,5},{9,12},{12,9},{3,6},{6,3},{7,10},{10,7},{1... | collective-permute-start | bytes 7864328 | tf_op jit(solution)/shard_map/ppermute | solution.py:27
  27.7 91.6 %collective-permute-start.14 = (bf16[5120,256]{1,0:T(8,128)(2,1)S(1)}, bf16[5120,256]{1,0:T(8,128)(2,1)}, u32[]{:S(2)}, u32[]{:S(2)}) collective-permute-start(bf16[5120,256]{1,0:T(8,128)(2,1)S(1)} %dynamic-slice_bitcast_fusion), channel_id=1, source_target_pairs={{1,4},{4,1},{5,8},{8,5},{9,12},{12,9},{3,6},{6,3},{7,10},{10,7},{1... | collective-permute-start | bytes 7864328 | tf_op jit(solution)/shard_map/ppermute | solution.py:27
  89.5 64.8 %collective-permute-start = (bf16[3,256,256]{2,1,0:T(8,128)(2,1)S(1)}, bf16[3,256,256]{2,1,0:T(8,128)(2,1)S(1)}, u32[]{:S(2)}, u32[]{:S(2)}) collective-permute-start(bf16[3,256,256]{2,1,0:T(8,128)(2,1)S(1)} %copy-done.7), channel_id=1, source_target_pairs={{0,2},{2,0},{1,3},{3,1},{4,6},{6,4},{5,7},{7,5},{8,10},{10,8},{9,1... | collective-permute-start | bytes 1179656 | tf_op jit(solution)/shard_map/ppermute | solution.py:34
  97.4 29.8 %collective-permute-start.2 = (bf16[3,256,256]{2,1,0:T(8,128)(2,1)S(1)}, bf16[3,256,256]{2,1,0:T(8,128)(2,1)S(1)}, u32[]{:S(2)}, u32[]{:S(2)}) collective-permute-start(bf16[3,256,256]{2,1,0:T(8,128)(2,1)S(1)} %copy-done.18), channel_id=1, source_target_pairs={{0,2},{2,0},{1,3},{3,1},{4,6},{6,4},{5,7},{7,5},{8,10},{10,8},{9,1... | collective-permute-start | bytes 1179656 | tf_op jit(solution)/shard_map/ppermute | solution.py:34
  104.4 23.3 %collective-permute-start.4 = (bf16[3,256,256]{2,1,0:T(8,128)(2,1)S(1)}, bf16[3,256,256]{2,1,0:T(8,128)(2,1)S(1)}, u32[]{:S(2)}, u32[]{:S(2)}) collective-permute-start(bf16[3,256,256]{2,1,0:T(8,128)(2,1)S(1)} %copy-done.17), channel_id=1, source_target_pairs={{0,2},{2,0},{1,3},{3,1},{4,6},{6,4},{5,7},{7,5},{8,10},{10,8},{9,1... | collective-permute-start | bytes 1179656 | tf_op jit(solution)/shard_map/ppermute | solution.py:34
  112.3 16.7 %collective-permute-start.6 = (bf16[3,256,256]{2,1,0:T(8,128)(2,1)S(1)}, bf16[3,256,256]{2,1,0:T(8,128)(2,1)S(1)}, u32[]{:S(2)}, u32[]{:S(2)}) collective-permute-start(bf16[3,256,256]{2,1,0:T(8,128)(2,1)S(1)} %copy-done.13), channel_id=1, source_target_pairs={{0,2},{2,0},{1,3},{3,1},{4,6},{6,4},{5,7},{7,5},{8,10},{10,8},{9,1... | collective-permute-start | bytes 1179656 | tf_op jit(solution)/shard_map/ppermute | solution.py:34
  119.3 14.5 %collective-permute-start.11 = (bf16[3,256,256]{2,1,0:T(8,128)(2,1)S(1)}, bf16[3,256,256]{2,1,0:T(8,128)(2,1)S(1)}, u32[]{:S(2)}, u32[]{:S(2)}) collective-permute-start(bf16[3,256,256]{2,1,0:T(8,128)(2,1)S(1)} %copy-done.14), channel_id=1, source_target_pairs={{0,2},{2,0},{1,3},{3,1},{4,6},{6,4},{5,7},{7,5},{8,10},{10,8},{9,1... | collective-permute-start | bytes 1179656 | tf_op jit(solution)/shard_map/ppermute | solution.py:34
  127.2 15.1 %collective-permute-start.13 = (bf16[3,256,256]{2,1,0:T(8,128)(2,1)S(1)}, bf16[3,256,256]{2,1,0:T(8,128)(2,1)S(1)}, u32[]{:S(2)}, u32[]{:S(2)}) collective-permute-start(bf16[3,256,256]{2,1,0:T(8,128)(2,1)S(1)} %copy-done.15), channel_id=1, source_target_pairs={{0,2},{2,0},{1,3},{3,1},{4,6},{6,4},{5,7},{7,5},{8,10},{10,8},{9,1... | collective-permute-start | bytes 1179656 | tf_op jit(solution)/shard_map/ppermute | solution.py:34
  127.6 21.4 %collective-permute-start.15 = (bf16[3,256,256]{2,1,0:T(8,128)(2,1)}, bf16[3,256,256]{2,1,0:T(8,128)(2,1)S(1)}, u32[]{:S(2)}, u32[]{:S(2)}) collective-permute-start(bf16[3,256,256]{2,1,0:T(8,128)(2,1)} %mate_products.11), channel_id=1, source_target_pairs={{0,2},{2,0},{1,3},{3,1},{4,6},{6,4},{5,7},{7,5},{8,10},{10,8},{9,1... | collective-permute-start | bytes 1179656 | tf_op jit(solution)/shard_map/ppermute | solution.py:34
  129.0 27.2 %collective-permute-start.7 = (bf16[3,256,256]{2,1,0:T(8,128)(2,1)S(1)}, bf16[3,256,256]{2,1,0:T(8,128)(2,1)S(1)}, u32[]{:S(2)}, u32[]{:S(2)}) collective-permute-start(bf16[3,256,256]{2,1,0:T(8,128)(2,1)S(1)} %add_convert_fusion.5.refs_1_), channel_id=1, source_target_pairs={{0,1},{1,0},{2,3},{3,2},{4,5},{5,4},{6,7},{7,6},{8,9},{9,8},{10,11... | collective-permute-start | bytes 1179656 | tf_op jit(solution)/shard_map/ppermute | solution.py:19
  129.2 38.9 %copy-start.10 = (bf16[3,256,256]{2,1,0:T(8,128)(2,1)}, bf16[3,256,256]{2,1,0:T(8,128)(2,1)S(1)}, u32[]{:S(2)}) copy-start(bf16[3,256,256]{2,1,0:T(8,128)(2,1)S(1)} %add_convert_fusion.3.refs_3_) | copy-start | bytes 1179652
  133.8 27.5 %collective-permute-start.8 = (bf16[3,256,256]{2,1,0:T(8,128)(2,1)S(1)}, bf16[3,256,256]{2,1,0:T(8,128)(2,1)S(1)}, u32[]{:S(2)}, u32[]{:S(2)}) collective-permute-start(bf16[3,256,256]{2,1,0:T(8,128)(2,1)S(1)} %add_convert_fusion.4.refs_2_), channel_id=1, source_target_pairs={{0,1},{1,0},{2,3},{3,2},{4,5},{5,4},{6,7},{7,6},{8,9},{9,8},{10,11... | collective-permute-start | bytes 1179656 | tf_op jit(solution)/shard_map/ppermute | solution.py:19
  142.2 19.1 %collective-permute-start.9 = (bf16[3,256,256]{2,1,0:T(8,128)(2,1)S(1)}, bf16[3,256,256]{2,1,0:T(8,128)(2,1)S(1)}, u32[]{:S(2)}, u32[]{:S(2)}) collective-permute-start(bf16[3,256,256]{2,1,0:T(8,128)(2,1)S(1)} %add_convert_fusion.3.refs_3_), channel_id=1, source_target_pairs={{0,1},{1,0},{2,3},{3,2},{4,5},{5,4},{6,7},{7,6},{8,9},{9,8},{10,11... | collective-permute-start | bytes 1179656 | tf_op jit(solution)/shard_map/ppermute | solution.py:19
  149.0 12.3 %collective-permute-start.16 = (bf16[3,256,256]{2,1,0:T(8,128)(2,1)S(1)}, bf16[3,256,256]{2,1,0:T(8,128)(2,1)S(1)}, u32[]{:S(2)}, u32[]{:S(2)}) collective-permute-start(bf16[3,256,256]{2,1,0:T(8,128)(2,1)S(1)} %add_convert_fusion.2.refs_7_), channel_id=1, source_target_pairs={{1,4},{4,1},{5,8},{8,5},{9,12},{12,9},{3,6},{6,3},{7,10},{10,7},{1... | collective-permute-start | bytes 1179656 | tf_op jit(solution)/shard_map/ppermute | solution.py:27
  154.3 9.5 %collective-permute-start.17 = (bf16[3,256,256]{2,1,0:T(8,128)(2,1)S(1)}, bf16[3,256,256]{2,1,0:T(8,128)(2,1)S(1)}, u32[]{:S(2)}, u32[]{:S(2)}) collective-permute-start(bf16[3,256,256]{2,1,0:T(8,128)(2,1)S(1)} %add_convert_fusion.1.refs_8_), channel_id=1, source_target_pairs={{1,4},{4,1},{5,8},{8,5},{9,12},{12,9},{3,6},{6,3},{7,10},{10,7},{1... | collective-permute-start | bytes 1179656 | tf_op jit(solution)/shard_map/ppermute | solution.py:27
  156.3 11.8 %collective-permute-start.18 = (bf16[3,256,256]{2,1,0:T(8,128)(2,1)S(1)}, bf16[3,256,256]{2,1,0:T(8,128)(2,1)S(1)}, u32[]{:S(2)}, u32[]{:S(2)}) collective-permute-start(bf16[3,256,256]{2,1,0:T(8,128)(2,1)S(1)} %add_convert_fusion.refs_9_), channel_id=1, source_target_pairs={{1,4},{4,1},{5,8},{8,5},{9,12},{12,9},{3,6},{6,3},{7,10},{10,7},{1... | collective-permute-start | bytes 1179656 | tf_op jit(solution)/shard_map/ppermute | solution.py:27
  177.6 13.6 %collective-permute-start.19 = (bf16[8,256,256]{2,1,0:T(8,128)(2,1)}, bf16[8,256,256]{2,1,0:T(8,128)(2,1)S(1)}, u32[]{:S(2)}, u32[]{:S(2)}) collective-permute-start(bf16[8,256,256]{2,1,0:T(8,128)(2,1)} %get-tuple-element.7.own_ref), channel_id=1, source_target_pairs={{0,1},{1,0},{2,3},{3,2},{4,5},{5,4},{6,7},{7,6},{8,9},{9,8},{10,11... | collective-permute-start | bytes 3145736 | tf_op jit(solution)/shard_map/ppermute | solution.py:19
  177.6 16.4 %collective-permute-start.20 = (bf16[8,256,256]{2,1,0:T(8,128)(2,1)}, bf16[8,256,256]{2,1,0:T(8,128)(2,1)S(1)}, u32[]{:S(2)}, u32[]{:S(2)}) collective-permute-start(bf16[8,256,256]{2,1,0:T(8,128)(2,1)} %get-tuple-element.7.own_ref), channel_id=1, source_target_pairs={{1,4},{4,1},{5,8},{8,5},{9,12},{12,9},{3,6},{6,3},{7,10},{10,7},{1... | collective-permute-start | bytes 3145736 | tf_op jit(solution)/shard_map/ppermute | solution.py:27
  210.8 4.0 %collective-permute-start.21 = (bf16[8,256,256]{2,1,0:T(8,128)(2,1)}, bf16[8,256,256]{2,1,0:T(8,128)(2,1)S(1)}, u32[]{:S(2)}, u32[]{:S(2)}) collective-permute-start(bf16[8,256,256]{2,1,0:T(8,128)(2,1)} %sweep_amplitudes.2.own_ref), channel_id=1, source_target_pairs={{0,1},{1,0},{2,3},{3,2},{4,5},{5,4},{6,7},{7,6},{8,9},{9,8},{10,11... | collective-permute-start | bytes 3145736 | tf_op jit(solution)/shard_map/ppermute | solution.py:19
  210.8 16.7 %collective-permute-start.22 = (bf16[8,256,256]{2,1,0:T(8,128)(2,1)}, bf16[8,256,256]{2,1,0:T(8,128)(2,1)S(1)}, u32[]{:S(2)}, u32[]{:S(2)}) collective-permute-start(bf16[8,256,256]{2,1,0:T(8,128)(2,1)} %sweep_amplitudes.2.own_ref), channel_id=1, source_target_pairs={{1,4},{4,1},{5,8},{8,5},{9,12},{12,9},{3,6},{6,3},{7,10},{10,7},{1... | collective-permute-start | bytes 3145736 | tf_op jit(solution)/shard_map/ppermute | solution.py:27
  (32 other events, 391.0 us)

commit v2 on v1

v2 whole, which is shorter than its diff:
```python
import functools

import jax
import jax.numpy as jnp
from jax import lax
from jax.experimental import pallas as pl
from jax.experimental.pallas import tpu as pltpu
from jax.sharding import PartitionSpec as P

ITERS = 2
LINE = ("pair", "occ")
MIB = 1024 * 1024
F32 = jnp.float32
BF16 = jnp.bfloat16
ROWS = (((0,), (0,)), ((), ()))


def chip_mate(value):
    return lax.ppermute(value, "occ", [(0, 1), (1, 0)])


def line_mate(value):
    pairs = []
    for chip in range(lax.axis_size("pair") - 1):
        left, right = 2 * chip + 1, 2 * chip + 2
        pairs += [(left, right), (right, left)]
    return lax.ppermute(value, LINE, pairs)


def aux_terms(value):
    count = lax.axis_size("aux")
    step = 1
    while True:
        other = lax.ppermute(value, "aux", [(i, i ^ step) for i in range(count)])
        step *= 2
        if step >= count:
            return value, other
        value = (value.astype(F32) + other.astype(F32)).astype(BF16)


def in_vmem(count):
    return [pl.BlockSpec(memory_space=pltpu.VMEM)] * count


def in_smem(count):
    return [pl.BlockSpec(memory_space=pltpu.SMEM)] * count


def params(mib):
    return pltpu.CompilerParams(vmem_limit_bytes=mib * MIB)


def cost(flops, moved):
    return pl.CostEstimate(flops=flops, bytes_accessed=moved, transcendentals=0)


def tile_rows(rows):
    for tile in (2560, 1280, 1024, 640, 512, 256, 128):
        if rows % tile == 0:
            return tile
    return rows


def own_kernel(block_ref, out_ref):
    step = pl.program_id(0)

    @pl.when(step == 0)
    def _():
        out_ref[...] = jnp.zeros_like(out_ref)

    count = block_ref.shape[0]
    at = 0
    for left in range(count):
        for right in range(left + 1, count):
            out_ref[at] += lax.dot_general(block_ref[left], block_ref[right], ROWS, preferred_element_type=F32)
            at += 1


def own_products(blocks):
    count, rows, width = blocks.shape
    tile = tile_rows(rows)
    combos = count * (count - 1) // 2
    return pl.pallas_call(
        own_kernel,
        grid=(rows // tile,),
        in_specs=[pl.BlockSpec((count, tile, width), lambda t: (0, t, 0))],
        out_specs=pl.BlockSpec((combos, width, width), lambda t: (0, 0, 0)),
        out_shape=jax.ShapeDtypeStruct((combos, width, width), F32),
        compiler_params=params(16),
        cost_estimate=cost(2 * combos * rows * width * width, 2 * count * rows * width),
        name="own_products",
    )(blocks)


def mate_kernel(block_ref, mate_ref, out_ref):
    for orb in range(block_ref.shape[0]):
        out_ref[orb] = lax.dot_general(
            mate_ref[...], block_ref[orb], ROWS, preferred_element_type=F32
        ).astype(out_ref.dtype)


def mate_products(blocks, mate, dtype):
    count, rows, width = blocks.shape
    cols = mate.shape[1]
    return pl.pallas_call(
        mate_kernel,
        in_specs=in_vmem(2),
        out_specs=in_vmem(1)[0],
        out_shape=jax.ShapeDtypeStruct((count, cols, width), dtype),
        compiler_params=params(16),
        cost_estimate=cost(2 * count * rows * cols * width, 2 * rows * (count * width + cols)),
        name="mate_products",
    )(blocks, mate)


def pick(pieces, refs, orbital, index, into_ref, add=False):
    for (owner, start, size), group in zip(pieces, refs, strict=True):

        @pl.when(orbital == owner)
        def _(start=start, size=size, group=group):
            value = group[0][index].astype(F32)
            for ref in group[1:]:
                value = value + ref[index].astype(F32)
            into_ref[start : start + size] = value


def local_kernel(pieces, count, kind_ref, row_ref, col_ref, own_ref, *refs):
    n = len(pieces)
    sent, got = [(r,) for r in refs[:n]], [(r,) for r in refs[n : 2 * n]]
    out_ref, direct_ref, turned_ref = refs[2 * n :]

    def body(slot, carry):
        kind, row, col = kind_ref[slot], row_ref[slot], col_ref[slot]

        @pl.when(kind == 0)
        def _():
            low, high = jnp.minimum(row, col), jnp.maximum(row, col)
            value = own_ref[low * count - low * (low + 1) // 2 + high - low - 1]

            @pl.when(row < col)
            def _():
                out_ref[slot] = value.astype(BF16)

            @pl.when(row > col)
            def _():
                out_ref[slot] = value.T.astype(BF16)

        @pl.when(kind == 1)
        def _():
            pick(pieces, got, row, col, direct_ref)
            pick(pieces, sent, col, row, turned_ref)
            out_ref[slot] = (direct_ref[...] + turned_ref[...].T).astype(BF16)

        @pl.when(kind == 2)
        def _():
            out_ref[slot] = jnp.zeros(out_ref.shape[1:], BF16)

        return carry

    lax.fori_loop(0, out_ref.shape[0], body, 0)


def local_integrals(pieces, kind, row, col, own, sent, got):
    slots, width, count = kind.shape[0], own.shape[-1], sent[0].shape[0]
    return pl.pallas_call(
        functools.partial(local_kernel, pieces, count),
        in_specs=in_smem(3) + in_vmem(1 + len(sent) + len(got)),
        out_specs=in_vmem(1)[0],
        out_shape=jax.ShapeDtypeStruct((slots, width, width), BF16),
        scratch_shapes=[pltpu.VMEM((width, width), F32), pltpu.VMEM((width, width), F32)],
        compiler_params=params(16),
        cost_estimate=cost(4 * slots * width * width, 8 * MIB),
        name="local_integrals",
    )(kind, row, col, own, *sent, *got)


def cross_kernel(pieces, kind_ref, row_ref, col_ref, inverse_ref, base_ref, *refs):
    n = len(pieces)
    sent, got = list(zip(refs[:n], refs[n : 2 * n], strict=True)), [(r,) for r in refs[2 * n : 3 * n]]
    out_ref, rounded_ref, direct_ref, turned_ref = refs[3 * n :]

    def body(slot, carry):
        kind, row, col = kind_ref[slot], row_ref[slot], col_ref[slot]

        @pl.when(kind == 2)
        def _():
            pick(pieces, got, row, col, direct_ref)
            pick(pieces, sent, col, row, turned_ref)
            value = -(direct_ref[...] + turned_ref[...].T) * inverse_ref[slot]
            out_ref[slot] = value
            rounded_ref[slot] = value.astype(BF16)

        @pl.when(kind != 2)
        def _():
            value = base_ref[slot]
            out_ref[slot] = value
            rounded_ref[slot] = value.astype(BF16)

        return carry

    lax.fori_loop(0, out_ref.shape[0], body, 0)


def cross_amplitudes(pieces, kind, row, col, inverse, base, sent, others, got):
    slots, width, _ = base.shape
    return pl.pallas_call(
        functools.partial(cross_kernel, pieces),
        in_specs=in_smem(3) + in_vmem(2 + len(sent) + len(others) + len(got)),
        out_specs=in_vmem(2),
        out_shape=[jax.ShapeDtypeStruct((slots, width, width), F32), jax.ShapeDtypeStruct((slots, width, width), BF16)],
        scratch_shapes=[pltpu.VMEM((width, width), F32), pltpu.VMEM((width, width), F32)],
        compiler_params=params(24),
        cost_estimate=cost(4 * slots * width * width, 8 * MIB),
        name="cross_amplitudes",
    )(kind, row, col, inverse, base, *sent, *others, *got)


def sweep_kernel(at_ref, weight_ref, own_ref, chip_ref, line_ref, rows_ref, cols_ref, base_ref, inverse_ref, out_ref, held_ref):
    slots, neighbours = rows_ref.shape[:2]
    held_ref[:slots] = own_ref[...]
    held_ref[slots : 2 * slots] = chip_ref[...]
    held_ref[2 * slots :] = line_ref[...]
    for slot in range(slots):
        total = None
        for n in range(neighbours):
            source = held_ref[at_ref[slot, n]]
            selected = jnp.dot(rows_ref[slot, n], source, preferred_element_type=F32).astype(BF16)
            term = weight_ref[slot, n] * jnp.dot(selected, cols_ref[slot, n], preferred_element_type=F32)
            total = term if total is None else total + term
        out_ref[slot] = (base_ref[slot] + total * inverse_ref[slot]).astype(out_ref.dtype)


def sweep_amplitudes(at, weights, own, chip, line, row_match, col_match, base, inverse):
    slots, width, _ = own.shape
    neighbours = at.shape[1]
    return pl.pallas_call(
        sweep_kernel,
        in_specs=in_smem(2) + in_vmem(7),
        out_specs=in_vmem(1)[0],
        out_shape=jax.ShapeDtypeStruct((slots, width, width), BF16),
        scratch_shapes=[pltpu.VMEM((3 * slots, width, width), BF16)],
        compiler_params=params(32),
        cost_estimate=cost(4 * slots * neighbours * width**3, 16 * MIB),
        name="sweep_amplitudes",
    )(at, weights, own, chip, line, row_match, col_match, base, inverse)


def on_device(three_index, pair_orbs, live_pairs, domains, coupled, fock_coupling_weight, occ_energy, virt_energy):
    count, naux, width = three_index.shape
    slots = coupled.shape[0]
    half_rows = naux // 2
    owner = lax.axis_index(LINE)
    parity = lax.axis_index("occ")
    chip_owner = owner + 1 - 2 * parity

    pieces = [(j, 0, width) for j in range(count - 1)]
    pieces += [(count - 1, 0, width // 2), (count - 1, width // 2, width // 2)]
    away = (1 - parity) * half_rows
    sends = [
        lax.dynamic_slice(three_index, (j, away, start), (1, half_rows, size)).reshape(half_rows, size)
        for j, start, size in pieces
    ]
    from_line = [line_mate(s) for s in sends]
    three_index, domains, pair_orbs, coupled, *sends = lax.optimization_barrier(
        (three_index, domains, pair_orbs, coupled, *sends)
    )
    own = own_products(three_index)
    own, *sends = lax.optimization_barrier((own, *sends))
    from_chip = [chip_mate(s) for s in sends]
    block = lax.dynamic_slice(three_index, (0, parity * half_rows, 0), (count, half_rows, width))

    local = jnp.arange(slots, dtype=jnp.int32)
    pairs = lax.dynamic_slice_in_dim(pair_orbs, owner * slots, slots, 0)
    live = (local < live_pairs[owner]).astype(F32)[:, None, None]
    rows, cols = pairs[:, 0], pairs[:, 1]
    row_dom, col_dom = domains[rows], domains[cols]

    def kind_of(other):
        return jnp.where(other == owner, 0, jnp.where(other == chip_owner, 1, 2)).astype(jnp.int32)

    def energy(dom):
        listed = jnp.arange(virt_energy.shape[0], dtype=jnp.int32)
        return jnp.sum(jnp.where(dom[..., None] == listed, virt_energy, 0.0), axis=-1)

    gaps = (
        energy(row_dom)[:, :, None]
        + energy(col_dom)[:, None, :]
        - occ_energy[rows][:, None, None]
        - occ_energy[cols][:, None, None]
    )
    inverse = live / gaps
    source_rows = domains[pair_orbs[coupled, 0]]
    source_cols = domains[pair_orbs[coupled, 1]]
    row_match = (row_dom[:, None, :, None] == source_rows[:, :, None, :]).astype(BF16)
    col_match = (source_cols[:, :, :, None] == col_dom[:, None, None, :]).astype(BF16)
    kind, row, col = kind_of(cols // count), rows % count, cols % count
    at = kind_of(coupled // slots) * slots + coupled % slots

    chip_sent = [mate_products(block, m, F32) for m in from_chip]
    chip_got = [chip_mate(v) for v in chip_sent]
    part, other = aux_terms(local_integrals(pieces, kind, row, col, own, chip_sent, chip_got))
    base = -(part.astype(F32) + other.astype(F32)) * inverse

    terms = [aux_terms(mate_products(block, m, BF16)) for m in from_line]
    got = [line_mate((a.astype(F32) + b.astype(F32)).astype(BF16)) for a, b in terms]
    base, rounded = cross_amplitudes(
        pieces, kind, row, col, inverse, base, [a for a, _ in terms], [b for _, b in terms], got
    )
    for sweep in range(ITERS):
        rounded = sweep_amplitudes(
            at, fock_coupling_weight, rounded, chip_mate(rounded), line_mate(rounded),
            row_match, col_match, base, inverse,
        )
    return rounded


def solution(mesh):
    return jax.shard_map(
        on_device,
        mesh=mesh,
        in_specs=(
            P(("groups", "pair", "occ"), "aux", None),
            P("groups", None),
            P("groups"),
            P("groups", None),
            P(("groups", "pair", "occ"), None),
            P(("groups", "pair", "occ"), None),
            P("groups"),
            P("groups"),
        ),
        out_specs=P(("groups", "pair", "occ"), None, None),
        check_vma=False,
    )
```

time: 245 us -> 224 us (0.914)
  waiting for transfers between devices: 41.8 us -> 96.5 us
  Pallas kernels: 91.5 us -> 41 us
  local copies, waits for them, and re-layouts: 64.6 us -> 36.1 us
  starting transfers between devices: 35.3 us -> 41.4 us
    ppermute x8 -> x10, waiting for transfers between devices: 22.2 us -> 71.7 us  [line_mate(): return lax.ppermute(value, LINE, pairs)]
    pallas_call x9 -> x12, Pallas kernels: 80.4 us -> 34.8 us  [the longest x8 22.4 us: mate_products(): pl.pallas_call(mate_kernel, in_specs=in_vmem(2), out_specs=in_vmem(1)[0],...]
    gather x6 -> x2, local copies, waits for them, and re-layouts: 36.5 us -> 1.13 us  [on_device(): row_dom, col_dom = (domains[rows], domains[cols])]
    slice x1 -> x0, local copies, waits for them, and re-layouts: 12 us -> none  [on_device(): halves[j]]
    reshape x0 -> x2, local copies, waits for them, and re-layouts: none -> 9.92 us  [on_device(): lax.dynamic_slice(three_index, (j, away, start), (1, half_rows, size))]
    dynamic_slice x0 -> x1, local copies, waits for them, and re-layouts: none -> 7.68 us  [on_device(): lax.dynamic_slice(three_index, (0, parity * half_rows, 0), (count, half_r...]
    unnamed x69 -> x45, local copies, waits for them, and re-layouts: 5.41 us -> 12.1 us
    ppermute x8 -> x10, starting transfers between devices: 28.8 us -> 34.8 us  [line_mate(): return lax.ppermute(value, LINE, pairs)]
  transfers between devices with their start and end apart: 23 -> 25, of which waited for: 7 -> 7; matrix products, arithmetic and copies ran while one was open for 23% -> 10% of each run, Pallas kernels for 21% -> 11%
where the time goes in v2:
time: 224 us
  waiting for transfers between devices  96.5 us (43%)
  starting transfers between devices  41.4 us (18%)
  Pallas kernels  41 us (18%)
  local copies, waits for them, and re-layouts  36.1 us (16%)
  other arithmetic  8.36 us (4%)
    ppermute x10, waiting for transfers between devices, line_mate(): return lax.ppermute(value, LINE, pairs)  71.7 us
    ppermute x10, starting transfers between devices, line_mate(): return lax.ppermute(value, LINE, pairs)  34.8 us
    ppermute x5, waiting for transfers between devices, aux_terms(): other = lax.ppermute(value, 'aux', [(i, i ^ step) for i in range(count)])  24.7 us
    pallas_call x8, Pallas kernels, mate_products(): pl.pallas_call(mate_kernel, in_specs=in_vmem(2), out_specs=in_vmem(1)[0],...  22.4 us
    unnamed x45, local copies, waits for them, and re-layouts  12.1 us
    reshape x2, local copies, waits for them, and re-layouts, on_device(): lax.dynamic_slice(three_index, (j, away, start), (1, half_rows, size))  9.92 us
    pallas_call x2, Pallas kernels, sweep_amplitudes(): pl.pallas_call(sweep_kernel, in_specs=in_smem(2) + in_vmem(7), out_specs=...  8.82 us
    dynamic_slice x1, local copies, waits for them, and re-layouts, on_device(): lax.dynamic_slice(three_index, (0, parity * half_rows, 0), (count, half_r...  7.68 us
  transfers between devices with their start and end apart: 25, of which 7 were waited for; matrix products, arithmetic and copies ran while one was open for 10% of the time, Pallas kernels for 11%

profile of v2, /device:TPU:1, one launch (start us, length us, event | category | flops | bytes accessed | tf_op | source)
XLA Modules:
  0.0 223.9 jit_solution(16320994825947268470)
XLA Ops:
  0.0 5.7 %dynamic-slice_bitcast_fusion = (bf16[5120,256]{1,0:T(8,128)(2,1)}, bf16[5120,256]{1,0:T(8,128)(2,1)}) fusion(bf16[3,10240,256]{2,1,0:T(8,128)(2,1)} %block_ref, s32[]{:T(128)S(6)} %select_n.99), kind=kLoop, calls=%fused_computation.14 | loop fusion | bytes 10485764 | tf_op jit(solution)/shard_map/reshape | solution.py:260
  5.7 4.2 %dynamic-slice_bitcast_fusion.2 = (bf16[5120,128]{1,0:T(8,128)(2,1)}, bf16[5120,128]{1,0:T(8,128)(2,1)}) fusion(bf16[3,10240,256]{2,1,0:T(8,128)(2,1)} %block_ref, s32[]{:T(128)S(6)} %select_n.99), kind=kLoop, calls=%fused_computation.18 | loop fusion | bytes 5242884 | tf_op jit(solution)/shard_map/reshape | solution.py:260
  10.7 6.1 %own_products.1.own_ref = f32[3,256,256]{2,1,0:T(8,128)S(1)} custom-call(bf16[3,10240,256]{2,1,0:T(8,128)(2,1)S(1)} %copy-done.3), custom_call_target="tpu_custom_call" | custom-call | flops 4026531840 | bytes 15728640 | tf_op jit(solution)/shard_map/own_products/pallas_call | solution.py:83
  17.4 4.6 %collective-permute-start.11 = (bf16[5120,128]{1,0:T(8,128)(2,1)}, bf16[5120,128]{1,0:T(8,128)(2,1)}, u32[]{:S(2)}, u32[]{:S(2)}) collective-permute-start(bf16[5120,128]{1,0:T(8,128)(2,1)} %get-tuple-element.31), channel_id=1, source_target_pairs={{1,4},{4,1},{5,8},{8,5},{9,12},{12,9},{3,6},{6,3},{7,10},{10,7},{1... | collective-permute-start | bytes 3932168 | tf_op jit(solution)/shard_map/ppermute | solution.py:27
  25.2 4.3 %select_reduce_fusion.1 = (f32[8,256]{1,0:T(8,128)S(1)}, f32[8,256]{1,0:T(8,128)S(1)}) fusion(f32[1792]{0:T(1024)S(1)} %copy-done.18, s32[8,256]{1,0:T(8,128)S(1)} %gather_fusion, s32[8,256]{1,0:T(8,128)S(1)} %gather_fusion.1), kind=kLoop, calls=%fused_computation.10 | loop fusion | flops 22016000 | bytes 39936 | tf_op jit(solution)/shard_map/reduce_sum | solution.py:283
  29.6 7.9 %collective-permute-done.11.mate_ref = bf16[5120,128]{1,0:T(8,128)(2,1)} collective-permute-done((bf16[5120,128]{1,0:T(8,128)(2,1)}, bf16[5120,128]{1,0:T(8,128)(2,1)}, u32[]{:S(2)}, u32[]{:S(2)}) %collective-permute-start.11) | collective-permute-done | bytes 1310752 | tf_op jit(solution)/shard_map/ppermute | solution.py:27
  37.6 3.6 %collective-permute-start.9 = (bf16[5120,256]{1,0:T(8,128)(2,1)}, bf16[5120,256]{1,0:T(8,128)(2,1)}, u32[]{:S(2)}, u32[]{:S(2)}) collective-permute-start(bf16[5120,256]{1,0:T(8,128)(2,1)} %get-tuple-element.29), channel_id=1, source_target_pairs={{1,4},{4,1},{5,8},{8,5},{9,12},{12,9},{3,6},{6,3},{7,10},{10,7},{1... | collective-permute-start | bytes 7864328 | tf_op jit(solution)/shard_map/ppermute | solution.py:27
  44.3 7.7 %constant_dynamic-slice_fusion.block_ref = bf16[3,5120,256]{2,1,0:T(8,128)(2,1)} fusion(bf16[3,10240,256]{2,1,0:T(8,128)(2,1)} %block_ref, s32[]{:T(128)S(6)} %select_n.115), kind=kLoop, calls=%fused_computation.51 | loop fusion | bytes 15728644 | tf_op jit(solution)/shard_map/dynamic_slice | solution.py:270
  52.0 3.2 %copy-done.1 = bf16[3,5120,256]{2,1,0:T(8,128)(2,1)S(1)} copy-done((bf16[3,5120,256]{2,1,0:T(8,128)(2,1)S(1)}, bf16[3,5120,256]{2,1,0:T(8,128)(2,1)}, u32[]{:S(2)}) %copy-start.1) | copy-done | bytes 7864344
  64.5 4.1 %mate_products.8.refs_0_ = f32[3,256,256]{2,1,0:T(8,128)S(1)} custom-call(bf16[3,5120,256]{2,1,0:T(8,128)(2,1)S(1)} %copy-done.1, bf16[5120,256]{1,0:T(8,128)(2,1)} %collective-permute-done.mate_ref), custom_call_target="tpu_custom_call" | custom-call | flops 2013265920 | bytes 10485760 | tf_op jit(solution)/shard_map/mate_products/pallas_call | solution.py:105
  68.6 39.1 %collective-permute-done.12.mate_ref = bf16[5120,128]{1,0:T(8,128)(2,1)S(1)} collective-permute-done((bf16[5120,128]{1,0:T(8,128)(2,1)}, bf16[5120,128]{1,0:T(8,128)(2,1)S(1)}, u32[]{:S(2)}, u32[]{:S(2)}) %collective-permute-start.12) | collective-permute-done | bytes 1310752 | tf_op jit(solution)/shard_map/ppermute | solution.py:27
  122.1 4.0 %collective-permute-start.19 = (bf16[3,128,256]{2,1,0:T(8,128)(2,1)S(1)}, bf16[3,128,256]{2,1,0:T(8,128)(2,1)S(1)}, u32[]{:S(2)}, u32[]{:S(2)}) collective-permute-start(bf16[3,128,256]{2,1,0:T(8,128)(2,1)S(1)} %add_convert_fusion.3), channel_id=1, source_target_pairs={{1,4},{4,1},{5,8},{8,5},{9,12},{12,9},{3,6},{6,3},{7,10},{10,7},{1... | collective-permute-start | bytes 589832 | tf_op jit(solution)/shard_map/ppermute | solution.py:27
  128.8 4.1 %mate_products.13.refs_1_ = bf16[3,256,256]{2,1,0:T(8,128)(2,1)S(1)} custom-call(bf16[3,5120,256]{2,1,0:T(8,128)(2,1)S(1)} %bitcast.35, bf16[5120,256]{1,0:T(8,128)(2,1)} %collective-permute-done.10.mate_ref), custom_call_target="tpu_custom_call" | custom-call | flops 2013265920 | bytes 10485760 | tf_op jit(solution)/shard_map/mate_products/pallas_call | solution.py:105
  134.2 4.1 %mate_products.12.refs_0_ = bf16[3,256,256]{2,1,0:T(8,128)(2,1)S(1)} custom-call(bf16[3,5120,256]{2,1,0:T(8,128)(2,1)S(1)} %bitcast.35, bf16[5120,256]{1,0:T(8,128)(2,1)} %collective-permute-done.9.mate_ref), custom_call_target="tpu_custom_call" | custom-call | flops 2013265920 | bytes 10485760 | tf_op jit(solution)/shard_map/mate_products/pallas_call | solution.py:105
  141.5 20.8 %collective-permute-done.14.refs_5_ = bf16[3,256,256]{2,1,0:T(8,128)(2,1)S(1)} collective-permute-done((bf16[3,256,256]{2,1,0:T(8,128)(2,1)S(1)}, bf16[3,256,256]{2,1,0:T(8,128)(2,1)S(1)}, u32[]{:S(2)}, u32[]{:S(2)}) %collective-permute-start.14) | collective-permute-done | bytes 393248 | tf_op jit(solution)/shard_map/ppermute | solution.py:34
  164.8 4.0 %collective-permute-done.13.refs_4_ = bf16[3,256,256]{2,1,0:T(8,128)(2,1)S(1)} collective-permute-done((bf16[3,256,256]{2,1,0:T(8,128)(2,1)S(1)}, bf16[3,256,256]{2,1,0:T(8,128)(2,1)S(1)}, u32[]{:S(2)}, u32[]{:S(2)}) %collective-permute-start.13) | collective-permute-done | bytes 393248 | tf_op jit(solution)/shard_map/ppermute | solution.py:34
  168.9 4.3 %collective-permute-start.17 = (bf16[3,256,256]{2,1,0:T(8,128)(2,1)S(1)}, bf16[3,256,256]{2,1,0:T(8,128)(2,1)S(1)}, u32[]{:S(2)}, u32[]{:S(2)}) collective-permute-start(bf16[3,256,256]{2,1,0:T(8,128)(2,1)S(1)} %add_convert_fusion.1), channel_id=1, source_target_pairs={{1,4},{4,1},{5,8},{8,5},{9,12},{12,9},{3,6},{6,3},{7,10},{10,7},{1... | collective-permute-start | bytes 1179656 | tf_op jit(solution)/shard_map/ppermute | solution.py:27
  174.1 4.6 %collective-permute-done.17.refs_8_ = bf16[3,256,256]{2,1,0:T(8,128)(2,1)S(1)} collective-permute-done((bf16[3,256,256]{2,1,0:T(8,128)(2,1)S(1)}, bf16[3,256,256]{2,1,0:T(8,128)(2,1)S(1)}, u32[]{:S(2)}, u32[]{:S(2)}) %collective-permute-start.17) | collective-permute-done | bytes 393248 | tf_op jit(solution)/shard_map/ppermute | solution.py:27
  181.3 4.9 %collective-permute-start.22 = (bf16[8,256,256]{2,1,0:T(8,128)(2,1)S(1)}, bf16[8,256,256]{2,1,0:T(8,128)(2,1)}, u32[]{:S(2)}, u32[]{:S(2)}) collective-permute-start(bf16[8,256,256]{2,1,0:T(8,128)(2,1)S(1)} %get-tuple-element.33.own_ref), channel_id=1, source_target_pairs={{1,4},{4,1},{5,8},{8,5},{9,12},{12,9},{3,6},{6,3},{7,10},{10,7},{1... | collective-permute-start | bytes 3145736 | tf_op jit(solution)/shard_map/ppermute | solution.py:27
  190.9 7.9 %collective-permute-done.22.line_ref = bf16[8,256,256]{2,1,0:T(8,128)(2,1)} collective-permute-done((bf16[8,256,256]{2,1,0:T(8,128)(2,1)S(1)}, bf16[8,256,256]{2,1,0:T(8,128)(2,1)}, u32[]{:S(2)}, u32[]{:S(2)}) %collective-permute-start.22) | collective-permute-done | bytes 1048608 | tf_op jit(solution)/shard_map/ppermute | solution.py:27
  198.8 4.4 %sweep_amplitudes.2.own_ref = bf16[8,256,256]{2,1,0:T(8,128)(2,1)S(1)} custom-call(s32[8,4]{1,0:T(8,128)S(1)} %get-tuple-element.45.at_ref, f32[8,4]{1,0:T(8,128)S(1)} %copy.32.weight_ref, bf16[8,256,256]{2,1,0:T(8,128)(2,1)S(1)} %get-tuple-element.33.own_ref, bf16[8,256,256]{2,1,0:T(8,128)(2,1)} %collective-permute-done.21.chip_ref, ...), custom_call_target="tpu_custom_call" | custom-call | flops 2147483648 | bytes 16777216 | tf_op jit(solution)/shard_map/sweep_amplitudes/pallas_call | solution.py:236
  203.2 4.0 %collective-permute-start.24 = (bf16[8,256,256]{2,1,0:T(8,128)(2,1)S(1)}, bf16[8,256,256]{2,1,0:T(8,128)(2,1)S(1)}, u32[]{:S(2)}, u32[]{:S(2)}) collective-permute-start(bf16[8,256,256]{2,1,0:T(8,128)(2,1)S(1)} %sweep_amplitudes.2.own_ref), channel_id=1, source_target_pairs={{1,4},{4,1},{5,8},{8,5},{9,12},{12,9},{3,6},{6,3},{7,10},{10,7},{1... | collective-permute-start | bytes 3145736 | tf_op jit(solution)/shard_map/ppermute | solution.py:27
  207.3 12.2 %collective-permute-done.24.line_ref = bf16[8,256,256]{2,1,0:T(8,128)(2,1)S(1)} collective-permute-done((bf16[8,256,256]{2,1,0:T(8,128)(2,1)S(1)}, bf16[8,256,256]{2,1,0:T(8,128)(2,1)S(1)}, u32[]{:S(2)}, u32[]{:S(2)}) %collective-permute-start.24) | collective-permute-done | bytes 1048608 | tf_op jit(solution)/shard_map/ppermute | solution.py:27
  219.5 4.5 %sweep_amplitudes.3 = bf16[8,256,256]{2,1,0:T(8,128)(2,1)} custom-call(s32[8,4]{1,0:T(8,128)S(1)} %get-tuple-element.45.at_ref, f32[8,4]{1,0:T(8,128)S(1)} %copy.32.weight_ref, bf16[8,256,256]{2,1,0:T(8,128)(2,1)S(1)} %sweep_amplitudes.2.own_ref, bf16[8,256,256]{2,1,0:T(8,128)(2,1)S(1)} %collective-permute-done.23.chip_ref, ...), custom_call_target="tpu_custom_call" | custom-call | flops 2147483648 | bytes 16777216 | tf_op jit(solution)/shard_map/sweep_amplitudes/pallas_call | solution.py:236
  (124 shorter events, 49.2 us)
Async XLA Ops:
  16.8 27.4 %collective-permute-start.1 = (bf16[5120,256]{1,0:T(8,128)(2,1)}, bf16[5120,256]{1,0:T(8,128)(2,1)S(1)}, u32[]{:S(2)}, u32[]{:S(2)}) collective-permute-start(bf16[5120,256]{1,0:T(8,128)(2,1)} %get-tuple-element.30), channel_id=1, source_target_pairs={{0,1},{1,0},{2,3},{3,2},{4,5},{5,4},{6,7},{7,6},{8,9},{9,8},{10,11... | collective-permute-start | bytes 7864328 | tf_op jit(solution)/shard_map/ppermute | solution.py:19
  16.9 43.9 %collective-permute-start = (bf16[5120,256]{1,0:T(8,128)(2,1)}, bf16[5120,256]{1,0:T(8,128)(2,1)}, u32[]{:S(2)}, u32[]{:S(2)}) collective-permute-start(bf16[5120,256]{1,0:T(8,128)(2,1)} %get-tuple-element.29), channel_id=1, source_target_pairs={{0,1},{1,0},{2,3},{3,2},{4,5},{5,4},{6,7},{7,6},{8,9},{9,8},{10,11... | collective-permute-start | bytes 7864328 | tf_op jit(solution)/shard_map/ppermute | solution.py:19
  17.4 20.2 %collective-permute-start.11 = (bf16[5120,128]{1,0:T(8,128)(2,1)}, bf16[5120,128]{1,0:T(8,128)(2,1)}, u32[]{:S(2)}, u32[]{:S(2)}) collective-permute-start(bf16[5120,128]{1,0:T(8,128)(2,1)} %get-tuple-element.31), channel_id=1, source_target_pairs={{1,4},{4,1},{5,8},{8,5},{9,12},{12,9},{3,6},{6,3},{7,10},{10,7},{1... | collective-permute-start | bytes 3932168 | tf_op jit(solution)/shard_map/ppermute | solution.py:27
  22.0 106.8 %collective-permute-start.10 = (bf16[5120,256]{1,0:T(8,128)(2,1)}, bf16[5120,256]{1,0:T(8,128)(2,1)}, u32[]{:S(2)}, u32[]{:S(2)}) collective-permute-start(bf16[5120,256]{1,0:T(8,128)(2,1)} %get-tuple-element.30), channel_id=1, source_target_pairs={{1,4},{4,1},{5,8},{8,5},{9,12},{12,9},{3,6},{6,3},{7,10},{10,7},{1... | collective-permute-start | bytes 7864328 | tf_op jit(solution)/shard_map/ppermute | solution.py:27
  23.9 18.2 %collective-permute-start.3 = (bf16[5120,128]{1,0:T(8,128)(2,1)}, bf16[5120,128]{1,0:T(8,128)(2,1)}, u32[]{:S(2)}, u32[]{:S(2)}) collective-permute-start(bf16[5120,128]{1,0:T(8,128)(2,1)} %get-tuple-element.32), channel_id=1, source_target_pairs={{0,1},{1,0},{2,3},{3,2},{4,5},{5,4},{6,7},{7,6},{8,9},{9,8},{10,11... | collective-permute-start | bytes 3932168 | tf_op jit(solution)/shard_map/ppermute | solution.py:19
  37.6 96.6 %collective-permute-start.9 = (bf16[5120,256]{1,0:T(8,128)(2,1)}, bf16[5120,256]{1,0:T(8,128)(2,1)}, u32[]{:S(2)}, u32[]{:S(2)}) collective-permute-start(bf16[5120,256]{1,0:T(8,128)(2,1)} %get-tuple-element.29), channel_id=1, source_target_pairs={{1,4},{4,1},{5,8},{8,5},{9,12},{12,9},{3,6},{6,3},{7,10},{10,7},{1... | collective-permute-start | bytes 7864328 | tf_op jit(solution)/shard_map/ppermute | solution.py:27
  42.1 65.5 %collective-permute-start.12 = (bf16[5120,128]{1,0:T(8,128)(2,1)}, bf16[5120,128]{1,0:T(8,128)(2,1)S(1)}, u32[]{:S(2)}, u32[]{:S(2)}) collective-permute-start(bf16[5120,128]{1,0:T(8,128)(2,1)} %get-tuple-element.32), channel_id=1, source_target_pairs={{1,4},{4,1},{5,8},{8,5},{9,12},{12,9},{3,6},{6,3},{7,10},{10,7},{1... | collective-permute-start | bytes 3932168 | tf_op jit(solution)/shard_map/ppermute | solution.py:27
  44.3 64.5 %collective-permute-start.2 = (bf16[5120,128]{1,0:T(8,128)(2,1)}, bf16[5120,128]{1,0:T(8,128)(2,1)S(1)}, u32[]{:S(2)}, u32[]{:S(2)}) collective-permute-start(bf16[5120,128]{1,0:T(8,128)(2,1)} %get-tuple-element.31), channel_id=1, source_target_pairs={{0,1},{1,0},{2,3},{3,2},{4,5},{5,4},{6,7},{7,6},{8,9},{9,8},{10,11... | collective-permute-start | bytes 3932168 | tf_op jit(solution)/shard_map/ppermute | solution.py:19
  60.8 49.5 %collective-permute-start.15 = (bf16[3,128,256]{2,1,0:T(8,128)(2,1)S(1)}, bf16[3,128,256]{2,1,0:T(8,128)(2,1)S(1)}, u32[]{:S(2)}, u32[]{:S(2)}) collective-permute-start(bf16[3,128,256]{2,1,0:T(8,128)(2,1)S(1)} %mate_products.14.refs_2_), channel_id=1, source_target_pairs={{0,2},{2,0},{1,3},{3,1},{4,6},{6,4},{5,7},{7,5},{8,10},{10,8},{9,1... | collective-permute-start | bytes 589832 | tf_op jit(solution)/shard_map/ppermute | solution.py:34
  108.8 9.4 %collective-permute-start.7 = (f32[3,128,256]{2,1,0:T(8,128)S(1)}, f32[3,128,256]{2,1,0:T(8,128)S(1)}, u32[]{:S(2)}, u32[]{:S(2)}) collective-permute-start(f32[3,128,256]{2,1,0:T(8,128)S(1)} %mate_products.11.refs_3_), channel_id=1, source_target_pairs={{0,1},{1,0},{2,3},{3,2},{4,5},{5,4},{6,7},{7,6},{8,9},{9,8},{10,11... | collective-permute-start | bytes 1179656 | tf_op jit(solution)/shard_map/ppermute | solution.py:19
  109.8 12.3 %collective-permute-start.5 = (f32[3,256,256]{2,1,0:T(8,128)S(1)}, f32[3,256,256]{2,1,0:T(8,128)}, u32[]{:S(2)}, u32[]{:S(2)}) collective-permute-start(f32[3,256,256]{2,1,0:T(8,128)S(1)} %mate_products.9.refs_1_), channel_id=1, source_target_pairs={{0,1},{1,0},{2,3},{3,2},{4,5},{5,4},{6,7},{7,6},{8,9},{9,8},{10,11... | collective-permute-start | bytes 2359304 | tf_op jit(solution)/shard_map/ppermute | solution.py:19
  110.3 15.8 %collective-permute-start.4 = (f32[3,256,256]{2,1,0:T(8,128)S(1)}, f32[3,256,256]{2,1,0:T(8,128)}, u32[]{:S(2)}, u32[]{:S(2)}) collective-permute-start(f32[3,256,256]{2,1,0:T(8,128)S(1)} %mate_products.8.refs_0_), channel_id=1, source_target_pairs={{0,1},{1,0},{2,3},{3,2},{4,5},{5,4},{6,7},{7,6},{8,9},{9,8},{10,11... | collective-permute-start | bytes 2359304 | tf_op jit(solution)/shard_map/ppermute | solution.py:19
  120.7 17.8 %collective-permute-start.16 = (bf16[3,128,256]{2,1,0:T(8,128)(2,1)S(1)}, bf16[3,128,256]{2,1,0:T(8,128)(2,1)S(1)}, u32[]{:S(2)}, u32[]{:S(2)}) collective-permute-start(bf16[3,128,256]{2,1,0:T(8,128)(2,1)S(1)} %mate_products.15.refs_3_), channel_id=1, source_target_pairs={{0,2},{2,0},{1,3},{3,1},{4,6},{6,4},{5,7},{7,5},{8,10},{10,8},{9,1... | collective-permute-start | bytes 589832 | tf_op jit(solution)/shard_map/ppermute | solution.py:34
  122.1 52.0 %collective-permute-start.19 = (bf16[3,128,256]{2,1,0:T(8,128)(2,1)S(1)}, bf16[3,128,256]{2,1,0:T(8,128)(2,1)S(1)}, u32[]{:S(2)}, u32[]{:S(2)}) collective-permute-start(bf16[3,128,256]{2,1,0:T(8,128)(2,1)S(1)} %add_convert_fusion.3), channel_id=1, source_target_pairs={{1,4},{4,1},{5,8},{8,5},{9,12},{12,9},{3,6},{6,3},{7,10},{10,7},{1... | collective-permute-start | bytes 589832 | tf_op jit(solution)/shard_map/ppermute | solution.py:27
  128.5 44.8 %collective-permute-start.8 = (bf16[8,256,256]{2,1,0:T(8,128)(2,1)S(1)}, bf16[8,256,256]{2,1,0:T(8,128)(2,1)S(1)}, u32[]{:S(2)}, u32[]{:S(2)}) collective-permute-start(bf16[8,256,256]{2,1,0:T(8,128)(2,1)S(1)} %local_integrals.1), channel_id=1, source_target_pairs={{0,2},{2,0},{1,3},{3,1},{4,6},{6,4},{5,7},{7,5},{8,10},{10,8},{9,1... | collective-permute-start | bytes 3145736 | tf_op jit(solution)/shard_map/ppermute | solution.py:34
  132.9 29.3 %collective-permute-start.14 = (bf16[3,256,256]{2,1,0:T(8,128)(2,1)S(1)}, bf16[3,256,256]{2,1,0:T(8,128)(2,1)S(1)}, u32[]{:S(2)}, u32[]{:S(2)}) collective-permute-start(bf16[3,256,256]{2,1,0:T(8,128)(2,1)S(1)} %mate_products.13.refs_1_), channel_id=1, source_target_pairs={{0,2},{2,0},{1,3},{3,1},{4,6},{6,4},{5,7},{7,5},{8,10},{10,8},{9,1... | collective-permute-start | bytes 1179656 | tf_op jit(solution)/shard_map/ppermute | solution.py:34
  138.2 30.6 %collective-permute-start.13 = (bf16[3,256,256]{2,1,0:T(8,128)(2,1)S(1)}, bf16[3,256,256]{2,1,0:T(8,128)(2,1)S(1)}, u32[]{:S(2)}, u32[]{:S(2)}) collective-permute-start(bf16[3,256,256]{2,1,0:T(8,128)(2,1)S(1)} %mate_products.12.refs_0_), channel_id=1, source_target_pairs={{0,2},{2,0},{1,3},{3,1},{4,6},{6,4},{5,7},{7,5},{8,10},{10,8},{9,1... | collective-permute-start | bytes 1179656 | tf_op jit(solution)/shard_map/ppermute | solution.py:34
  138.6 35.5 %collective-permute-start.20 = (bf16[3,128,256]{2,1,0:T(8,128)(2,1)S(1)}, bf16[3,128,256]{2,1,0:T(8,128)(2,1)S(1)}, u32[]{:S(2)}, u32[]{:S(2)}) collective-permute-start(bf16[3,128,256]{2,1,0:T(8,128)(2,1)S(1)} %add_convert_fusion.2), channel_id=1, source_target_pairs={{1,4},{4,1},{5,8},{8,5},{9,12},{12,9},{3,6},{6,3},{7,10},{10,7},{1... | collective-permute-start | bytes 589832 | tf_op jit(solution)/shard_map/ppermute | solution.py:27
  162.3 11.8 %collective-permute-start.18 = (bf16[3,256,256]{2,1,0:T(8,128)(2,1)S(1)}, bf16[3,256,256]{2,1,0:T(8,128)(2,1)S(1)}, u32[]{:S(2)}, u32[]{:S(2)}) collective-permute-start(bf16[3,256,256]{2,1,0:T(8,128)(2,1)S(1)} %add_convert_fusion), channel_id=1, source_target_pairs={{1,4},{4,1},{5,8},{8,5},{9,12},{12,9},{3,6},{6,3},{7,10},{10,7},{1... | collective-permute-start | bytes 1179656 | tf_op jit(solution)/shard_map/ppermute | solution.py:27
  168.9 9.8 %collective-permute-start.17 = (bf16[3,256,256]{2,1,0:T(8,128)(2,1)S(1)}, bf16[3,256,256]{2,1,0:T(8,128)(2,1)S(1)}, u32[]{:S(2)}, u32[]{:S(2)}) collective-permute-start(bf16[3,256,256]{2,1,0:T(8,128)(2,1)S(1)} %add_convert_fusion.1), channel_id=1, source_target_pairs={{1,4},{4,1},{5,8},{8,5},{9,12},{12,9},{3,6},{6,3},{7,10},{10,7},{1... | collective-permute-start | bytes 1179656 | tf_op jit(solution)/shard_map/ppermute | solution.py:27
  181.3 9.6 %collective-permute-start.21 = (bf16[8,256,256]{2,1,0:T(8,128)(2,1)S(1)}, bf16[8,256,256]{2,1,0:T(8,128)(2,1)}, u32[]{:S(2)}, u32[]{:S(2)}) collective-permute-start(bf16[8,256,256]{2,1,0:T(8,128)(2,1)S(1)} %get-tuple-element.33.own_ref), channel_id=1, source_target_pairs={{0,1},{1,0},{2,3},{3,2},{4,5},{5,4},{6,7},{7,6},{8,9},{9,8},{10,11... | collective-permute-start | bytes 3145736 | tf_op jit(solution)/shard_map/ppermute | solution.py:19
  181.3 17.5 %collective-permute-start.22 = (bf16[8,256,256]{2,1,0:T(8,128)(2,1)S(1)}, bf16[8,256,256]{2,1,0:T(8,128)(2,1)}, u32[]{:S(2)}, u32[]{:S(2)}) collective-permute-start(bf16[8,256,256]{2,1,0:T(8,128)(2,1)S(1)} %get-tuple-element.33.own_ref), channel_id=1, source_target_pairs={{1,4},{4,1},{5,8},{8,5},{9,12},{12,9},{3,6},{6,3},{7,10},{10,7},{1... | collective-permute-start | bytes 3145736 | tf_op jit(solution)/shard_map/ppermute | solution.py:27
  203.2 4.1 %collective-permute-start.23 = (bf16[8,256,256]{2,1,0:T(8,128)(2,1)S(1)}, bf16[8,256,256]{2,1,0:T(8,128)(2,1)S(1)}, u32[]{:S(2)}, u32[]{:S(2)}) collective-permute-start(bf16[8,256,256]{2,1,0:T(8,128)(2,1)S(1)} %sweep_amplitudes.2.own_ref), channel_id=1, source_target_pairs={{0,1},{1,0},{2,3},{3,2},{4,5},{5,4},{6,7},{7,6},{8,9},{9,8},{10,11... | collective-permute-start | bytes 3145736 | tf_op jit(solution)/shard_map/ppermute | solution.py:19
  203.2 16.2 %collective-permute-start.24 = (bf16[8,256,256]{2,1,0:T(8,128)(2,1)S(1)}, bf16[8,256,256]{2,1,0:T(8,128)(2,1)S(1)}, u32[]{:S(2)}, u32[]{:S(2)}) collective-permute-start(bf16[8,256,256]{2,1,0:T(8,128)(2,1)S(1)} %sweep_amplitudes.2.own_ref), channel_id=1, source_target_pairs={{1,4},{4,1},{5,8},{8,5},{9,12},{12,9},{3,6},{6,3},{7,10},{10,7},{1... | collective-permute-start | bytes 3145736 | tf_op jit(solution)/shard_map/ppermute | solution.py:27
  (23 other events, 244.4 us)

commit v3 on v2

v3 whole, which is shorter than its diff:
```python
import functools

import jax
import jax.numpy as jnp
from jax import lax
from jax.experimental import pallas as pl
from jax.experimental.pallas import tpu as pltpu
from jax.sharding import PartitionSpec as P

ITERS = 2
LINE = ("pair", "occ")
MIB = 1024 * 1024
F32 = jnp.float32
BF16 = jnp.bfloat16
ROWS = (((0,), (0,)), ((), ()))


def chip_mate(value):
    return lax.ppermute(value, "occ", [(0, 1), (1, 0)])


def line_mate(value):
    pairs = []
    for chip in range(lax.axis_size("pair") - 1):
        left, right = 2 * chip + 1, 2 * chip + 2
        pairs += [(left, right), (right, left)]
    return lax.ppermute(value, LINE, pairs)


def aux_terms(value):
    count = lax.axis_size("aux")
    step = 1
    while True:
        other = lax.ppermute(value, "aux", [(i, i ^ step) for i in range(count)])
        step *= 2
        if step >= count:
            return value, other
        value = (value.astype(F32) + other.astype(F32)).astype(BF16)


def in_vmem(count):
    return [pl.BlockSpec(memory_space=pltpu.VMEM)] * count


def in_smem(count):
    return [pl.BlockSpec(memory_space=pltpu.SMEM)] * count


def params(mib):
    return pltpu.CompilerParams(vmem_limit_bytes=mib * MIB)


def cost(flops, moved):
    return pl.CostEstimate(flops=flops // 1024, bytes_accessed=moved // 1024, transcendentals=0)


def after(value, *earlier):
    return lax.optimization_barrier((value, *earlier))[0]


CHUNKS = 2


def chunk(k, rows):
    return pl.ds(k * (rows // CHUNKS), rows // CHUNKS)


def half_chunk(half_ref, k, rows):
    size = rows // CHUNKS
    return pl.ds(pl.multiple_of(half_ref[0] * rows + k * size, size), size)


def tally(total_ref, out_ref, k, where, term):
    if k:
        term = term + total_ref[where]
    if k < CHUNKS - 1:
        total_ref[where] = term
    else:
        out_ref[where] = term.astype(out_ref.dtype)


def pairs_of(count):
    return [(i, j) for i in range(count) for j in range(i + 1, count)]


def send_kernel(half_ref, blocks_ref, *refs):
    count = blocks_ref.shape[0]
    sends, tail_ref, own_ref, block_ref, total_ref, arrived, written = refs[:count], *refs[count:]
    rows, cut = tail_ref.shape

    def read(k):
        block = blocks_ref.at[:, half_chunk(half_ref, k, rows)]
        return pltpu.make_async_copy(block, block_ref.at[:, chunk(k, rows)], arrived.at[k])

    def writes(k):
        part = chunk(k, rows)
        for j in range(count):
            yield pltpu.make_async_copy(block_ref.at[j, part], sends[j].at[part], written.at[k, j])
        tail = block_ref.at[count - 1, part, pl.ds(block_ref.shape[2] - cut, cut)]
        yield pltpu.make_async_copy(tail, tail_ref.at[part], written.at[k, count])

    for k in range(CHUNKS):
        read(k).start()
    for k in range(CHUNKS):
        read(k).wait()
        for copy in writes(k):
            copy.start()
        part = chunk(k, rows)
        for at, (i, j) in enumerate(pairs_of(count)):
            term = lax.dot_general(block_ref[i, part], block_ref[j, part], ROWS, preferred_element_type=F32)
            tally(total_ref, own_ref, k, at, term)
    for k in range(CHUNKS):
        for copy in writes(k):
            copy.wait()


def send_blocks(half, blocks, cut):
    count, rows, width = blocks.shape
    rows, combos = rows // 2, count * (count - 1) // 2
    anywhere = pl.BlockSpec(memory_space=pl.ANY)
    return pl.pallas_call(
        send_kernel,
        in_specs=in_smem(1) + [anywhere],
        out_specs=[anywhere] * (count + 1) + in_vmem(1),
        out_shape=[jax.ShapeDtypeStruct((rows, width), BF16)] * count
        + [jax.ShapeDtypeStruct((rows, cut), BF16), jax.ShapeDtypeStruct((combos, width, width), F32)],
        scratch_shapes=[
            pltpu.VMEM((count, rows, width), BF16),
            pltpu.VMEM((combos, width, width), F32),
            pltpu.SemaphoreType.DMA((CHUNKS,)),
            pltpu.SemaphoreType.DMA((CHUNKS, count + 1)),
        ],
        compiler_params=params(49),
        cost_estimate=cost(2 * combos * rows * width * width, 4 * count * rows * width),
        name="send_blocks",
    )(half, blocks)


def mate_kernel(n, with_own, half_ref, blocks_ref, *refs):
    mates, refs = refs[:n], refs[n:]
    if with_own:
        (away_ref, out_ref, own_ref), refs = refs[:3], refs[3:]
    else:
        out_ref, refs = refs[0], refs[1:]
    held, (block_ref, total_ref, arrived, *own_total) = refs[:n], refs[n:]
    count, rows, _ = block_ref.shape

    def copies(k):
        part = chunk(k, rows)
        block = blocks_ref.at[:, half_chunk(half_ref, k, rows)]
        yield pltpu.make_async_copy(block, block_ref.at[:, part], arrived.at[k, 0])
        for m in range(n):
            yield pltpu.make_async_copy(mates[m].at[part], held[m].at[part], arrived.at[k, m + 1])

    for k in range(CHUNKS):
        for copy in copies(k):
            copy.start()
    for k in range(CHUNKS):
        for copy in copies(k):
            copy.wait()
        part = chunk(k, rows)
        at = 0
        for mate_ref in held:
            cols = mate_ref.shape[1]
            for orb in range(count):
                term = lax.dot_general(mate_ref[part], block_ref[orb, part], ROWS, preferred_element_type=F32)
                tally(total_ref, out_ref, k, (orb, slice(at, at + cols)), term)
            at += cols
        if with_own:
            for at, (i, j) in enumerate(pairs_of(count)):
                term = lax.dot_general(block_ref[i, part], block_ref[j, part], ROWS, preferred_element_type=F32)
                if k == 0:
                    term = term + away_ref[at]
                tally(own_total[0], own_ref, k, at, term)


def mate_products(half, blocks, mates, away=None):
    count, rows, width = blocks.shape
    rows = rows // 2
    n, cols = len(mates), sum(m.shape[1] for m in mates)
    anywhere = pl.BlockSpec(memory_space=pl.ANY)
    out = [jax.ShapeDtypeStruct((count, cols, width), BF16)]
    own_total = []
    if away is not None:
        out.append(jax.ShapeDtypeStruct(away.shape, F32))
        own_total.append(pltpu.VMEM(away.shape, F32))
    results = pl.pallas_call(
        functools.partial(mate_kernel, n, away is not None),
        in_specs=in_smem(1) + [anywhere] * (1 + n) + in_vmem(len(out) - 1),
        out_specs=in_vmem(len(out)),
        out_shape=out,
        scratch_shapes=[
            *(pltpu.VMEM(m.shape, BF16) for m in mates),
            pltpu.VMEM((count, rows, width), BF16),
            pltpu.VMEM((count, cols, width), F32),
            pltpu.SemaphoreType.DMA((CHUNKS, n + 1)),
            *own_total,
        ],
        compiler_params=params(49),
        cost_estimate=cost(2 * count * rows * cols * width, 2 * rows * (count * width + cols)),
        name="mate_products",
    )(half, blocks, *mates, *([] if away is None else [away]))
    return results[0] if away is None else results


def local_kernel(kind_ref, row_ref, col_ref, own_ref, sent_ref, got_ref, out_ref):
    count, _, width = sent_ref.shape

    def rows_of(orbital):
        return pl.ds(pl.multiple_of(orbital * width, width), width)

    def body(slot, carry):
        kind, row, col = kind_ref[slot], row_ref[slot], col_ref[slot]

        @pl.when(kind == 0)
        def _():
            low, high = jnp.minimum(row, col), jnp.maximum(row, col)
            value = own_ref[low * count - low * (low + 1) // 2 + high - low - 1]

            @pl.when(row < col)
            def _():
                out_ref[slot] = value.astype(BF16)

            @pl.when(row > col)
            def _():
                out_ref[slot] = value.T.astype(BF16)

        @pl.when(kind == 1)
        def _():
            direct = got_ref[col, rows_of(row)].astype(F32)
            out_ref[slot] = (direct + sent_ref[row, rows_of(col)].astype(F32).T).astype(BF16)

        @pl.when(kind == 2)
        def _():
            out_ref[slot] = jnp.zeros(out_ref.shape[1:], BF16)

        return carry

    lax.fori_loop(0, out_ref.shape[0], body, 0)


def local_integrals(kind, row, col, own, sent, got):
    slots, width = kind.shape[0], own.shape[-1]
    return pl.pallas_call(
        local_kernel,
        in_specs=in_smem(3) + in_vmem(3),
        out_specs=in_vmem(1)[0],
        out_shape=jax.ShapeDtypeStruct((slots, width, width), BF16),
        compiler_params=params(8),
        cost_estimate=cost(4 * slots * width * width, 8 * MIB),
        name="local_integrals",
    )(kind, row, col, own, sent, got)


def pick(groups, refs, orbital, index, into_ref):
    for group, sources in zip(groups, refs, strict=True):
        at = 0
        for owner, start, size in group:

            @pl.when(orbital == owner)
            def _(at=at, start=start, size=size, sources=sources):
                value = sources[0][index, at : at + size].astype(F32)
                for ref in sources[1:]:
                    value = value + ref[index, at : at + size].astype(F32)
                into_ref[start : start + size] = value

            at += size


def cross_kernel(groups, kind_ref, row_ref, col_ref, inverse_ref, part_ref, other_ref, *refs):
    n = len(groups)
    sent, got = list(zip(refs[:n], refs[n : 2 * n], strict=True)), [(r,) for r in refs[2 * n : 3 * n]]
    base_ref, rounded_ref, direct_ref, turned_ref = refs[3 * n :]

    def body(slot, carry):
        kind, row, col = kind_ref[slot], row_ref[slot], col_ref[slot]

        def store(value):
            value = -value * inverse_ref[slot]
            base_ref[slot] = value
            rounded_ref[slot] = value.astype(BF16)

        @pl.when(kind == 2)
        def _():
            pick(groups, got, row, col, direct_ref)
            pick(groups, sent, col, row, turned_ref)
            store(direct_ref[...] + turned_ref[...].T)

        @pl.when(kind != 2)
        def _():
            store(part_ref[slot].astype(F32) + other_ref[slot].astype(F32))

        return carry

    lax.fori_loop(0, kind_ref.shape[0], body, 0)


def cross_amplitudes(groups, kind, row, col, inverse, local, sent, others, got):
    slots, width, _ = inverse.shape
    return pl.pallas_call(
        functools.partial(cross_kernel, groups),
        in_specs=in_smem(3) + in_vmem(3 + len(sent) + len(others) + len(got)),
        out_specs=in_vmem(2),
        out_shape=[jax.ShapeDtypeStruct((slots, width, width), F32), jax.ShapeDtypeStruct((slots, width, width), BF16)],
        scratch_shapes=[pltpu.VMEM((width, width), F32), pltpu.VMEM((width, width), F32)],
        compiler_params=params(8),
        cost_estimate=cost(4 * slots * width * width, 8 * MIB),
        name="cross_amplitudes",
    )(kind, row, col, inverse, *local, *sent, *others, *got)


def sweep_kernel(at_ref, weight_ref, own_ref, chip_ref, line_ref, rows_ref, cols_ref, base_ref, inverse_ref, out_ref, held_ref):
    slots, neighbours = rows_ref.shape[:2]
    held_ref[:slots] = own_ref[...]
    held_ref[slots : 2 * slots] = chip_ref[...]
    held_ref[2 * slots :] = line_ref[...]
    for slot in range(slots):
        total = None
        for n in range(neighbours):
            source = held_ref[at_ref[slot, n]]
            selected = jnp.dot(rows_ref[slot, n], source, preferred_element_type=F32).astype(BF16)
            term = weight_ref[slot, n] * jnp.dot(selected, cols_ref[slot, n], preferred_element_type=F32)
            total = term if total is None else total + term
        out_ref[slot] = (base_ref[slot] + total * inverse_ref[slot]).astype(out_ref.dtype)


def sweep_amplitudes(at, weights, own, chip, line, row_match, col_match, base, inverse):
    slots, width, _ = own.shape
    neighbours = at.shape[1]
    return pl.pallas_call(
        sweep_kernel,
        in_specs=in_smem(2) + in_vmem(7),
        out_specs=in_vmem(1)[0],
        out_shape=jax.ShapeDtypeStruct((slots, width, width), BF16),
        scratch_shapes=[pltpu.VMEM((3 * slots, width, width), BF16)],
        compiler_params=params(8),
        cost_estimate=cost(4 * slots * neighbours * width**3, 16 * MIB),
        name="sweep_amplitudes",
    )(at, weights, own, chip, line, row_match, col_match, base, inverse)


def on_device(three_index, pair_orbs, live_pairs, domains, coupled, fock_coupling_weight, occ_energy, virt_energy):
    count, naux, width = three_index.shape
    slots = coupled.shape[0]
    half_rows = naux // 2
    owner = lax.axis_index(LINE)
    parity = lax.axis_index("occ")
    chip_owner = owner + 1 - 2 * parity

    cut = width // 2
    head, tail = (count - 1, 0, cut), (count - 1, cut, width - cut)
    groups = [[head, (0, 0, width)], *[[(j, 0, width)] for j in range(1, count - 1)], [tail]]
    half = jnp.reshape(parity, (1,)).astype(jnp.int32)
    first = lax.dynamic_slice(three_index, (count - 1, (1 - parity) * half_rows, 0), (1, half_rows, cut))[0]
    *sends, last, own_away = send_blocks(1 - half, after(three_index, first), width - cut)
    from_line = [[line_mate(first), line_mate(sends[0])], *[[line_mate(s)] for s in sends[1:-1]], [line_mate(last)]]
    from_chip = [chip_mate(s) for s in sends]

    def total(terms, *earlier):
        a, b = lax.optimization_barrier((*terms, *earlier))[:2]
        return (a.astype(F32) + b.astype(F32)).astype(BF16)

    def cross_products(k, *earlier):
        mates = lax.optimization_barrier((*from_line[k], *earlier))[: len(from_line[k])]
        return mate_products(half, three_index, mates)

    domains, pair_orbs, coupled = lax.optimization_barrier((domains, pair_orbs, coupled, own_away, from_line[0][0]))[:3]

    local = jnp.arange(slots, dtype=jnp.int32)
    pairs = lax.dynamic_slice_in_dim(pair_orbs, owner * slots, slots, 0)
    live = (local < live_pairs[owner]).astype(F32)[:, None, None]
    rows, cols = pairs[:, 0], pairs[:, 1]
    row_dom, col_dom = domains[rows], domains[cols]

    def kind_of(other):
        return jnp.where(other == owner, 0, jnp.where(other == chip_owner, 1, 2)).astype(jnp.int32)

    def energy(dom):
        listed = jnp.arange(virt_energy.shape[0], dtype=jnp.int32)
        return jnp.sum(jnp.where(dom[..., None] == listed, virt_energy, 0.0), axis=-1)

    gaps = (
        energy(row_dom)[:, :, None]
        + energy(col_dom)[:, None, :]
        - occ_energy[rows][:, None, None]
        - occ_energy[cols][:, None, None]
    )
    inverse = live / gaps
    source_rows = domains[pair_orbs[coupled, 0]]
    source_cols = domains[pair_orbs[coupled, 1]]
    kind, row, col = kind_of(cols // count), rows % count, cols % count
    at = kind_of(coupled // slots) * slots + coupled % slots

    chip_sent, own = mate_products(half, after(three_index, inverse, source_rows, source_cols), from_chip, own_away)
    sent = [cross_products(0, chip_sent)]
    terms = [aux_terms(sent[0])]
    local = local_integrals(kind, row, col, own, chip_sent, after(chip_mate(chip_sent), sent[0]))
    local_terms = aux_terms(local)
    sums = []
    earlier = (local,)
    for k in range(1, len(groups)):
        sent.append(cross_products(k, *earlier))
        terms.append(aux_terms(sent[k]))
        sums.append(total(terms[k - 1], sent[k]))
        earlier = (sums[-1],)
    sums.append(total(terms[-1]))
    got = [line_mate(v) for v in sums]
    base, rounded = cross_amplitudes(
        groups, kind, row, col, inverse, local_terms, [a for a, _ in terms], [b for _, b in terms], got
    )
    row_dom, col_dom, source_rows, source_cols = lax.optimization_barrier(
        (row_dom, col_dom, source_rows, source_cols, rounded)
    )[:4]
    row_match = (row_dom[:, None, :, None] == source_rows[:, :, None, :]).astype(BF16)
    col_match = (source_cols[:, :, :, None] == col_dom[:, None, None, :]).astype(BF16)
    for sweep in range(ITERS):
        rounded = sweep_amplitudes(
            at, fock_coupling_weight, rounded, chip_mate(rounded), line_mate(rounded),
            row_match, col_match, base, inverse,
        )
    return rounded


def solution(mesh):
    return jax.shard_map(
        on_device,
        mesh=mesh,
        in_specs=(
            P(("groups", "pair", "occ"), "aux", None),
            P("groups", None),
            P("groups"),
            P("groups", None),
            P(("groups", "pair", "occ"), None),
            P(("groups", "pair", "occ"), None),
            P("groups"),
            P("groups"),
        ),
        out_specs=P(("groups", "pair", "occ"), None, None),
        check_vma=False,
    )
```

time: 224 us -> 166 us (0.74)
  waiting for transfers between devices: 96.5 us -> 61.3 us
  local copies, waits for them, and re-layouts: 36.1 us -> 11.5 us
  Pallas kernels: 41 us -> 45.5 us
  starting transfers between devices: 41.4 us -> 38.9 us
    ppermute x5 -> x4, waiting for transfers between devices: 24.7 us -> 6.42 us  [aux_terms(): other = lax.ppermute(value, 'aux', [(i, i ^ step) for i in range(count)])]
    ppermute x10 -> x9, waiting for transfers between devices: 71.7 us -> 54.9 us  [line_mate(): return lax.ppermute(value, LINE, pairs)]
    reshape x2 -> x0, local copies, waits for them, and re-layouts: 9.92 us -> none  [on_device(): lax.dynamic_slice(three_index, (j, away, start), (1, half_rows, size))]
    unnamed x45 -> x29, local copies, waits for them, and re-layouts: 12.1 us -> 2.61 us
    dynamic_slice x1 -> x0, local copies, waits for them, and re-layouts: 7.68 us -> none  [on_device(): lax.dynamic_slice(three_index, (0, parity * half_rows, 0), (count, half_r...]
    pallas_call x11 -> x7, Pallas kernels: 32.1 us -> 36.8 us  [the longest x4 27.9 us: mate_products(): pl.pallas_call(functools.partial(mate_kernel, n, away is not None), in_sp...]
    squeeze x0 -> x1, local copies, waits for them, and re-layouts: none -> 2.46 us  [on_device(): lax.dynamic_slice(three_index, (count - 1, (1 - parity) * half_rows, 0),...]
    ppermute x10 -> x9, starting transfers between devices: 34.8 us -> 33.9 us  [line_mate(): return lax.ppermute(value, LINE, pairs)]
  transfers between devices with their start and end apart: 25 -> 19, of which waited for: 7 -> 7; matrix products, arithmetic and copies ran while one was open for 10% -> 9% of each run, Pallas kernels for 11% -> 21%
where the time goes in v3:
time: 166 us
  waiting for transfers between devices  61.3 us (37%)
  Pallas kernels  45.5 us (27%)
  starting transfers between devices  38.9 us (23%)
  local copies, waits for them, and re-layouts  11.5 us (7%)
  other arithmetic  8.08 us (5%)
    ppermute x9, waiting for transfers between devices, line_mate(): return lax.ppermute(value, LINE, pairs)  54.9 us
    ppermute x9, starting transfers between devices, line_mate(): return lax.ppermute(value, LINE, pairs)  33.9 us
    pallas_call x4, Pallas kernels, mate_products(): pl.pallas_call(functools.partial(mate_kernel, n, away is not None), in_sp...  27.9 us
    pallas_call x2, Pallas kernels, sweep_amplitudes(): pl.pallas_call(sweep_kernel, in_specs=in_smem(2) + in_vmem(7), out_specs=...  8.77 us
    ppermute x4, waiting for transfers between devices, aux_terms(): other = lax.ppermute(value, 'aux', [(i, i ^ step) for i in range(count)])  6.42 us
    pallas_call x1, Pallas kernels, send_blocks(): pl.pallas_call(send_kernel, in_specs=in_smem(1) + [anywhere], out_specs=[...  5.86 us
    reduce_sum x1, other arithmetic, energy(): jnp.sum(jnp.where(dom[..., None] == listed, virt_energy, 0.0), axis=-1)  4.3 us
    ppermute x4, starting transfers between devices, aux_terms(): other = lax.ppermute(value, 'aux', [(i, i ^ step) for i in range(count)])  4.15 us
  transfers between devices with their start and end apart: 19, of which 7 were waited for; matrix products, arithmetic and copies ran while one was open for 9% of the time, Pallas kernels for 21%

profile of v3, /device:TPU:1, one launch (start us, length us, event | category | flops | bytes accessed | tf_op | source)
XLA Modules:
  0.0 165.8 jit_solution(9601334434881586926)
XLA Ops:
  0.0 2.5 %dynamic-slice_bitcast_fusion = bf16[5120,128]{1,0:T(8,128)(2,1)} fusion(bf16[3,10240,256]{2,1,0:T(8,128)(2,1)} %blocks_ref.7, s32[]{:T(128)S(6)} %select_n.93), kind=kLoop, calls=%fused_computation.15 | loop fusion | bytes 2621444 | tf_op jit(solution)/shard_map/squeeze | solution.py:354
  2.5 4.6 %collective-permute-start = (bf16[5120,128]{1,0:T(8,128)(2,1)}, bf16[5120,128]{1,0:T(8,128)(2,1)S(1)}, u32[]{:S(2)}, u32[]{:S(2)}) collective-permute-start(bf16[5120,128]{1,0:T(8,128)(2,1)} %dynamic-slice_bitcast_fusion), channel_id=1, source_target_pairs={{1,4},{4,1},{5,8},{8,5},{9,12},{12,9},{3,6},{6,3},{7,10},{10,7},{1... | collective-permute-start | bytes 3932168 | tf_op jit(solution)/shard_map/ppermute | solution.py:27
  7.1 5.9 %send_blocks.1 = (bf16[5120,256]{1,0:T(8,128)(2,1)}, bf16[5120,256]{1,0:T(8,128)(2,1)}, bf16[5120,256]{1,0:T(8,128)(2,1)}, bf16[5120,128]{1,0:T(8,128)(2,1)S(1)}, f32[3,256,256]{2,1,0:T(8,128)S(1)}) custom-call(s32[1]{0:T(128)S(6)} %sub.35.half_ref, bf16[3,10240,256]{2,1,0:T(8,128)(2,1)} %blocks_ref.7), custom_call_target="tpu_custom_call" | custom-call | flops 1966080 | bytes 15360 | tf_op jit(solution)/shard_map/send_blocks/pallas_call | solution.py:121
  13.7 3.5 %collective-permute-start.5 = (bf16[5120,256]{1,0:T(8,128)(2,1)}, bf16[5120,256]{1,0:T(8,128)(2,1)}, u32[]{:S(2)}, u32[]{:S(2)}) collective-permute-start(bf16[5120,256]{1,0:T(8,128)(2,1)} %get-tuple-element.40), channel_id=1, source_target_pairs={{1,4},{4,1},{5,8},{8,5},{9,12},{12,9},{3,6},{6,3},{7,10},{10,7},{1... | collective-permute-start | bytes 7864328 | tf_op jit(solution)/shard_map/ppermute | solution.py:27
  18.5 4.0 %collective-permute-done.refs_0_ = bf16[5120,128]{1,0:T(8,128)(2,1)S(1)} collective-permute-done((bf16[5120,128]{1,0:T(8,128)(2,1)}, bf16[5120,128]{1,0:T(8,128)(2,1)S(1)}, u32[]{:S(2)}, u32[]{:S(2)}) %collective-permute-start) | collective-permute-done | bytes 1310752 | tf_op jit(solution)/shard_map/ppermute | solution.py:27
  22.5 3.8 %collective-permute-start.7 = (bf16[5120,256]{1,0:T(8,128)(2,1)}, bf16[5120,256]{1,0:T(8,128)(2,1)}, u32[]{:S(2)}, u32[]{:S(2)}) collective-permute-start(bf16[5120,256]{1,0:T(8,128)(2,1)} %get-tuple-element.41), channel_id=1, source_target_pairs={{1,4},{4,1},{5,8},{8,5},{9,12},{12,9},{3,6},{6,3},{7,10},{10,7},{1... | collective-permute-start | bytes 7864328 | tf_op jit(solution)/shard_map/ppermute | solution.py:27
  32.3 4.3 %select_reduce_fusion.1 = (f32[8,256]{1,0:T(8,128)S(1)}, f32[8,256]{1,0:T(8,128)S(1)}) fusion(f32[1792]{0:T(1024)S(1)} %copy-done.12, s32[8,256]{1,0:T(8,128)S(1)} %gather_fusion, s32[8,256]{1,0:T(8,128)S(1)} %gather_fusion.1), kind=kLoop, calls=%fused_computation.10 | loop fusion | flops 22016000 | bytes 39936 | tf_op jit(solution)/shard_map/reduce_sum | solution.py:380
  38.3 11.9 %mate_products.4 = (bf16[3,768,256]{2,1,0:T(8,128)(2,1)S(1)}, f32[3,256,256]{2,1,0:T(8,128)S(1)}) custom-call(s32[1]{0:T(128)} %bitcast.half_ref, bf16[3,10240,256]{2,1,0:T(8,128)(2,1)} %blocks_ref.7, bf16[5120,256]{1,0:T(8,128)(2,1)} %collective-permute-done.1.refs_0_, bf16[5120,256]{1,0:T(8,128)(2,1)} %collective-permute-done.2.refs_1_, ...), custom_call_target="tpu_custom_call" | custom-call | flops 5898240 | bytes 15360 | tf_op jit(solution)/shard_map/mate_products/pallas_call | solution.py:187
  50.2 3.8 %collective-permute-start.8 = (bf16[5120,128]{1,0:T(8,128)(2,1)S(1)}, bf16[5120,128]{1,0:T(8,128)(2,1)S(1)}, u32[]{:S(2)}, u32[]{:S(2)}) collective-permute-start(bf16[5120,128]{1,0:T(8,128)(2,1)S(1)} %copy-done.7), channel_id=1, source_target_pairs={{1,4},{4,1},{5,8},{8,5},{9,12},{12,9},{3,6},{6,3},{7,10},{10,7},{1... | collective-permute-start | bytes 3932168 | tf_op jit(solution)/shard_map/ppermute | solution.py:27
  54.1 6.2 %mate_products.5.refs_0_ = bf16[3,384,256]{2,1,0:T(8,128)(2,1)S(1)} custom-call(s32[1]{0:T(128)} %bitcast.half_ref, bf16[3,10240,256]{2,1,0:T(8,128)(2,1)} %blocks_ref.7, bf16[5120,128]{1,0:T(8,128)(2,1)S(1)} %collective-permute-done.refs_0_, bf16[5120,256]{1,0:T(8,128)(2,1)} %collective-permute-done.5.refs_1_), custom_call_target="tpu_custom_call" | custom-call | flops 2949120 | bytes 11520 | tf_op jit(solution)/shard_map/mate_products/pallas_call | solution.py:187
  63.1 15.9 %collective-permute-done.7.refs_0_ = bf16[5120,256]{1,0:T(8,128)(2,1)} collective-permute-done((bf16[5120,256]{1,0:T(8,128)(2,1)}, bf16[5120,256]{1,0:T(8,128)(2,1)}, u32[]{:S(2)}, u32[]{:S(2)}) %collective-permute-start.7) | collective-permute-done | bytes 2621472 | tf_op jit(solution)/shard_map/ppermute | solution.py:27
  79.0 5.6 %mate_products.6.refs_1_ = bf16[3,256,256]{2,1,0:T(8,128)(2,1)S(1)} custom-call(s32[1]{0:T(128)} %bitcast.half_ref, bf16[3,10240,256]{2,1,0:T(8,128)(2,1)} %blocks_ref.7, bf16[5120,256]{1,0:T(8,128)(2,1)} %collective-permute-done.7.refs_0_), custom_call_target="tpu_custom_call" | custom-call | flops 1966080 | bytes 10240 | tf_op jit(solution)/shard_map/mate_products/pallas_call | solution.py:187
  86.0 7.0 %collective-permute-done.8.refs_0_ = bf16[5120,128]{1,0:T(8,128)(2,1)S(1)} collective-permute-done((bf16[5120,128]{1,0:T(8,128)(2,1)S(1)}, bf16[5120,128]{1,0:T(8,128)(2,1)S(1)}, u32[]{:S(2)}, u32[]{:S(2)}) %collective-permute-start.8) | collective-permute-done | bytes 1310752 | tf_op jit(solution)/shard_map/ppermute | solution.py:27
  93.1 4.3 %mate_products.7.refs_2_ = bf16[3,128,256]{2,1,0:T(8,128)(2,1)S(1)} custom-call(s32[1]{0:T(128)} %bitcast.half_ref, bf16[3,10240,256]{2,1,0:T(8,128)(2,1)} %blocks_ref.7, bf16[5120,128]{1,0:T(8,128)(2,1)S(1)} %collective-permute-done.8.refs_0_), custom_call_target="tpu_custom_call" | custom-call | flops 983040 | bytes 8960 | tf_op jit(solution)/shard_map/mate_products/pallas_call | solution.py:187
  98.6 3.6 %collective-permute-start.12 = (bf16[3,384,256]{2,1,0:T(8,128)(2,1)S(1)}, bf16[3,384,256]{2,1,0:T(8,128)(2,1)S(1)}, u32[]{:S(2)}, u32[]{:S(2)}) collective-permute-start(bf16[3,384,256]{2,1,0:T(8,128)(2,1)S(1)} %add_convert_fusion), channel_id=1, source_target_pairs={{1,4},{4,1},{5,8},{8,5},{9,12},{12,9},{3,6},{6,3},{7,10},{10,7},{1... | collective-permute-start | bytes 1769480 | tf_op jit(solution)/shard_map/ppermute | solution.py:27
  102.2 6.4 %collective-permute-done.11.refs_5_ = bf16[3,128,256]{2,1,0:T(8,128)(2,1)S(1)} collective-permute-done((bf16[3,128,256]{2,1,0:T(8,128)(2,1)S(1)}, bf16[3,128,256]{2,1,0:T(8,128)(2,1)S(1)}, u32[]{:S(2)}, u32[]{:S(2)}) %collective-permute-start.11) | collective-permute-done | bytes 196640 | tf_op jit(solution)/shard_map/ppermute | solution.py:34
  108.7 4.4 %collective-permute-start.13 = (bf16[3,256,256]{2,1,0:T(8,128)(2,1)S(1)}, bf16[3,256,256]{2,1,0:T(8,128)(2,1)S(1)}, u32[]{:S(2)}, u32[]{:S(2)}) collective-permute-start(bf16[3,256,256]{2,1,0:T(8,128)(2,1)S(1)} %add_convert_fusion.1), channel_id=1, source_target_pairs={{1,4},{4,1},{5,8},{8,5},{9,12},{12,9},{3,6},{6,3},{7,10},{10,7},{1... | collective-permute-start | bytes 1179656 | tf_op jit(solution)/shard_map/ppermute | solution.py:27
  115.2 5.6 %collective-permute-done.14.refs_8_ = bf16[3,128,256]{2,1,0:T(8,128)(2,1)S(1)} collective-permute-done((bf16[3,128,256]{2,1,0:T(8,128)(2,1)S(1)}, bf16[3,128,256]{2,1,0:T(8,128)(2,1)S(1)}, u32[]{:S(2)}, u32[]{:S(2)}) %collective-permute-start.14) | collective-permute-done | bytes 196640 | tf_op jit(solution)/shard_map/ppermute | solution.py:27
  123.9 4.5 %collective-permute-start.16 = (bf16[8,256,256]{2,1,0:T(8,128)(2,1)S(1)}, bf16[8,256,256]{2,1,0:T(8,128)(2,1)}, u32[]{:S(2)}, u32[]{:S(2)}) collective-permute-start(bf16[8,256,256]{2,1,0:T(8,128)(2,1)S(1)} %get-tuple-element.57.own_ref), channel_id=1, source_target_pairs={{1,4},{4,1},{5,8},{8,5},{9,12},{12,9},{3,6},{6,3},{7,10},{10,7},{1... | collective-permute-start | bytes 3145736 | tf_op jit(solution)/shard_map/ppermute | solution.py:27
  130.8 9.9 %collective-permute-done.16.line_ref = bf16[8,256,256]{2,1,0:T(8,128)(2,1)} collective-permute-done((bf16[8,256,256]{2,1,0:T(8,128)(2,1)S(1)}, bf16[8,256,256]{2,1,0:T(8,128)(2,1)}, u32[]{:S(2)}, u32[]{:S(2)}) %collective-permute-start.16) | collective-permute-done | bytes 1048608 | tf_op jit(solution)/shard_map/ppermute | solution.py:27
  140.8 4.3 %sweep_amplitudes.2.own_ref = bf16[8,256,256]{2,1,0:T(8,128)(2,1)S(1)} custom-call(s32[8,4]{1,0:T(8,128)S(1)} %get-tuple-element.67.at_ref, f32[8,4]{1,0:T(8,128)S(1)} %copy.32.weight_ref, bf16[8,256,256]{2,1,0:T(8,128)(2,1)S(1)} %get-tuple-element.57.own_ref, bf16[8,256,256]{2,1,0:T(8,128)(2,1)} %collective-permute-done.15.chip_ref, ...), custom_call_target="tpu_custom_call" | custom-call | flops 2097152 | bytes 16384 | tf_op jit(solution)/shard_map/sweep_amplitudes/pallas_call | solution.py:330
  145.2 3.7 %collective-permute-start.18 = (bf16[8,256,256]{2,1,0:T(8,128)(2,1)S(1)}, bf16[8,256,256]{2,1,0:T(8,128)(2,1)S(1)}, u32[]{:S(2)}, u32[]{:S(2)}) collective-permute-start(bf16[8,256,256]{2,1,0:T(8,128)(2,1)S(1)} %sweep_amplitudes.2.own_ref), channel_id=1, source_target_pairs={{1,4},{4,1},{5,8},{8,5},{9,12},{12,9},{3,6},{6,3},{7,10},{10,7},{1... | collective-permute-start | bytes 3145736 | tf_op jit(solution)/shard_map/ppermute | solution.py:27
  148.9 12.5 %collective-permute-done.18.line_ref = bf16[8,256,256]{2,1,0:T(8,128)(2,1)S(1)} collective-permute-done((bf16[8,256,256]{2,1,0:T(8,128)(2,1)S(1)}, bf16[8,256,256]{2,1,0:T(8,128)(2,1)S(1)}, u32[]{:S(2)}, u32[]{:S(2)}) %collective-permute-start.18) | collective-permute-done | bytes 1048608 | tf_op jit(solution)/shard_map/ppermute | solution.py:27
  161.4 4.4 %sweep_amplitudes.3 = bf16[8,256,256]{2,1,0:T(8,128)(2,1)} custom-call(s32[8,4]{1,0:T(8,128)S(1)} %get-tuple-element.67.at_ref, f32[8,4]{1,0:T(8,128)S(1)} %copy.32.weight_ref, bf16[8,256,256]{2,1,0:T(8,128)(2,1)S(1)} %sweep_amplitudes.2.own_ref, bf16[8,256,256]{2,1,0:T(8,128)(2,1)S(1)} %collective-permute-done.17.chip_ref, ...), custom_call_target="tpu_custom_call" | custom-call | flops 2097152 | bytes 16384 | tf_op jit(solution)/shard_map/sweep_amplitudes/pallas_call | solution.py:330
  (88 shorter events, 22.7 us)
Async XLA Ops:
  0.0 26.5 %copy-start = (s32[24,256]{1,0:T(8,128)S(1)}, s32[24,256]{1,0:T(8,128)}, u32[]{:S(2)}) copy-start(s32[24,256]{1,0:T(8,128)} %param.11) | copy-start | bytes 73732
  2.5 20.1 %collective-permute-start = (bf16[5120,128]{1,0:T(8,128)(2,1)}, bf16[5120,128]{1,0:T(8,128)(2,1)S(1)}, u32[]{:S(2)}, u32[]{:S(2)}) collective-permute-start(bf16[5120,128]{1,0:T(8,128)(2,1)} %dynamic-slice_bitcast_fusion), channel_id=1, source_target_pairs={{1,4},{4,1},{5,8},{8,5},{9,12},{12,9},{3,6},{6,3},{7,10},{10,7},{1... | collective-permute-start | bytes 3932168 | tf_op jit(solution)/shard_map/ppermute | solution.py:27
  7.1 19.3 %copy-start.8 = (s32[64,2]{0,1:T(2,128)S(1)}, s32[64,2]{0,1:T(2,128)}, u32[]{:S(2)}) copy-start(s32[64,2]{0,1:T(2,128)} %param.9) | copy-start | bytes 1540
  7.1 20.5 %copy-start.9 = (f32[24]{0:T(128)S(1)}, f32[24]{0:T(128)}, u32[]{:S(2)}) copy-start(f32[24]{0:T(128)} %param.14) | copy-start | bytes 292
  7.1 21.8 %copy-start.10 = (s32[8,4]{0,1:T(4,128)S(1)}, s32[8,4]{0,1:T(4,128)}, u32[]{:S(2)}) copy-start(s32[8,4]{0,1:T(4,128)} %param.12) | copy-start | bytes 388
  13.0 16.9 %copy-start.4 = (f32[3,256,256]{2,1,0:T(8,128)}, f32[3,256,256]{2,1,0:T(8,128)S(1)}, u32[]{:S(2)}) copy-start(f32[3,256,256]{2,1,0:T(8,128)S(1)} %get-tuple-element.35.refs_3_) | copy-start | bytes 2359300
  13.0 24.1 %collective-permute-start.1 = (bf16[5120,256]{1,0:T(8,128)(2,1)}, bf16[5120,256]{1,0:T(8,128)(2,1)}, u32[]{:S(2)}, u32[]{:S(2)}) collective-permute-start(bf16[5120,256]{1,0:T(8,128)(2,1)} %get-tuple-element.40), channel_id=1, source_target_pairs={{0,1},{1,0},{2,3},{3,2},{4,5},{5,4},{6,7},{7,6},{8,9},{9,8},{10,11... | collective-permute-start | bytes 7864328 | tf_op jit(solution)/shard_map/ppermute | solution.py:19
  13.1 24.1 %collective-permute-start.2 = (bf16[5120,256]{1,0:T(8,128)(2,1)}, bf16[5120,256]{1,0:T(8,128)(2,1)}, u32[]{:S(2)}, u32[]{:S(2)}) collective-permute-start(bf16[5120,256]{1,0:T(8,128)(2,1)} %get-tuple-element.41), channel_id=1, source_target_pairs={{0,1},{1,0},{2,3},{3,2},{4,5},{5,4},{6,7},{7,6},{8,9},{9,8},{10,11... | collective-permute-start | bytes 7864328 | tf_op jit(solution)/shard_map/ppermute | solution.py:19
  13.6 23.6 %collective-permute-start.3 = (bf16[5120,256]{1,0:T(8,128)(2,1)}, bf16[5120,256]{1,0:T(8,128)(2,1)}, u32[]{:S(2)}, u32[]{:S(2)}) collective-permute-start(bf16[5120,256]{1,0:T(8,128)(2,1)} %get-tuple-element.42), channel_id=1, source_target_pairs={{0,1},{1,0},{2,3},{3,2},{4,5},{5,4},{6,7},{7,6},{8,9},{9,8},{10,11... | collective-permute-start | bytes 7864328 | tf_op jit(solution)/shard_map/ppermute | solution.py:19
  13.7 40.4 %collective-permute-start.5 = (bf16[5120,256]{1,0:T(8,128)(2,1)}, bf16[5120,256]{1,0:T(8,128)(2,1)}, u32[]{:S(2)}, u32[]{:S(2)}) collective-permute-start(bf16[5120,256]{1,0:T(8,128)(2,1)} %get-tuple-element.40), channel_id=1, source_target_pairs={{1,4},{4,1},{5,8},{8,5},{9,12},{12,9},{3,6},{6,3},{7,10},{10,7},{1... | collective-permute-start | bytes 7864328 | tf_op jit(solution)/shard_map/ppermute | solution.py:27
  22.5 56.5 %collective-permute-start.7 = (bf16[5120,256]{1,0:T(8,128)(2,1)}, bf16[5120,256]{1,0:T(8,128)(2,1)}, u32[]{:S(2)}, u32[]{:S(2)}) collective-permute-start(bf16[5120,256]{1,0:T(8,128)(2,1)} %get-tuple-element.41), channel_id=1, source_target_pairs={{1,4},{4,1},{5,8},{8,5},{9,12},{12,9},{3,6},{6,3},{7,10},{10,7},{1... | collective-permute-start | bytes 7864328 | tf_op jit(solution)/shard_map/ppermute | solution.py:27
  50.2 11.4 %collective-permute-start.4 = (bf16[3,768,256]{2,1,0:T(8,128)(2,1)S(1)}, bf16[3,768,256]{2,1,0:T(8,128)(2,1)S(1)}, u32[]{:S(2)}, u32[]{:S(2)}) collective-permute-start(bf16[3,768,256]{2,1,0:T(8,128)(2,1)S(1)} %get-tuple-element.44.sent_ref), channel_id=1, source_target_pairs={{0,1},{1,0},{2,3},{3,2},{4,5},{5,4},{6,7},{7,6},{8,9},{9,8},{10,11... | collective-permute-start | bytes 3538952 | tf_op jit(solution)/shard_map/ppermute | solution.py:19
  50.2 42.8 %collective-permute-start.8 = (bf16[5120,128]{1,0:T(8,128)(2,1)S(1)}, bf16[5120,128]{1,0:T(8,128)(2,1)S(1)}, u32[]{:S(2)}, u32[]{:S(2)}) collective-permute-start(bf16[5120,128]{1,0:T(8,128)(2,1)S(1)} %copy-done.7), channel_id=1, source_target_pairs={{1,4},{4,1},{5,8},{8,5},{9,12},{12,9},{3,6},{6,3},{7,10},{10,7},{1... | collective-permute-start | bytes 3932168 | tf_op jit(solution)/shard_map/ppermute | solution.py:27
  60.3 25.6 %collective-permute-start.9 = (bf16[3,384,256]{2,1,0:T(8,128)(2,1)S(1)}, bf16[3,384,256]{2,1,0:T(8,128)(2,1)S(1)}, u32[]{:S(2)}, u32[]{:S(2)}) collective-permute-start(bf16[3,384,256]{2,1,0:T(8,128)(2,1)S(1)} %mate_products.5.refs_0_), channel_id=1, source_target_pairs={{0,2},{2,0},{1,3},{3,1},{4,6},{6,4},{5,7},{7,5},{8,10},{10,8},{9,1... | collective-permute-start | bytes 1769480 | tf_op jit(solution)/shard_map/ppermute | solution.py:34
  62.8 58.0 %collective-permute-start.6 = (bf16[8,256,256]{2,1,0:T(8,128)(2,1)S(1)}, bf16[8,256,256]{2,1,0:T(8,128)(2,1)S(1)}, u32[]{:S(2)}, u32[]{:S(2)}) collective-permute-start(bf16[8,256,256]{2,1,0:T(8,128)(2,1)S(1)} %local_integrals.1.part_ref), channel_id=1, source_target_pairs={{0,2},{2,0},{1,3},{3,1},{4,6},{6,4},{5,7},{7,5},{8,10},{10,8},{9,1... | collective-permute-start | bytes 3145736 | tf_op jit(solution)/shard_map/ppermute | solution.py:34
  84.6 24.0 %collective-permute-start.10 = (bf16[3,256,256]{2,1,0:T(8,128)(2,1)S(1)}, bf16[3,256,256]{2,1,0:T(8,128)(2,1)S(1)}, u32[]{:S(2)}, u32[]{:S(2)}) collective-permute-start(bf16[3,256,256]{2,1,0:T(8,128)(2,1)S(1)} %mate_products.6.refs_1_), channel_id=1, source_target_pairs={{0,2},{2,0},{1,3},{3,1},{4,6},{6,4},{5,7},{7,5},{8,10},{10,8},{9,1... | collective-permute-start | bytes 1179656 | tf_op jit(solution)/shard_map/ppermute | solution.py:34
  97.3 11.3 %collective-permute-start.11 = (bf16[3,128,256]{2,1,0:T(8,128)(2,1)S(1)}, bf16[3,128,256]{2,1,0:T(8,128)(2,1)S(1)}, u32[]{:S(2)}, u32[]{:S(2)}) collective-permute-start(bf16[3,128,256]{2,1,0:T(8,128)(2,1)S(1)} %mate_products.7.refs_2_), channel_id=1, source_target_pairs={{0,2},{2,0},{1,3},{3,1},{4,6},{6,4},{5,7},{7,5},{8,10},{10,8},{9,1... | collective-permute-start | bytes 589832 | tf_op jit(solution)/shard_map/ppermute | solution.py:34
  98.6 22.2 %collective-permute-start.12 = (bf16[3,384,256]{2,1,0:T(8,128)(2,1)S(1)}, bf16[3,384,256]{2,1,0:T(8,128)(2,1)S(1)}, u32[]{:S(2)}, u32[]{:S(2)}) collective-permute-start(bf16[3,384,256]{2,1,0:T(8,128)(2,1)S(1)} %add_convert_fusion), channel_id=1, source_target_pairs={{1,4},{4,1},{5,8},{8,5},{9,12},{12,9},{3,6},{6,3},{7,10},{10,7},{1... | collective-permute-start | bytes 1769480 | tf_op jit(solution)/shard_map/ppermute | solution.py:27
  108.7 12.0 %collective-permute-start.13 = (bf16[3,256,256]{2,1,0:T(8,128)(2,1)S(1)}, bf16[3,256,256]{2,1,0:T(8,128)(2,1)S(1)}, u32[]{:S(2)}, u32[]{:S(2)}) collective-permute-start(bf16[3,256,256]{2,1,0:T(8,128)(2,1)S(1)} %add_convert_fusion.1), channel_id=1, source_target_pairs={{1,4},{4,1},{5,8},{8,5},{9,12},{12,9},{3,6},{6,3},{7,10},{10,7},{1... | collective-permute-start | bytes 1179656 | tf_op jit(solution)/shard_map/ppermute | solution.py:27
  113.3 7.5 %collective-permute-start.14 = (bf16[3,128,256]{2,1,0:T(8,128)(2,1)S(1)}, bf16[3,128,256]{2,1,0:T(8,128)(2,1)S(1)}, u32[]{:S(2)}, u32[]{:S(2)}) collective-permute-start(bf16[3,128,256]{2,1,0:T(8,128)(2,1)S(1)} %add_convert_fusion.2), channel_id=1, source_target_pairs={{1,4},{4,1},{5,8},{8,5},{9,12},{12,9},{3,6},{6,3},{7,10},{10,7},{1... | collective-permute-start | bytes 589832 | tf_op jit(solution)/shard_map/ppermute | solution.py:27
  123.9 6.9 %collective-permute-start.15 = (bf16[8,256,256]{2,1,0:T(8,128)(2,1)S(1)}, bf16[8,256,256]{2,1,0:T(8,128)(2,1)}, u32[]{:S(2)}, u32[]{:S(2)}) collective-permute-start(bf16[8,256,256]{2,1,0:T(8,128)(2,1)S(1)} %get-tuple-element.57.own_ref), channel_id=1, source_target_pairs={{0,1},{1,0},{2,3},{3,2},{4,5},{5,4},{6,7},{7,6},{8,9},{9,8},{10,11... | collective-permute-start | bytes 3145736 | tf_op jit(solution)/shard_map/ppermute | solution.py:19
  123.9 16.8 %collective-permute-start.16 = (bf16[8,256,256]{2,1,0:T(8,128)(2,1)S(1)}, bf16[8,256,256]{2,1,0:T(8,128)(2,1)}, u32[]{:S(2)}, u32[]{:S(2)}) collective-permute-start(bf16[8,256,256]{2,1,0:T(8,128)(2,1)S(1)} %get-tuple-element.57.own_ref), channel_id=1, source_target_pairs={{1,4},{4,1},{5,8},{8,5},{9,12},{12,9},{3,6},{6,3},{7,10},{10,7},{1... | collective-permute-start | bytes 3145736 | tf_op jit(solution)/shard_map/ppermute | solution.py:27
  145.1 3.8 %collective-permute-start.17 = (bf16[8,256,256]{2,1,0:T(8,128)(2,1)S(1)}, bf16[8,256,256]{2,1,0:T(8,128)(2,1)S(1)}, u32[]{:S(2)}, u32[]{:S(2)}) collective-permute-start(bf16[8,256,256]{2,1,0:T(8,128)(2,1)S(1)} %sweep_amplitudes.2.own_ref), channel_id=1, source_target_pairs={{0,1},{1,0},{2,3},{3,2},{4,5},{5,4},{6,7},{7,6},{8,9},{9,8},{10,11... | collective-permute-start | bytes 3145736 | tf_op jit(solution)/shard_map/ppermute | solution.py:19
  145.2 16.2 %collective-permute-start.18 = (bf16[8,256,256]{2,1,0:T(8,128)(2,1)S(1)}, bf16[8,256,256]{2,1,0:T(8,128)(2,1)S(1)}, u32[]{:S(2)}, u32[]{:S(2)}) collective-permute-start(bf16[8,256,256]{2,1,0:T(8,128)(2,1)S(1)} %sweep_amplitudes.2.own_ref), channel_id=1, source_target_pairs={{1,4},{4,1},{5,8},{8,5},{9,12},{12,9},{3,6},{6,3},{7,10},{10,7},{1... | collective-permute-start | bytes 3145736 | tf_op jit(solution)/shard_map/ppermute | solution.py:27
  (9 other events, 76.0 us)

commit v4 on v3

--- a/solution.py
+++ b/solution.py
@@ -136,14 +136,10 @@
     )(half, blocks)
 
 
-def mate_kernel(n, with_own, half_ref, blocks_ref, *refs):
-    mates, refs = refs[:n], refs[n:]
-    if with_own:
-        (away_ref, out_ref, own_ref), refs = refs[:3], refs[3:]
-    else:
-        out_ref, refs = refs[0], refs[1:]
-    held, (block_ref, total_ref, arrived, *own_total) = refs[:n], refs[n:]
-    count, rows, _ = block_ref.shape
+def chip_kernel(n, half_ref, blocks_ref, *refs):
+    mates, (away_ref, out_ref, own_ref, block_ref), refs = refs[:n], refs[n : n + 4], refs[n + 4 :]
+    held, (total_ref, own_total_ref, arrived) = refs[:n], refs[n:]
+    count, rows, width = block_ref.shape
 
     def copies(k):
         part = chunk(k, rows)
@@ -151,6 +147,58 @@
         yield pltpu.make_async_copy(block, block_ref.at[:, part], arrived.at[k, 0])
         for m in range(n):
             yield pltpu.make_async_copy(mates[m].at[part], held[m].at[part], arrived.at[k, m + 1])
+
+    for k in range(CHUNKS):
+        for copy in copies(k):
+            copy.start()
+    for k in range(CHUNKS):
+        for copy in copies(k):
+            copy.wait()
+        part = chunk(k, rows)
+        for m, mate_ref in enumerate(held):
+            for orb in range(count):
+                term = lax.dot_general(mate_ref[part], block_ref[orb, part], ROWS, preferred_element_type=F32)
+                tally(total_ref, out_ref, k, (orb, slice(m * width, (m + 1) * width)), term)
+        for at, (i, j) in enumerate(pairs_of(count)):
+            term = lax.dot_general(block_ref[i, part], block_ref[j, part], ROWS, preferred_element_type=F32)
+            if k == 0:
+                term = term + away_ref[at]
+            tally(own_total_ref, own_ref, k, at, term)
+
+
+def chip_products(half, blocks, mates, away):
+    count, rows, width = blocks.shape
+    rows, n = rows // 2, len(mates)
+    anywhere = pl.BlockSpec(memory_space=pl.ANY)
+    return pl.pallas_call(
+        functools.partial(chip_kernel, n),
+        in_specs=in_smem(1) + [anywhere] * (1 + n) + in_vmem(1),
+        out_specs=in_vmem(3),
+        out_shape=[
+            jax.ShapeDtypeStruct((count, n * width, width), BF16),
+            jax.ShapeDtypeStruct(away.shape, F32),
+            jax.ShapeDtypeStruct((count, rows, width), BF16),
+        ],
+        scratch_shapes=[
+            *(pltpu.VMEM(m.shape, BF16) for m in mates),
+            pltpu.VMEM((count, n * width, width), F32),
+            pltpu.VMEM(away.shape, F32),
+            pltpu.SemaphoreType.DMA((CHUNKS, n + 1)),
+        ],
+        compiler_params=params(40),
+        cost_estimate=cost(2 * count * rows * n * width * width, 4 * rows * count * width),
+        name="chip_products",
+    )(half, blocks, *mates, away)
+
+
+def line_kernel(n, block_ref, *refs):
+    mates, out_ref, held, (total_ref, arrived) = refs[:n], refs[n], refs[n + 1 : 2 * n + 1], refs[2 * n + 1 :]
+    count, rows, _ = block_ref.shape
+
+    def copies(k):
+        for m in range(n):
+            part = chunk(k, rows)
+            yield pltpu.make_async_copy(mates[m].at[part], held[m].at[part], arrived.at[k, m])
 
     for k in range(CHUNKS):
         for copy in copies(k):
@@ -166,51 +214,36 @@
                 term = lax.dot_general(mate_ref[part], block_ref[orb, part], ROWS, preferred_element_type=F32)
                 tally(total_ref, out_ref, k, (orb, slice(at, at + cols)), term)
             at += cols
-        if with_own:
-            for at, (i, j) in enumerate(pairs_of(count)):
-                term = lax.dot_general(block_ref[i, part], block_ref[j, part], ROWS, preferred_element_type=F32)
-                if k == 0:
-                    term = term + away_ref[at]
-                tally(own_total[0], own_ref, k, at, term)
-
-
-def mate_products(half, blocks, mates, away=None):
-    count, rows, width = blocks.shape
-    rows = rows // 2
+
+
+def line_products(block, mates):
+    count, rows, width = block.shape
     n, cols = len(mates), sum(m.shape[1] for m in mates)
-    anywhere = pl.BlockSpec(memory_space=pl.ANY)
-    out = [jax.ShapeDtypeStruct((count, cols, width), BF16)]
-    own_total = []
-    if away is not None:
-        out.append(jax.ShapeDtypeStruct(away.shape, F32))
-        own_total.append(pltpu.VMEM(away.shape, F32))
-    results = pl.pallas_call(
-        functools.partial(mate_kernel, n, away is not None),
-        in_specs=in_smem(1) + [anywhere] * (1 + n) + in_vmem(len(out) - 1),
-        out_specs=in_vmem(len(out)),
-        out_shape=out,
+    return pl.pallas_call(
+        functools.partial(line_kernel, n),
+        in_specs=in_vmem(1) + [pl.BlockSpec(memory_space=pl.ANY)] * n,
+        out_specs=in_vmem(1)[0],
+        out_shape=jax.ShapeDtypeStruct((count, cols, width), BF16),
         scratch_shapes=[
             *(pltpu.VMEM(m.shape, BF16) for m in mates),
-            pltpu.VMEM((count, rows, width), BF16),
             pltpu.VMEM((count, cols, width), F32),
-            pltpu.SemaphoreType.DMA((CHUNKS, n + 1)),
-            *own_total,
+            pltpu.SemaphoreType.DMA((CHUNKS, n)),
         ],
-        compiler_params=params(49),
+        compiler_params=params(10),
         cost_estimate=cost(2 * count * rows * cols * width, 2 * rows * (count * width + cols)),
-        name="mate_products",
-    )(half, blocks, *mates, *([] if away is None else [away]))
-    return results[0] if away is None else results
-
-
-def local_kernel(kind_ref, row_ref, col_ref, own_ref, sent_ref, got_ref, out_ref):
+        name="line_products",
+    )(block, *mates)
+
+
+def local_kernel(at_ref, own_ref, sent_ref, got_ref, out_ref):
     count, _, width = sent_ref.shape
+    slots = out_ref.shape[0]
 
     def rows_of(orbital):
         return pl.ds(pl.multiple_of(orbital * width, width), width)
 
     def body(slot, carry):
-        kind, row, col = kind_ref[slot], row_ref[slot], col_ref[slot]
+        kind, row, col = at_ref[slot], at_ref[slots + slot], at_ref[2 * slots + slot]
 
         @pl.when(kind == 0)
         def _():
@@ -239,17 +272,17 @@
     lax.fori_loop(0, out_ref.shape[0], body, 0)
 
 
-def local_integrals(kind, row, col, own, sent, got):
-    slots, width = kind.shape[0], own.shape[-1]
+def local_integrals(slot_at, slots, own, sent, got):
+    width = own.shape[-1]
     return pl.pallas_call(
         local_kernel,
-        in_specs=in_smem(3) + in_vmem(3),
+        in_specs=in_smem(1) + in_vmem(3),
         out_specs=in_vmem(1)[0],
         out_shape=jax.ShapeDtypeStruct((slots, width, width), BF16),
         compiler_params=params(8),
         cost_estimate=cost(4 * slots * width * width, 8 * MIB),
         name="local_integrals",
-    )(kind, row, col, own, sent, got)
+    )(slot_at, own, sent, got)
 
 
 def pick(groups, refs, orbital, index, into_ref):
@@ -267,13 +300,14 @@
             at += size
 
 
-def cross_kernel(groups, kind_ref, row_ref, col_ref, inverse_ref, part_ref, other_ref, *refs):
+def cross_kernel(groups, at_ref, row_gap_ref, col_gap_ref, inverse_ref, part_ref, other_ref, *refs):
     n = len(groups)
     sent, got = list(zip(refs[:n], refs[n : 2 * n], strict=True)), [(r,) for r in refs[2 * n : 3 * n]]
-    base_ref, rounded_ref, direct_ref, turned_ref = refs[3 * n :]
+    base_ref, rounded_ref, mate_ref, direct_ref, turned_ref = refs[3 * n :]
+    slots = rounded_ref.shape[0]
 
     def body(slot, carry):
-        kind, row, col = kind_ref[slot], row_ref[slot], col_ref[slot]
+        kind, row, col = at_ref[slot], at_ref[slots + slot], at_ref[2 * slots + slot]
 
         def store(value):
             value = -value * inverse_ref[slot]
@@ -290,53 +324,80 @@
         def _():
             store(part_ref[slot].astype(F32) + other_ref[slot].astype(F32))
 
+        row, col = at_ref[4 * slots + slot], at_ref[5 * slots + slot]
+
+        @pl.when(at_ref[3 * slots + slot] == 1)
+        def _():
+            pick(groups, sent, row, col, direct_ref)
+            pick(groups, got, col, row, turned_ref)
+            gap = row_gap_ref[row] + col_gap_ref[col]
+            mate_ref[slot] = (-(direct_ref[...] + turned_ref[...].T) / gap).astype(BF16)
+
         return carry
 
-    lax.fori_loop(0, kind_ref.shape[0], body, 0)
-
-
-def cross_amplitudes(groups, kind, row, col, inverse, local, sent, others, got):
+    lax.fori_loop(0, slots, body, 0)
+
+
+def cross_amplitudes(groups, at, row_gap, col_gap, inverse, local, sent, others, got):
     slots, width, _ = inverse.shape
     return pl.pallas_call(
         functools.partial(cross_kernel, groups),
-        in_specs=in_smem(3) + in_vmem(3 + len(sent) + len(others) + len(got)),
-        out_specs=in_vmem(2),
-        out_shape=[jax.ShapeDtypeStruct((slots, width, width), F32), jax.ShapeDtypeStruct((slots, width, width), BF16)],
-        scratch_shapes=[pltpu.VMEM((width, width), F32), pltpu.VMEM((width, width), F32)],
+        in_specs=in_smem(1) + in_vmem(5 + len(sent) + len(others) + len(got)),
+        out_specs=in_vmem(3),
+        out_shape=[jax.ShapeDtypeStruct((slots, width, width), F32)]
+        + [jax.ShapeDtypeStruct((slots, width, width), BF16)] * 2,
+        scratch_shapes=[
+            pltpu.VMEM((width, width), F32),
+            pltpu.VMEM((width, width), F32),
+        ],
         compiler_params=params(8),
         cost_estimate=cost(4 * slots * width * width, 8 * MIB),
         name="cross_amplitudes",
-    )(kind, row, col, inverse, *local, *sent, *others, *got)
-
-
-def sweep_kernel(at_ref, weight_ref, own_ref, chip_ref, line_ref, rows_ref, cols_ref, base_ref, inverse_ref, out_ref, held_ref):
+    )(at, row_gap, col_gap, inverse, *local, *sent, *others, *got)
+
+
+def sweep_kernel(patched, at_ref, weight_ref, *refs):
+    if patched:
+        patch_at_ref, patch_ref, *refs = refs
+    own_ref, chip_ref, line_ref, rows_ref, cols_ref, inverse_ref, base_ref, out_ref, held_ref = refs
     slots, neighbours = rows_ref.shape[:2]
+
     held_ref[:slots] = own_ref[...]
     held_ref[slots : 2 * slots] = chip_ref[...]
     held_ref[2 * slots :] = line_ref[...]
+    if patched:
+
+        def patch(slot, carry):
+            @pl.when(patch_at_ref[3 * slots + slot] == 1)
+            def _():
+                held_ref[2 * slots + slot] = patch_ref[slot]
+
+            return carry
+
+        lax.fori_loop(0, slots, patch, 0)
     for slot in range(slots):
         total = None
         for n in range(neighbours):
-            source = held_ref[at_ref[slot, n]]
+            source = held_ref[at_ref[slot * neighbours + n]]
             selected = jnp.dot(rows_ref[slot, n], source, preferred_element_type=F32).astype(BF16)
-            term = weight_ref[slot, n] * jnp.dot(selected, cols_ref[slot, n], preferred_element_type=F32)
+            term = weight_ref[slot * neighbours + n] * jnp.dot(selected, cols_ref[slot, n], preferred_element_type=F32)
             total = term if total is None else total + term
         out_ref[slot] = (base_ref[slot] + total * inverse_ref[slot]).astype(out_ref.dtype)
 
 
-def sweep_amplitudes(at, weights, own, chip, line, row_match, col_match, base, inverse):
+def sweep_amplitudes(at, weights, own, chip, line, row_match, col_match, base, inverse, patch=()):
     slots, width, _ = own.shape
-    neighbours = at.shape[1]
+    neighbours = row_match.shape[1]
     return pl.pallas_call(
-        sweep_kernel,
-        in_specs=in_smem(2) + in_vmem(7),
+        functools.partial(sweep_kernel, bool(patch)),
+        in_specs=in_smem(2 + len(patch[:1])) + in_vmem(7 + len(patch[1:])),
         out_specs=in_vmem(1)[0],
         out_shape=jax.ShapeDtypeStruct((slots, width, width), BF16),
         scratch_shapes=[pltpu.VMEM((3 * slots, width, width), BF16)],
         compiler_params=params(8),
         cost_estimate=cost(4 * slots * neighbours * width**3, 16 * MIB),
         name="sweep_amplitudes",
-    )(at, weights, own, chip, line, row_match, col_match, base, inverse)
+    )(at, weights, *patch, own, chip, line, row_match, col_match, inverse, base)
 
 
 def on_device(three_index, pair_orbs, live_pairs, domains, coupled, fock_coupling_weight, occ_energy, virt_energy):
@@ -362,51 +423,71 @@
 
     def cross_products(k, *earlier):
         mates = lax.optimization_barrier((*from_line[k], *earlier))[: len(from_line[k])]
-        return mate_products(half, three_index, mates)
+        return line_products(block, mates)
 
     domains, pair_orbs, coupled = lax.optimization_barrier((domains, pair_orbs, coupled, own_away, from_line[0][0]))[:3]
 
-    local = jnp.arange(slots, dtype=jnp.int32)
     pairs = lax.dynamic_slice_in_dim(pair_orbs, owner * slots, slots, 0)
-    live = (local < live_pairs[owner]).astype(F32)[:, None, None]
+    line_owner = owner - 1 + 2 * parity
+    mate_pairs = lax.dynamic_slice_in_dim(pair_orbs, line_owner * slots, slots, 0)
     rows, cols = pairs[:, 0], pairs[:, 1]
     row_dom, col_dom = domains[rows], domains[cols]
 
     def kind_of(other):
         return jnp.where(other == owner, 0, jnp.where(other == chip_owner, 1, 2)).astype(jnp.int32)
 
-    def energy(dom):
-        listed = jnp.arange(virt_energy.shape[0], dtype=jnp.int32)
-        return jnp.sum(jnp.where(dom[..., None] == listed, virt_energy, 0.0), axis=-1)
-
-    gaps = (
-        energy(row_dom)[:, :, None]
-        + energy(col_dom)[:, None, :]
-        - occ_energy[rows][:, None, None]
-        - occ_energy[cols][:, None, None]
+    seen = min(3 * count, domains.shape[0])
+    window = jnp.clip((owner - 1) * count, 0, domains.shape[0] - seen)
+    listed = jnp.arange(virt_energy.shape[0], dtype=jnp.int32)
+    seen_dom = lax.dynamic_slice_in_dim(domains, window, seen, 0)
+    seen_energy = jnp.sum(jnp.where(seen_dom[:, :, None] == listed, virt_energy, 0.0), axis=-1)
+    seen_gap = seen_energy - lax.dynamic_slice_in_dim(occ_energy, window, seen, 0)[:, None]
+    inverse = (jnp.arange(slots) < live_pairs[owner]).astype(F32)[:, None, None] / (
+        seen_gap[rows - window][:, :, None] + seen_gap[cols - window][:, None, :]
     )
-    inverse = live / gaps
+    own_gap = lax.dynamic_slice_in_dim(seen_gap, owner * count - window, count, 0)
+    line_gap = lax.dynamic_slice_in_dim(seen_gap, line_owner * count - window, count, 0)
+    row_gap = jnp.broadcast_to(line_gap[:, :, None], (count, width, width))
     source_rows = domains[pair_orbs[coupled, 0]]
     source_cols = domains[pair_orbs[coupled, 1]]
     kind, row, col = kind_of(cols // count), rows % count, cols % count
-    at = kind_of(coupled // slots) * slots + coupled % slots
-
-    chip_sent, own = mate_products(half, after(three_index, inverse, source_rows, source_cols), from_chip, own_away)
-    sent = [cross_products(0, chip_sent)]
-    terms = [aux_terms(sent[0])]
-    local = local_integrals(kind, row, col, own, chip_sent, after(chip_mate(chip_sent), sent[0]))
+    inward = (
+        (mate_pairs[:, 1] // count == owner)
+        & (mate_pairs[:, 0] // count == line_owner)
+        & (jnp.arange(slots) < live_pairs[line_owner])
+    )
+    slot_at = jnp.concatenate(
+        [kind, row, col, inward.astype(jnp.int32), mate_pairs[:, 0] % count, mate_pairs[:, 1] % count]
+    )
+    at = (kind_of(coupled // slots) * slots + coupled % slots).reshape(-1)
+    weights = fock_coupling_weight.reshape(-1)
+
+    three_index, slot_at, at, weights, row_gap, own_gap, inverse, row_dom, col_dom, source_rows, source_cols = (
+        lax.optimization_barrier(
+            (three_index, slot_at, at, weights, row_gap, own_gap[:, None, :], inverse, row_dom, col_dom, source_rows, source_cols)
+        )
+    )
+    chip_sent, own, block = chip_products(half, three_index, from_chip, own_away)
+    local = local_integrals(slot_at, slots, own, chip_sent, chip_mate(chip_sent))
     local_terms = aux_terms(local)
-    sums = []
+    sent, terms, sums, got = [], [], [], []
     earlier = (local,)
-    for k in range(1, len(groups)):
+    for k in range(len(groups)):
         sent.append(cross_products(k, *earlier))
         terms.append(aux_terms(sent[k]))
-        sums.append(total(terms[k - 1], sent[k]))
-        earlier = (sums[-1],)
-    sums.append(total(terms[-1]))
-    got = [line_mate(v) for v in sums]
-    base, rounded = cross_amplitudes(
-        groups, kind, row, col, inverse, local_terms, [a for a, _ in terms], [b for _, b in terms], got
+        if k == 1:
+            part, other = lax.optimization_barrier((*local_terms, sent[1]))[:2]
+            mate_start = (-(part.astype(F32) + other.astype(F32)) * inverse).astype(BF16)
+        if k:
+            sums.append(total(terms[k - 1], sent[k]))
+            got.append(line_mate(sums[-1]))
+        earlier = (sent[k], *([mate_start] if k == 1 else []), *(sums[-1:] if k else local_terms))
+    sums.append(total(terms[-1], got[0]))
+    got.append(line_mate(sums[-1]))
+    from_mate = line_mate(after(mate_start, sums[-1]))
+    base, rounded, patch = cross_amplitudes(
+        groups, slot_at, row_gap, own_gap, inverse, local_terms,
+        [a for a, _ in terms], [b for _, b in terms], got,
     )
     row_dom, col_dom, source_rows, source_cols = lax.optimization_barrier(
         (row_dom, col_dom, source_rows, source_cols, rounded)
@@ -414,9 +495,9 @@
     row_match = (row_dom[:, None, :, None] == source_rows[:, :, None, :]).astype(BF16)
     col_match = (source_cols[:, :, :, None] == col_dom[:, None, None, :]).astype(BF16)
     for sweep in range(ITERS):
+        from_line, patches = (line_mate(rounded), ()) if sweep else (from_mate, (slot_at, patch))
         rounded = sweep_amplitudes(
-            at, fock_coupling_weight, rounded, chip_mate(rounded), line_mate(rounded),
-            row_match, col_match, base, inverse,
+            at, weights, rounded, chip_mate(rounded), from_line, row_match, col_match, base, inverse, patches
         )
     return rounded
 

time: 166 us -> 150 us (0.904)
  waiting for transfers between devices: 61.3 us -> 44.5 us
  local copies, waits for them, and re-layouts: 11.5 us -> 16.3 us
  Pallas kernels: 45.5 us -> 41.5 us
  starting transfers between devices: 38.9 us -> 36.8 us
    ppermute x9, waiting for transfers between devices: 54.9 us -> 33.3 us  [line_mate(): return lax.ppermute(value, LINE, pairs)]
    pallas_call x7, Pallas kernels: 37.9 us -> 33.8 us  [the longest x1 14.3 us: chip_products(): pl.pallas_call(functools.partial(chip_kernel, n), in_specs=in_smem(1) + [...]
    ppermute x6, waiting for transfers between devices: 0.02 us -> 2.49 us  [chip_mate(): return lax.ppermute(value, 'occ', [(0, 1), (1, 0)])]
    ppermute x4, waiting for transfers between devices: 6.42 us -> 8.66 us  [aux_terms(): other = lax.ppermute(value, 'aux', [(i, i ^ step) for i in range(count)])]
    convert_element_type x1 -> x3, other arithmetic: 0.69 us -> 2.84 us  [the longest x1 1.2 us: on_device(): inward.astype(jnp.int32)]
    ppermute x9, starting transfers between devices: 33.9 us -> 31.8 us  [line_mate(): return lax.ppermute(value, LINE, pairs)]
    reduce_sum x1, other arithmetic: 4.3 us -> 2.23 us  [on_device(): jnp.sum(jnp.where(seen_dom[:, :, None] == listed, virt_energy, 0.0), axis...]
    unnamed x29, local copies, waits for them, and re-layouts: 2.61 us -> 4.46 us
  transfers between devices with their start and end apart: 19 -> 19, of which waited for: 7 -> 8; matrix products, arithmetic and copies ran while one was open for 9% -> 13% of each run, Pallas kernels for 21% -> 23%
where the time goes in v4:
time: 150 us; the launch traced here: 149 us
  waiting for transfers between devices  44.5 us (30%)
  Pallas kernels  41.5 us (28%)
  starting transfers between devices  36.8 us (25%)
  local copies, waits for them, and re-layouts  16.3 us (11%)
  other arithmetic  9.48 us (6%)
    ppermute x9, waiting for transfers between devices, line_mate(): return lax.ppermute(value, LINE, pairs)  33.3 us
    ppermute x9, starting transfers between devices, line_mate(): return lax.ppermute(value, LINE, pairs)  31.8 us
    pallas_call x1, Pallas kernels, chip_products(): pl.pallas_call(functools.partial(chip_kernel, n), in_specs=in_smem(1) + [...  14.3 us
    pallas_call x3, Pallas kernels, line_products(): pl.pallas_call(functools.partial(line_kernel, n), in_specs=in_vmem(1) + [...  10.6 us
    ppermute x4, waiting for transfers between devices, aux_terms(): other = lax.ppermute(value, 'aux', [(i, i ^ step) for i in range(count)])  8.66 us
    pallas_call x2, Pallas kernels, sweep_amplitudes(): pl.pallas_call(functools.partial(sweep_kernel, bool(patch)), in_specs=in_...  7.64 us
    pallas_call x1, Pallas kernels, send_blocks(): pl.pallas_call(send_kernel, in_specs=in_smem(1) + [anywhere], out_specs=[...  5.78 us
    unnamed x29, local copies, waits for them, and re-layouts  4.46 us
  transfers between devices with their start and end apart: 19, of which 8 were waited for; matrix products, arithmetic and copies ran while one was open for 13% of the time, Pallas kernels for 23%

profile of v4, /device:TPU:1, one launch (start us, length us, event | category | flops | bytes accessed | tf_op | source)
XLA Modules:
  0.0 149.1 jit_solution(5437339597086840714)
XLA Ops:
  0.0 2.5 %dynamic-slice_bitcast_fusion = bf16[5120,128]{1,0:T(8,128)(2,1)} fusion(bf16[3,10240,256]{2,1,0:T(8,128)(2,1)} %blocks_ref.1, s32[]{:T(128)S(6)} %select_n.124), kind=kLoop, calls=%fused_computation.14 | loop fusion | bytes 2621444 | tf_op jit(solution)/shard_map/squeeze | solution.py:415
  2.5 4.6 %collective-permute-start = (bf16[5120,128]{1,0:T(8,128)(2,1)}, bf16[5120,128]{1,0:T(8,128)(2,1)}, u32[]{:S(2)}, u32[]{:S(2)}) collective-permute-start(bf16[5120,128]{1,0:T(8,128)(2,1)} %dynamic-slice_bitcast_fusion), channel_id=1, source_target_pairs={{1,4},{4,1},{5,8},{8,5},{9,12},{12,9},{3,6},{6,3},{7,10},{10,7},{1... | collective-permute-start | bytes 3932168 | tf_op jit(solution)/shard_map/ppermute | solution.py:27
  7.2 5.8 %send_blocks.1 = (bf16[5120,256]{1,0:T(8,128)(2,1)}, bf16[5120,256]{1,0:T(8,128)(2,1)}, bf16[5120,256]{1,0:T(8,128)(2,1)}, bf16[5120,128]{1,0:T(8,128)(2,1)S(1)}, f32[3,256,256]{2,1,0:T(8,128)S(1)}) custom-call(s32[1]{0:T(128)S(6)} %sub.55.half_ref, bf16[3,10240,256]{2,1,0:T(8,128)(2,1)} %blocks_ref.1), custom_call_target="tpu_custom_call" | custom-call | flops 1966080 | bytes 15360 | tf_op jit(solution)/shard_map/send_blocks/pallas_call | solution.py:121
  16.0 3.8 %collective-permute-start.7 = (bf16[5120,256]{1,0:T(8,128)(2,1)}, bf16[5120,256]{1,0:T(8,128)(2,1)S(1)}, u32[]{:S(2)}, u32[]{:S(2)}) collective-permute-start(bf16[5120,256]{1,0:T(8,128)(2,1)} %get-tuple-element.61), channel_id=1, source_target_pairs={{1,4},{4,1},{5,8},{8,5},{9,12},{12,9},{3,6},{6,3},{7,10},{10,7},{1... | collective-permute-start | bytes 7864328 | tf_op jit(solution)/shard_map/ppermute | solution.py:27
  24.9 2.2 %select_reduce_fusion = f32[9,256]{1,0:T(8,128)S(1)} fusion(f32[1792]{0:T(1024)S(1)} %copy-done.10, s32[9,256]{1,0:T(8,128)S(1)} %constant_dynamic-slice_fusion.2), kind=kLoop, calls=%fused_computation.8 | loop fusion | flops 12384000 | bytes 25600 | tf_op jit(solution)/shard_map/reduce_sum | solution.py:443
  36.7 14.3 %chip_products.1 = (bf16[3,768,256]{2,1,0:T(8,128)(2,1)S(1)}, f32[3,256,256]{2,1,0:T(8,128)S(1)}, bf16[3,5120,256]{2,1,0:T(8,128)(2,1)}) custom-call(s32[1]{0:T(128)} %bitcast.half_ref, bf16[3,10240,256]{2,1,0:T(8,128)(2,1)} %blocks_ref.1, bf16[5120,256]{1,0:T(8,128)(2,1)} %collective-permute-done.1.refs_0_, ...), custom_call_target="tpu_custom_call" | custom-call | flops 5898240 | bytes 15360 | tf_op jit(solution)/shard_map/chip_products/pallas_call | solution.py:173
  51.5 2.5 %collective-permute-done.4.got_ref = bf16[3,768,256]{2,1,0:T(8,128)(2,1)S(1)} collective-permute-done((bf16[3,768,256]{2,1,0:T(8,128)(2,1)S(1)}, bf16[3,768,256]{2,1,0:T(8,128)(2,1)S(1)}, u32[]{:S(2)}, u32[]{:S(2)}) %collective-permute-start.4) | collective-permute-done | bytes 1179680 | tf_op jit(solution)/shard_map/ppermute | solution.py:19
  56.6 3.8 %collective-permute-start.8 = (bf16[5120,128]{1,0:T(8,128)(2,1)S(1)}, bf16[5120,128]{1,0:T(8,128)(2,1)S(1)}, u32[]{:S(2)}, u32[]{:S(2)}) collective-permute-start(bf16[5120,128]{1,0:T(8,128)(2,1)S(1)} %copy-done.4), channel_id=1, source_target_pairs={{1,4},{4,1},{5,8},{8,5},{9,12},{12,9},{3,6},{6,3},{7,10},{10,7},{1... | collective-permute-start | bytes 3932168 | tf_op jit(solution)/shard_map/ppermute | solution.py:27
  60.5 3.2 %copy-done.2 = bf16[3,5120,256]{2,1,0:T(8,128)(2,1)S(1)} copy-done((bf16[3,5120,256]{2,1,0:T(8,128)(2,1)S(1)}, bf16[3,5120,256]{2,1,0:T(8,128)(2,1)}, u32[]{:S(2)}) %copy-start.2) | copy-done | bytes 7864344
  63.7 5.4 %line_products.3.refs_0_ = bf16[3,384,256]{2,1,0:T(8,128)(2,1)S(1)} custom-call(bf16[3,5120,256]{2,1,0:T(8,128)(2,1)S(1)} %copy-done.2, bf16[5120,128]{1,0:T(8,128)(2,1)} %collective-permute-done.refs_0_, bf16[5120,256]{1,0:T(8,128)(2,1)} %collective-permute-done.6.refs_1_), custom_call_target="tpu_custom_call" | custom-call | flops 2949120 | bytes 11520 | tf_op jit(solution)/shard_map/line_products/pallas_call | solution.py:222
  69.4 9.7 %collective-permute-done.7.refs_0_ = bf16[5120,256]{1,0:T(8,128)(2,1)S(1)} collective-permute-done((bf16[5120,256]{1,0:T(8,128)(2,1)}, bf16[5120,256]{1,0:T(8,128)(2,1)S(1)}, u32[]{:S(2)}, u32[]{:S(2)}) %collective-permute-start.7) | collective-permute-done | bytes 2621472 | tf_op jit(solution)/shard_map/ppermute | solution.py:27
  79.4 3.1 %line_products.4.refs_1_ = bf16[3,256,256]{2,1,0:T(8,128)(2,1)S(1)} custom-call(bf16[3,5120,256]{2,1,0:T(8,128)(2,1)S(1)} %copy-done.2, bf16[5120,256]{1,0:T(8,128)(2,1)S(1)} %collective-permute-done.7.refs_0_), custom_call_target="tpu_custom_call" | custom-call | flops 1966080 | bytes 10240 | tf_op jit(solution)/shard_map/line_products/pallas_call | solution.py:222
  83.9 8.2 %collective-permute-done.9.refs_3_ = bf16[3,384,256]{2,1,0:T(8,128)(2,1)S(1)} collective-permute-done((bf16[3,384,256]{2,1,0:T(8,128)(2,1)S(1)}, bf16[3,384,256]{2,1,0:T(8,128)(2,1)S(1)}, u32[]{:S(2)}, u32[]{:S(2)}) %collective-permute-start.9) | collective-permute-done | bytes 589856 | tf_op jit(solution)/shard_map/ppermute | solution.py:34
  92.2 5.5 %collective-permute-start.12 = (bf16[3,384,256]{2,1,0:T(8,128)(2,1)S(1)}, bf16[3,384,256]{2,1,0:T(8,128)(2,1)S(1)}, u32[]{:S(2)}, u32[]{:S(2)}) collective-permute-start(bf16[3,384,256]{2,1,0:T(8,128)(2,1)S(1)} %add_convert_fusion), channel_id=1, source_target_pairs={{1,4},{4,1},{5,8},{8,5},{9,12},{12,9},{3,6},{6,3},{7,10},{10,7},{1... | collective-permute-start | bytes 1769480 | tf_op jit(solution)/shard_map/ppermute | solution.py:27
  98.2 2.1 %line_products.5.refs_2_ = bf16[3,128,256]{2,1,0:T(8,128)(2,1)S(1)} custom-call(bf16[3,5120,256]{2,1,0:T(8,128)(2,1)S(1)} %bitcast.57, bf16[5120,128]{1,0:T(8,128)(2,1)S(1)} %collective-permute-done.8.refs_0_), custom_call_target="tpu_custom_call" | custom-call | flops 983040 | bytes 8960 | tf_op jit(solution)/shard_map/line_products/pallas_call | solution.py:222
  101.7 3.8 %collective-permute-start.13 = (bf16[3,256,256]{2,1,0:T(8,128)(2,1)S(1)}, bf16[3,256,256]{2,1,0:T(8,128)(2,1)S(1)}, u32[]{:S(2)}, u32[]{:S(2)}) collective-permute-start(bf16[3,256,256]{2,1,0:T(8,128)(2,1)S(1)} %add_convert_fusion.1), channel_id=1, source_target_pairs={{1,4},{4,1},{5,8},{8,5},{9,12},{12,9},{3,6},{6,3},{7,10},{10,7},{1... | collective-permute-start | bytes 1179656 | tf_op jit(solution)/shard_map/ppermute | solution.py:27
  105.6 3.6 %collective-permute-start.14 = (bf16[3,128,256]{2,1,0:T(8,128)(2,1)S(1)}, bf16[3,128,256]{2,1,0:T(8,128)(2,1)S(1)}, u32[]{:S(2)}, u32[]{:S(2)}) collective-permute-start(bf16[3,128,256]{2,1,0:T(8,128)(2,1)S(1)} %add_convert_fusion.2), channel_id=1, source_target_pairs={{1,4},{4,1},{5,8},{8,5},{9,12},{12,9},{3,6},{6,3},{7,10},{10,7},{1... | collective-permute-start | bytes 589832 | tf_op jit(solution)/shard_map/ppermute | solution.py:27
  109.2 2.2 %collective-permute-start.16 = (bf16[8,256,256]{2,1,0:T(8,128)(2,1)S(1)}, bf16[8,256,256]{2,1,0:T(8,128)(2,1)S(1)}, u32[]{:S(2)}, u32[]{:S(2)}) collective-permute-start(bf16[8,256,256]{2,1,0:T(8,128)(2,1)S(1)} %multiply_convert_fusion), channel_id=1, source_target_pairs={{1,4},{4,1},{5,8},{8,5},{9,12},{12,9},{3,6},{6,3},{7,10},{10,7},{1... | collective-permute-start | bytes 3145736 | tf_op jit(solution)/shard_map/ppermute | solution.py:27
  113.0 1.9 %cross_amplitudes.1 = (f32[8,256,256]{2,1,0:T(8,128)S(1)}, bf16[8,256,256]{2,1,0:T(8,128)(2,1)S(1)}, bf16[8,256,256]{2,1,0:T(8,128)(2,1)S(1)}) custom-call(s32[48]{0:T(128)S(1)} %concatenate.9.at_ref.refs_0_, f32[3,256,256]{2,1,0:T(8,128)S(1)} %broadcast_in_dim.31.row_gap_ref, f32[3,1,256]{2,1,0:T(1,128)S(1)} %broadcast_in_dim.34.col_gap_ref, ...), custom_call_target="tpu_custom_call" | custom-call | flops 2048 | bytes 8192 | tf_op jit(solution)/shard_map/cross_amplitudes/pallas_call | solution.py:343
  117.4 8.0 %collective-permute-done.16.refs_4_ = bf16[8,256,256]{2,1,0:T(8,128)(2,1)S(1)} collective-permute-done((bf16[8,256,256]{2,1,0:T(8,128)(2,1)S(1)}, bf16[8,256,256]{2,1,0:T(8,128)(2,1)S(1)}, u32[]{:S(2)}, u32[]{:S(2)}) %collective-permute-start.16) | collective-permute-done | bytes 1048608 | tf_op jit(solution)/shard_map/ppermute | solution.py:27
  125.3 3.4 %sweep_amplitudes.2.refs_0_ = bf16[8,256,256]{2,1,0:T(8,128)(2,1)S(1)} custom-call(s32[32]{0:T(128)S(1)} %reshape.73.at_ref, f32[32]{0:T(128)S(1)} %reshape.74.weight_ref, s32[48]{0:T(128)S(1)} %concatenate.9.at_ref.refs_0_, bf16[8,256,256]{2,1,0:T(8,128)(2,1)S(1)} %get-tuple-element.79.refs_1_, bf16[8,256,256]{2,1,0:T(8,128)(2,1)S(1)} %get-tuple-element.80.refs_2_, ...), custom_call_target="tpu_custom_call" | custom-call | flops 2097152 | bytes 16384 | tf_op jit(solution)/shard_map/sweep_amplitudes/pallas_call | solution.py:391
  128.7 2.6 %collective-permute-start.18 = (bf16[8,256,256]{2,1,0:T(8,128)(2,1)S(1)}, bf16[8,256,256]{2,1,0:T(8,128)(2,1)S(1)}, u32[]{:S(2)}, u32[]{:S(2)}) collective-permute-start(bf16[8,256,256]{2,1,0:T(8,128)(2,1)S(1)} %sweep_amplitudes.2.refs_0_), channel_id=1, source_target_pairs={{1,4},{4,1},{5,8},{8,5},{9,12},{12,9},{3,6},{6,3},{7,10},{10,7},{1... | collective-permute-start | bytes 3145736 | tf_op jit(solution)/shard_map/ppermute | solution.py:27
  131.4 13.4 %collective-permute-done.18.refs_2_ = bf16[8,256,256]{2,1,0:T(8,128)(2,1)S(1)} collective-permute-done((bf16[8,256,256]{2,1,0:T(8,128)(2,1)S(1)}, bf16[8,256,256]{2,1,0:T(8,128)(2,1)S(1)}, u32[]{:S(2)}, u32[]{:S(2)}) %collective-permute-start.18) | collective-permute-done | bytes 1048608 | tf_op jit(solution)/shard_map/ppermute | solution.py:27
  144.8 4.2 %sweep_amplitudes.3 = bf16[8,256,256]{2,1,0:T(8,128)(2,1)} custom-call(s32[32]{0:T(128)S(1)} %reshape.73.at_ref, f32[32]{0:T(128)S(1)} %reshape.74.weight_ref, bf16[8,256,256]{2,1,0:T(8,128)(2,1)S(1)} %sweep_amplitudes.2.refs_0_, bf16[8,256,256]{2,1,0:T(8,128)(2,1)S(1)} %collective-permute-done.17.refs_1_, ...), custom_call_target="tpu_custom_call" | custom-call | flops 2097152 | bytes 16384 | tf_op jit(solution)/shard_map/sweep_amplitudes/pallas_call | solution.py:391
  (103 shorter events, 28.8 us)
Async XLA Ops:
  0.0 24.8 %copy-start = (s32[24,256]{1,0:T(8,128)S(1)}, s32[24,256]{1,0:T(8,128)}, u32[]{:S(2)}) copy-start(s32[24,256]{1,0:T(8,128)} %param.11) | copy-start | bytes 73732
  2.5 20.2 %collective-permute-start = (bf16[5120,128]{1,0:T(8,128)(2,1)}, bf16[5120,128]{1,0:T(8,128)(2,1)}, u32[]{:S(2)}, u32[]{:S(2)}) collective-permute-start(bf16[5120,128]{1,0:T(8,128)(2,1)} %dynamic-slice_bitcast_fusion), channel_id=1, source_target_pairs={{1,4},{4,1},{5,8},{8,5},{9,12},{12,9},{3,6},{6,3},{7,10},{10,7},{1... | collective-permute-start | bytes 3932168 | tf_op jit(solution)/shard_map/ppermute | solution.py:27
  7.1 15.6 %copy-start.9 = (s32[8,4]{0,1:T(4,128)S(1)}, s32[8,4]{0,1:T(4,128)}, u32[]{:S(2)}) copy-start(s32[8,4]{0,1:T(4,128)} %param.12) | copy-start | bytes 388
  7.1 15.6 %copy-start.5 = (s32[64,2]{0,1:T(2,128)S(1)}, s32[64,2]{0,1:T(2,128)}, u32[]{:S(2)}) copy-start(s32[64,2]{0,1:T(2,128)} %param.9) | copy-start | bytes 1540
  14.1 46.4 %collective-permute-start.6 = (bf16[5120,256]{1,0:T(8,128)(2,1)}, bf16[5120,256]{1,0:T(8,128)(2,1)}, u32[]{:S(2)}, u32[]{:S(2)}) collective-permute-start(bf16[5120,256]{1,0:T(8,128)(2,1)} %get-tuple-element.60), channel_id=1, source_target_pairs={{1,4},{4,1},{5,8},{8,5},{9,12},{12,9},{3,6},{6,3},{7,10},{10,7},{1... | collective-permute-start | bytes 7864328 | tf_op jit(solution)/shard_map/ppermute | solution.py:27
  16.0 20.7 %collective-permute-start.1 = (bf16[5120,256]{1,0:T(8,128)(2,1)}, bf16[5120,256]{1,0:T(8,128)(2,1)}, u32[]{:S(2)}, u32[]{:S(2)}) collective-permute-start(bf16[5120,256]{1,0:T(8,128)(2,1)} %get-tuple-element.60), channel_id=1, source_target_pairs={{0,1},{1,0},{2,3},{3,2},{4,5},{5,4},{6,7},{7,6},{8,9},{9,8},{10,11... | collective-permute-start | bytes 7864328 | tf_op jit(solution)/shard_map/ppermute | solution.py:19
  16.0 63.0 %collective-permute-start.7 = (bf16[5120,256]{1,0:T(8,128)(2,1)}, bf16[5120,256]{1,0:T(8,128)(2,1)S(1)}, u32[]{:S(2)}, u32[]{:S(2)}) collective-permute-start(bf16[5120,256]{1,0:T(8,128)(2,1)} %get-tuple-element.61), channel_id=1, source_target_pairs={{1,4},{4,1},{5,8},{8,5},{9,12},{12,9},{3,6},{6,3},{7,10},{10,7},{1... | collective-permute-start | bytes 7864328 | tf_op jit(solution)/shard_map/ppermute | solution.py:27
  19.9 16.8 %collective-permute-start.2 = (bf16[5120,256]{1,0:T(8,128)(2,1)}, bf16[5120,256]{1,0:T(8,128)(2,1)}, u32[]{:S(2)}, u32[]{:S(2)}) collective-permute-start(bf16[5120,256]{1,0:T(8,128)(2,1)} %get-tuple-element.61), channel_id=1, source_target_pairs={{0,1},{1,0},{2,3},{3,2},{4,5},{5,4},{6,7},{7,6},{8,9},{9,8},{10,11... | collective-permute-start | bytes 7864328 | tf_op jit(solution)/shard_map/ppermute | solution.py:19
  22.7 14.0 %collective-permute-start.3 = (bf16[5120,256]{1,0:T(8,128)(2,1)}, bf16[5120,256]{1,0:T(8,128)(2,1)}, u32[]{:S(2)}, u32[]{:S(2)}) collective-permute-start(bf16[5120,256]{1,0:T(8,128)(2,1)} %get-tuple-element.62), channel_id=1, source_target_pairs={{0,1},{1,0},{2,3},{3,2},{4,5},{5,4},{6,7},{7,6},{8,9},{9,8},{10,11... | collective-permute-start | bytes 7864328 | tf_op jit(solution)/shard_map/ppermute | solution.py:19
  51.0 3.0 %collective-permute-start.4 = (bf16[3,768,256]{2,1,0:T(8,128)(2,1)S(1)}, bf16[3,768,256]{2,1,0:T(8,128)(2,1)S(1)}, u32[]{:S(2)}, u32[]{:S(2)}) collective-permute-start(bf16[3,768,256]{2,1,0:T(8,128)(2,1)S(1)} %get-tuple-element.64.sent_ref), channel_id=1, source_target_pairs={{0,1},{1,0},{2,3},{3,2},{4,5},{5,4},{6,7},{7,6},{8,9},{9,8},{10,11... | collective-permute-start | bytes 3538952 | tf_op jit(solution)/shard_map/ppermute | solution.py:19
  55.3 24.1 %collective-permute-start.5 = (bf16[8,256,256]{2,1,0:T(8,128)(2,1)S(1)}, bf16[8,256,256]{2,1,0:T(8,128)(2,1)S(1)}, u32[]{:S(2)}, u32[]{:S(2)}) collective-permute-start(bf16[8,256,256]{2,1,0:T(8,128)(2,1)S(1)} %local_integrals.1.part_ref), channel_id=1, source_target_pairs={{0,2},{2,0},{1,3},{3,1},{4,6},{6,4},{5,7},{7,5},{8,10},{10,8},{9,1... | collective-permute-start | bytes 3145736 | tf_op jit(solution)/shard_map/ppermute | solution.py:34
  56.6 41.6 %collective-permute-start.8 = (bf16[5120,128]{1,0:T(8,128)(2,1)S(1)}, bf16[5120,128]{1,0:T(8,128)(2,1)S(1)}, u32[]{:S(2)}, u32[]{:S(2)}) collective-permute-start(bf16[5120,128]{1,0:T(8,128)(2,1)S(1)} %copy-done.4), channel_id=1, source_target_pairs={{1,4},{4,1},{5,8},{8,5},{9,12},{12,9},{3,6},{6,3},{7,10},{10,7},{1... | collective-permute-start | bytes 3932168 | tf_op jit(solution)/shard_map/ppermute | solution.py:27
  63.7 34.5 %slice-start = ((s8[7864320]{0:T(1024)(128)(4,1)}), s8[3670016]{0:T(1024)(128)(4,1)S(1)}, s32[]{:S(2)}) async-start(s8[7864320]{0:T(1024)(128)(4,1)} %bitcast.56), calls=%async_computation | async-start | bytes 7340032
  69.1 29.2 %slice-start.1 = ((s8[7864320]{0:T(1024)(128)(4,1)}), s8[4194304]{0:T(1024)(128)(4,1)S(1)}, s32[]{:S(2)}) async-start(s8[7864320]{0:T(1024)(128)(4,1)} %bitcast.56), calls=%async_computation.1 | async-start | bytes 8388608
  69.1 23.0 %collective-permute-start.9 = (bf16[3,384,256]{2,1,0:T(8,128)(2,1)S(1)}, bf16[3,384,256]{2,1,0:T(8,128)(2,1)S(1)}, u32[]{:S(2)}, u32[]{:S(2)}) collective-permute-start(bf16[3,384,256]{2,1,0:T(8,128)(2,1)S(1)} %line_products.3.refs_0_), channel_id=1, source_target_pairs={{0,2},{2,0},{1,3},{3,1},{4,6},{6,4},{5,7},{7,5},{8,10},{10,8},{9,1... | collective-permute-start | bytes 1769480 | tf_op jit(solution)/shard_map/ppermute | solution.py:34
  82.6 19.0 %collective-permute-start.10 = (bf16[3,256,256]{2,1,0:T(8,128)(2,1)S(1)}, bf16[3,256,256]{2,1,0:T(8,128)(2,1)S(1)}, u32[]{:S(2)}, u32[]{:S(2)}) collective-permute-start(bf16[3,256,256]{2,1,0:T(8,128)(2,1)S(1)} %line_products.4.refs_1_), channel_id=1, source_target_pairs={{0,2},{2,0},{1,3},{3,1},{4,6},{6,4},{5,7},{7,5},{8,10},{10,8},{9,1... | collective-permute-start | bytes 1179656 | tf_op jit(solution)/shard_map/ppermute | solution.py:34
  92.2 13.3 %collective-permute-start.12 = (bf16[3,384,256]{2,1,0:T(8,128)(2,1)S(1)}, bf16[3,384,256]{2,1,0:T(8,128)(2,1)S(1)}, u32[]{:S(2)}, u32[]{:S(2)}) collective-permute-start(bf16[3,384,256]{2,1,0:T(8,128)(2,1)S(1)} %add_convert_fusion), channel_id=1, source_target_pairs={{1,4},{4,1},{5,8},{8,5},{9,12},{12,9},{3,6},{6,3},{7,10},{10,7},{1... | collective-permute-start | bytes 1769480 | tf_op jit(solution)/shard_map/ppermute | solution.py:27
  100.3 5.2 %collective-permute-start.11 = (bf16[3,128,256]{2,1,0:T(8,128)(2,1)S(1)}, bf16[3,128,256]{2,1,0:T(8,128)(2,1)S(1)}, u32[]{:S(2)}, u32[]{:S(2)}) collective-permute-start(bf16[3,128,256]{2,1,0:T(8,128)(2,1)S(1)} %line_products.5.refs_2_), channel_id=1, source_target_pairs={{0,2},{2,0},{1,3},{3,1},{4,6},{6,4},{5,7},{7,5},{8,10},{10,8},{9,1... | collective-permute-start | bytes 589832 | tf_op jit(solution)/shard_map/ppermute | solution.py:34
  101.7 11.3 %collective-permute-start.13 = (bf16[3,256,256]{2,1,0:T(8,128)(2,1)S(1)}, bf16[3,256,256]{2,1,0:T(8,128)(2,1)S(1)}, u32[]{:S(2)}, u32[]{:S(2)}) collective-permute-start(bf16[3,256,256]{2,1,0:T(8,128)(2,1)S(1)} %add_convert_fusion.1), channel_id=1, source_target_pairs={{1,4},{4,1},{5,8},{8,5},{9,12},{12,9},{3,6},{6,3},{7,10},{10,7},{1... | collective-permute-start | bytes 1179656 | tf_op jit(solution)/shard_map/ppermute | solution.py:27
  105.6 7.4 %collective-permute-start.14 = (bf16[3,128,256]{2,1,0:T(8,128)(2,1)S(1)}, bf16[3,128,256]{2,1,0:T(8,128)(2,1)S(1)}, u32[]{:S(2)}, u32[]{:S(2)}) collective-permute-start(bf16[3,128,256]{2,1,0:T(8,128)(2,1)S(1)} %add_convert_fusion.2), channel_id=1, source_target_pairs={{1,4},{4,1},{5,8},{8,5},{9,12},{12,9},{3,6},{6,3},{7,10},{10,7},{1... | collective-permute-start | bytes 589832 | tf_op jit(solution)/shard_map/ppermute | solution.py:27
  109.2 16.1 %collective-permute-start.16 = (bf16[8,256,256]{2,1,0:T(8,128)(2,1)S(1)}, bf16[8,256,256]{2,1,0:T(8,128)(2,1)S(1)}, u32[]{:S(2)}, u32[]{:S(2)}) collective-permute-start(bf16[8,256,256]{2,1,0:T(8,128)(2,1)S(1)} %multiply_convert_fusion), channel_id=1, source_target_pairs={{1,4},{4,1},{5,8},{8,5},{9,12},{12,9},{3,6},{6,3},{7,10},{10,7},{1... | collective-permute-start | bytes 3145736 | tf_op jit(solution)/shard_map/ppermute | solution.py:27
  115.0 10.4 %collective-permute-start.15 = (bf16[8,256,256]{2,1,0:T(8,128)(2,1)S(1)}, bf16[8,256,256]{2,1,0:T(8,128)(2,1)S(1)}, u32[]{:S(2)}, u32[]{:S(2)}) collective-permute-start(bf16[8,256,256]{2,1,0:T(8,128)(2,1)S(1)} %get-tuple-element.80.refs_2_), channel_id=1, source_target_pairs={{0,1},{1,0},{2,3},{3,2},{4,5},{5,4},{6,7},{7,6},{8,9},{9,8},{10,11... | collective-permute-start | bytes 3145736 | tf_op jit(solution)/shard_map/ppermute | solution.py:19
  128.7 16.1 %collective-permute-start.18 = (bf16[8,256,256]{2,1,0:T(8,128)(2,1)S(1)}, bf16[8,256,256]{2,1,0:T(8,128)(2,1)S(1)}, u32[]{:S(2)}, u32[]{:S(2)}) collective-permute-start(bf16[8,256,256]{2,1,0:T(8,128)(2,1)S(1)} %sweep_amplitudes.2.refs_0_), channel_id=1, source_target_pairs={{1,4},{4,1},{5,8},{8,5},{9,12},{12,9},{3,6},{6,3},{7,10},{10,7},{1... | collective-permute-start | bytes 3145736 | tf_op jit(solution)/shard_map/ppermute | solution.py:27
  131.3 13.5 %collective-permute-start.17 = (bf16[8,256,256]{2,1,0:T(8,128)(2,1)S(1)}, bf16[8,256,256]{2,1,0:T(8,128)(2,1)S(1)}, u32[]{:S(2)}, u32[]{:S(2)}) collective-permute-start(bf16[8,256,256]{2,1,0:T(8,128)(2,1)S(1)} %sweep_amplitudes.2.refs_0_), channel_id=1, source_target_pairs={{0,1},{1,0},{2,3},{3,2},{4,5},{5,4},{6,7},{7,6},{8,9},{9,8},{10,11... | collective-permute-start | bytes 3145736 | tf_op jit(solution)/shard_map/ppermute | solution.py:19
  (9 other events, 63.8 us)

commit v5 on v4

--- a/solution.py
+++ b/solution.py
@@ -59,6 +59,7 @@
 
 
 CHUNKS = 2
+FILL = 60 * 10**9
 
 
 def chunk(k, rows):
@@ -356,6 +357,27 @@
     )(at, row_gap, col_gap, inverse, *local, *sent, *others, *got)
 
 
+def energy_kernel(energy_ref, dom_ref, out_ref):
+    dom = dom_ref[...]
+
+    def body(k, total):
+        return jnp.where(dom == k, energy_ref[k], total)
+
+    out_ref[...] = lax.fori_loop(0, energy_ref.shape[0], body, jnp.zeros(dom.shape, F32), unroll=8)
+
+
+def energies_of(energies, dom):
+    return pl.pallas_call(
+        energy_kernel,
+        in_specs=in_smem(1) + in_vmem(1),
+        out_specs=in_vmem(1)[0],
+        out_shape=jax.ShapeDtypeStruct(dom.shape, F32),
+        compiler_params=params(8),
+        cost_estimate=pl.CostEstimate(flops=FILL, bytes_accessed=0, transcendentals=0),
+        name="energies_of",
+    )(energies, dom)
+
+
 def sweep_kernel(patched, at_ref, weight_ref, *refs):
     if patched:
         patch_at_ref, patch_ref, *refs = refs
@@ -414,7 +436,7 @@
     half = jnp.reshape(parity, (1,)).astype(jnp.int32)
     first = lax.dynamic_slice(three_index, (count - 1, (1 - parity) * half_rows, 0), (1, half_rows, cut))[0]
     *sends, last, own_away = send_blocks(1 - half, after(three_index, first), width - cut)
-    from_line = [[line_mate(first), line_mate(sends[0])], *[[line_mate(s)] for s in sends[1:-1]], [line_mate(last)]]
+    from_line = [[line_mate(first), line_mate(sends[0])]]
     from_chip = [chip_mate(s) for s in sends]
 
     def total(terms, *earlier):
@@ -427,54 +449,55 @@
 
     domains, pair_orbs, coupled = lax.optimization_barrier((domains, pair_orbs, coupled, own_away, from_line[0][0]))[:3]
 
-    pairs = lax.dynamic_slice_in_dim(pair_orbs, owner * slots, slots, 0)
-    line_owner = owner - 1 + 2 * parity
-    mate_pairs = lax.dynamic_slice_in_dim(pair_orbs, line_owner * slots, slots, 0)
-    rows, cols = pairs[:, 0], pairs[:, 1]
-    row_dom, col_dom = domains[rows], domains[cols]
-
     def kind_of(other):
         return jnp.where(other == owner, 0, jnp.where(other == chip_owner, 1, 2)).astype(jnp.int32)
 
+    line_owner = owner - 1 + 2 * parity
+    pairs = lax.dynamic_slice_in_dim(after(pair_orbs, own_away), owner * slots, slots, 0)
+    rows, cols = pairs[:, 0], pairs[:, 1]
+    slot_at = jnp.concatenate([kind_of(cols // count), rows % count, cols % count])
     seen = min(3 * count, domains.shape[0])
     window = jnp.clip((owner - 1) * count, 0, domains.shape[0] - seen)
-    listed = jnp.arange(virt_energy.shape[0], dtype=jnp.int32)
-    seen_dom = lax.dynamic_slice_in_dim(domains, window, seen, 0)
-    seen_energy = jnp.sum(jnp.where(seen_dom[:, :, None] == listed, virt_energy, 0.0), axis=-1)
+    seen_dom = lax.dynamic_slice_in_dim(after(domains, own_away), window, seen, 0)
+    seen_energy = energies_of(virt_energy, after(seen_dom, from_line[0][0], slot_at))
+
+    chip_sent, own, block = chip_products(half, after(three_index, seen_energy), from_chip, own_away)
+    local = local_integrals(slot_at, slots, own, chip_sent, chip_mate(chip_sent))
+    local_terms = aux_terms(local)
+    from_line += [[line_mate(s)] for s in sends[1:-1]]
+    domains, pair_orbs, coupled, rows, cols, weights, seen_energy = lax.optimization_barrier(
+        (domains, pair_orbs, coupled, rows, cols, fock_coupling_weight, seen_energy, local, from_line[0][1])
+    )[:7]
+    row_dom, col_dom = domains[rows], domains[cols]
+    source_rows = domains[pair_orbs[coupled, 0]]
+    source_cols = domains[pair_orbs[coupled, 1]]
+    at = (kind_of(coupled // slots) * slots + coupled % slots).reshape(-1)
     seen_gap = seen_energy - lax.dynamic_slice_in_dim(occ_energy, window, seen, 0)[:, None]
     inverse = (jnp.arange(slots) < live_pairs[owner]).astype(F32)[:, None, None] / (
         seen_gap[rows - window][:, :, None] + seen_gap[cols - window][:, None, :]
     )
-    own_gap = lax.dynamic_slice_in_dim(seen_gap, owner * count - window, count, 0)
-    line_gap = lax.dynamic_slice_in_dim(seen_gap, line_owner * count - window, count, 0)
-    row_gap = jnp.broadcast_to(line_gap[:, :, None], (count, width, width))
-    source_rows = domains[pair_orbs[coupled, 0]]
-    source_cols = domains[pair_orbs[coupled, 1]]
-    kind, row, col = kind_of(cols // count), rows % count, cols % count
+    own_gap = lax.dynamic_slice_in_dim(seen_gap, owner * count - window, count, 0)[:, None, :]
+    row_gap = lax.dynamic_slice_in_dim(seen_gap, line_owner * count - window, count, 0)
+    row_gap = jnp.broadcast_to(row_gap[:, :, None], (count, width, width))
+    mate_pairs = lax.dynamic_slice_in_dim(pair_orbs, line_owner * slots, slots, 0)
     inward = (
         (mate_pairs[:, 1] // count == owner)
         & (mate_pairs[:, 0] // count == line_owner)
         & (jnp.arange(slots) < live_pairs[line_owner])
     )
     slot_at = jnp.concatenate(
-        [kind, row, col, inward.astype(jnp.int32), mate_pairs[:, 0] % count, mate_pairs[:, 1] % count]
+        [slot_at, inward.astype(jnp.int32), mate_pairs[:, 0] % count, mate_pairs[:, 1] % count]
     )
-    at = (kind_of(coupled // slots) * slots + coupled % slots).reshape(-1)
-    weights = fock_coupling_weight.reshape(-1)
-
-    three_index, slot_at, at, weights, row_gap, own_gap, inverse, row_dom, col_dom, source_rows, source_cols = (
-        lax.optimization_barrier(
-            (three_index, slot_at, at, weights, row_gap, own_gap[:, None, :], inverse, row_dom, col_dom, source_rows, source_cols)
-        )
-    )
-    chip_sent, own, block = chip_products(half, three_index, from_chip, own_away)
-    local = local_integrals(slot_at, slots, own, chip_sent, chip_mate(chip_sent))
-    local_terms = aux_terms(local)
+    weights = weights.reshape(-1)
+    tables = (row_dom, col_dom, source_rows, source_cols, at, inverse, own_gap, row_gap, slot_at, weights)
+
     sent, terms, sums, got = [], [], [], []
-    earlier = (local,)
+    earlier = tables
     for k in range(len(groups)):
         sent.append(cross_products(k, *earlier))
         terms.append(aux_terms(sent[k]))
+        if k == 0:
+            from_line.append([line_mate(after(last, sent[0]))])
         if k == 1:
             part, other = lax.optimization_barrier((*local_terms, sent[1]))[:2]
             mate_start = (-(part.astype(F32) + other.astype(F32)) * inverse).astype(BF16)

time: 150 us -> 146 us (0.973)
  other arithmetic: 9.48 us -> 5.13 us
  waiting for transfers between devices: 44.5 us -> 41.9 us
  Pallas kernels: 41.5 us -> 44 us
  starting transfers between devices: 36.8 us -> 39.3 us
  local copies, waits for them, and re-layouts: 16.3 us -> 14.8 us
    ppermute x4, waiting for transfers between devices: 8.66 us -> 1.74 us  [aux_terms(): other = lax.ppermute(value, 'aux', [(i, i ^ step) for i in range(count)])]
    ppermute x9, waiting for transfers between devices: 33.3 us -> 38.7 us  [line_mate(): return lax.ppermute(value, LINE, pairs)]
    pallas_call x0 -> x1, Pallas kernels: none -> 3.25 us  [energies_of(): pl.pallas_call(energy_kernel, in_specs=in_smem(1) + in_vmem(1), out_specs...]
    pallas_call x1, Pallas kernels: 14.3 us -> 11.9 us  [chip_products(): pl.pallas_call(functools.partial(chip_kernel, n), in_specs=in_smem(1) + [...]
    reduce_sum x1 -> x0, other arithmetic: 2.23 us -> none  [on_device(): jnp.sum(jnp.where(seen_dom[:, :, None] == listed, virt_energy, 0.0), axis...]
    unnamed x29 -> x28, local copies, waits for them, and re-layouts: 4.46 us -> 5.22 us
  transfers between devices with their start and end apart: 19 -> 19, of which waited for: 8 -> 9; matrix products, arithmetic and copies ran while one was open for 13% -> 8% of each run, Pallas kernels for 23% -> 25%
where the time goes in v5:
time: 146 us
  Pallas kernels  44 us (30%)
  waiting for transfers between devices  41.9 us (29%)
  starting transfers between devices  39.3 us (27%)
  local copies, waits for them, and re-layouts  14.8 us (10%)
  other arithmetic  5.13 us (4%)
    ppermute x9, waiting for transfers between devices, line_mate(): return lax.ppermute(value, LINE, pairs)  38.7 us
    ppermute x9, starting transfers between devices, line_mate(): return lax.ppermute(value, LINE, pairs)  33.3 us
    pallas_call x1, Pallas kernels, chip_products(): pl.pallas_call(functools.partial(chip_kernel, n), in_specs=in_smem(1) + [...  11.9 us
    pallas_call x3, Pallas kernels, line_products(): pl.pallas_call(functools.partial(line_kernel, n), in_specs=in_vmem(1) + [...  11.5 us
    pallas_call x2, Pallas kernels, sweep_amplitudes(): pl.pallas_call(functools.partial(sweep_kernel, bool(patch)), in_specs=in_...  7.71 us
    pallas_call x1, Pallas kernels, send_blocks(): pl.pallas_call(send_kernel, in_specs=in_smem(1) + [anywhere], out_specs=[...  5.75 us
    unnamed x28, local copies, waits for them, and re-layouts  5.22 us
    ppermute x4, starting transfers between devices, aux_terms(): other = lax.ppermute(value, 'aux', [(i, i ^ step) for i in range(count)])  5.1 us
  transfers between devices with their start and end apart: 19, of which 9 were waited for; matrix products, arithmetic and copies ran while one was open for 8% of the time, Pallas kernels for 25%

profile of v5, /device:TPU:1, one launch (start us, length us, event | category | flops | bytes accessed | tf_op | source)
XLA Modules:
  0.0 145.7 jit_solution(11532778418233448753)
XLA Ops:
  0.0 2.5 %dynamic-slice_bitcast_fusion = bf16[5120,128]{1,0:T(8,128)(2,1)} fusion(bf16[3,10240,256]{2,1,0:T(8,128)(2,1)} %blocks_ref.1, s32[]{:T(128)S(6)} %select_n.116), kind=kLoop, calls=%fused_computation.12 | loop fusion | bytes 2621444 | tf_op jit(solution)/shard_map/squeeze | solution.py:437
  2.5 4.6 %collective-permute-start = (bf16[5120,128]{1,0:T(8,128)(2,1)}, bf16[5120,128]{1,0:T(8,128)(2,1)}, u32[]{:S(2)}, u32[]{:S(2)}) collective-permute-start(bf16[5120,128]{1,0:T(8,128)(2,1)} %dynamic-slice_bitcast_fusion), channel_id=1, source_target_pairs={{1,4},{4,1},{5,8},{8,5},{9,12},{12,9},{3,6},{6,3},{7,10},{10,7},{1... | collective-permute-start | bytes 3932168 | tf_op jit(solution)/shard_map/ppermute | solution.py:27
  7.1 5.7 %send_blocks.1 = (bf16[5120,256]{1,0:T(8,128)(2,1)}, bf16[5120,256]{1,0:T(8,128)(2,1)}, bf16[5120,256]{1,0:T(8,128)(2,1)}, bf16[5120,128]{1,0:T(8,128)(2,1)S(1)}, f32[3,256,256]{2,1,0:T(8,128)S(1)}) custom-call(s32[1]{0:T(128)S(6)} %sub.53.half_ref, bf16[3,10240,256]{2,1,0:T(8,128)(2,1)} %blocks_ref.1), custom_call_target="tpu_custom_call" | custom-call | flops 1966080 | bytes 15360 | tf_op jit(solution)/shard_map/send_blocks/pallas_call | solution.py:122
  14.8 3.8 %collective-permute-start.5 = (bf16[5120,256]{1,0:T(8,128)(2,1)}, bf16[5120,256]{1,0:T(8,128)(2,1)}, u32[]{:S(2)}, u32[]{:S(2)}) collective-permute-start(bf16[5120,256]{1,0:T(8,128)(2,1)} %get-tuple-element.58), channel_id=1, source_target_pairs={{1,4},{4,1},{5,8},{8,5},{9,12},{12,9},{3,6},{6,3},{7,10},{10,7},{1... | collective-permute-start | bytes 7864328 | tf_op jit(solution)/shard_map/ppermute | solution.py:27
  19.2 3.5 %collective-permute-done.refs_0_ = bf16[5120,128]{1,0:T(8,128)(2,1)} collective-permute-done((bf16[5120,128]{1,0:T(8,128)(2,1)}, bf16[5120,128]{1,0:T(8,128)(2,1)}, u32[]{:S(2)}, u32[]{:S(2)}) %collective-permute-start) | collective-permute-done | bytes 1310752 | tf_op jit(solution)/shard_map/ppermute | solution.py:27
  22.9 3.2 %energies_of.1 = f32[9,256]{1,0:T(8,128)S(1)} custom-call(f32[1792]{0:T(1024)S(1)} %copy-done.6, s32[9,256]{1,0:T(8,128)S(1)} %constant_dynamic-slice_fusion.3.dom_ref), custom_call_target="tpu_custom_call" | custom-call | flops 60000002048 | tf_op jit(solution)/shard_map/energies_of/pallas_call | solution.py:370
  27.7 11.9 %chip_products.1 = (bf16[3,768,256]{2,1,0:T(8,128)(2,1)}, f32[3,256,256]{2,1,0:T(8,128)S(1)}, bf16[3,5120,256]{2,1,0:T(8,128)(2,1)}) custom-call(s32[1]{0:T(128)} %bitcast.half_ref, bf16[3,10240,256]{2,1,0:T(8,128)(2,1)} %blocks_ref.1, bf16[5120,256]{1,0:T(8,128)(2,1)S(1)} %collective-permute-done.1.refs_0_, ...), custom_call_target="tpu_custom_call" | custom-call | flops 5898240 | bytes 15360 | tf_op jit(solution)/shard_map/chip_products/pallas_call | solution.py:174
  39.8 3.7 %collective-permute-start.7 = (bf16[5120,256]{1,0:T(8,128)(2,1)}, bf16[5120,256]{1,0:T(8,128)(2,1)}, u32[]{:S(2)}, u32[]{:S(2)}) collective-permute-start(bf16[5120,256]{1,0:T(8,128)(2,1)} %get-tuple-element.59), channel_id=1, source_target_pairs={{1,4},{4,1},{5,8},{8,5},{9,12},{12,9},{3,6},{6,3},{7,10},{10,7},{1... | collective-permute-start | bytes 7864328 | tf_op jit(solution)/shard_map/ppermute | solution.py:27
  48.3 2.6 %collective-permute-done.5.refs_1_ = bf16[5120,256]{1,0:T(8,128)(2,1)} collective-permute-done((bf16[5120,256]{1,0:T(8,128)(2,1)}, bf16[5120,256]{1,0:T(8,128)(2,1)}, u32[]{:S(2)}, u32[]{:S(2)}) %collective-permute-start.5) | collective-permute-done | bytes 2621472 | tf_op jit(solution)/shard_map/ppermute | solution.py:27
  58.6 3.2 %copy-done.1 = bf16[3,5120,256]{2,1,0:T(8,128)(2,1)S(1)} copy-done((bf16[3,5120,256]{2,1,0:T(8,128)(2,1)S(1)}, bf16[3,5120,256]{2,1,0:T(8,128)(2,1)}, u32[]{:S(2)}) %copy-start.1) | copy-done | bytes 7864344
  61.8 5.3 %line_products.3.refs_0_ = bf16[3,384,256]{2,1,0:T(8,128)(2,1)S(1)} custom-call(bf16[3,5120,256]{2,1,0:T(8,128)(2,1)S(1)} %copy-done.1, bf16[5120,128]{1,0:T(8,128)(2,1)} %collective-permute-done.refs_0_, bf16[5120,256]{1,0:T(8,128)(2,1)} %collective-permute-done.5.refs_1_), custom_call_target="tpu_custom_call" | custom-call | flops 2949120 | bytes 11520 | tf_op jit(solution)/shard_map/line_products/pallas_call | solution.py:223
  67.1 3.7 %collective-permute-start.8 = (bf16[5120,128]{1,0:T(8,128)(2,1)S(1)}, bf16[5120,128]{1,0:T(8,128)(2,1)S(1)}, u32[]{:S(2)}, u32[]{:S(2)}) collective-permute-start(bf16[5120,128]{1,0:T(8,128)(2,1)S(1)} %copy-done.5), channel_id=1, source_target_pairs={{1,4},{4,1},{5,8},{8,5},{9,12},{12,9},{3,6},{6,3},{7,10},{10,7},{1... | collective-permute-start | bytes 3932168 | tf_op jit(solution)/shard_map/ppermute | solution.py:27
  72.1 6.9 %collective-permute-done.7.refs_0_ = bf16[5120,256]{1,0:T(8,128)(2,1)} collective-permute-done((bf16[5120,256]{1,0:T(8,128)(2,1)}, bf16[5120,256]{1,0:T(8,128)(2,1)}, u32[]{:S(2)}, u32[]{:S(2)}) %collective-permute-start.7) | collective-permute-done | bytes 2621472 | tf_op jit(solution)/shard_map/ppermute | solution.py:27
  79.0 4.3 %line_products.4.refs_1_ = bf16[3,256,256]{2,1,0:T(8,128)(2,1)S(1)} custom-call(bf16[3,5120,256]{2,1,0:T(8,128)(2,1)S(1)} %copy-done.1, bf16[5120,256]{1,0:T(8,128)(2,1)} %collective-permute-done.7.refs_0_), custom_call_target="tpu_custom_call" | custom-call | flops 1966080 | bytes 10240 | tf_op jit(solution)/shard_map/line_products/pallas_call | solution.py:223
  86.5 2.7 %collective-permute-start.12 = (bf16[3,384,256]{2,1,0:T(8,128)(2,1)S(1)}, bf16[3,384,256]{2,1,0:T(8,128)(2,1)S(1)}, u32[]{:S(2)}, u32[]{:S(2)}) collective-permute-start(bf16[3,384,256]{2,1,0:T(8,128)(2,1)S(1)} %add_convert_fusion), channel_id=1, source_target_pairs={{1,4},{4,1},{5,8},{8,5},{9,12},{12,9},{3,6},{6,3},{7,10},{10,7},{1... | collective-permute-start | bytes 1769480 | tf_op jit(solution)/shard_map/ppermute | solution.py:27
  89.8 3.2 %collective-permute-done.8.refs_0_ = bf16[5120,128]{1,0:T(8,128)(2,1)S(1)} collective-permute-done((bf16[5120,128]{1,0:T(8,128)(2,1)S(1)}, bf16[5120,128]{1,0:T(8,128)(2,1)S(1)}, u32[]{:S(2)}, u32[]{:S(2)}) %collective-permute-start.8) | collective-permute-done | bytes 1310752 | tf_op jit(solution)/shard_map/ppermute | solution.py:27
  96.5 3.6 %collective-permute-start.13 = (bf16[3,256,256]{2,1,0:T(8,128)(2,1)S(1)}, bf16[3,256,256]{2,1,0:T(8,128)(2,1)S(1)}, u32[]{:S(2)}, u32[]{:S(2)}) collective-permute-start(bf16[3,256,256]{2,1,0:T(8,128)(2,1)S(1)} %add_convert_fusion.1), channel_id=1, source_target_pairs={{1,4},{4,1},{5,8},{8,5},{9,12},{12,9},{3,6},{6,3},{7,10},{10,7},{1... | collective-permute-start | bytes 1179656 | tf_op jit(solution)/shard_map/ppermute | solution.py:27
  100.2 5.4 %collective-permute-start.14 = (bf16[3,128,256]{2,1,0:T(8,128)(2,1)S(1)}, bf16[3,128,256]{2,1,0:T(8,128)(2,1)S(1)}, u32[]{:S(2)}, u32[]{:S(2)}) collective-permute-start(bf16[3,128,256]{2,1,0:T(8,128)(2,1)S(1)} %add_convert_fusion.2), channel_id=1, source_target_pairs={{1,4},{4,1},{5,8},{8,5},{9,12},{12,9},{3,6},{6,3},{7,10},{10,7},{1... | collective-permute-start | bytes 589832 | tf_op jit(solution)/shard_map/ppermute | solution.py:27
  105.6 2.2 %collective-permute-start.16 = (bf16[8,256,256]{2,1,0:T(8,128)(2,1)S(1)}, bf16[8,256,256]{2,1,0:T(8,128)(2,1)S(1)}, u32[]{:S(2)}, u32[]{:S(2)}) collective-permute-start(bf16[8,256,256]{2,1,0:T(8,128)(2,1)S(1)} %multiply_convert_fusion), channel_id=1, source_target_pairs={{1,4},{4,1},{5,8},{8,5},{9,12},{12,9},{3,6},{6,3},{7,10},{10,7},{1... | collective-permute-start | bytes 3145736 | tf_op jit(solution)/shard_map/ppermute | solution.py:27
  113.1 8.7 %collective-permute-done.16.refs_4_ = bf16[8,256,256]{2,1,0:T(8,128)(2,1)S(1)} collective-permute-done((bf16[8,256,256]{2,1,0:T(8,128)(2,1)S(1)}, bf16[8,256,256]{2,1,0:T(8,128)(2,1)S(1)}, u32[]{:S(2)}, u32[]{:S(2)}) %collective-permute-start.16) | collective-permute-done | bytes 1048608 | tf_op jit(solution)/shard_map/ppermute | solution.py:27
  121.8 3.4 %sweep_amplitudes.2.refs_0_ = bf16[8,256,256]{2,1,0:T(8,128)(2,1)S(1)} custom-call(s32[32]{0:T(128)S(1)} %reshape.63.at_ref, f32[32]{0:T(128)S(1)} %reshape.64.weight_ref, s32[48]{0:T(128)S(1)} %concatenate.14.at_ref.refs_0_, bf16[8,256,256]{2,1,0:T(8,128)(2,1)S(1)} %get-tuple-element.85.refs_1_, bf16[8,256,256]{2,1,0:T(8,128)(2,1)S(1)} %get-tuple-element.86.refs_2_, ...), custom_call_target="tpu_custom_call" | custom-call | flops 2097152 | bytes 16384 | tf_op jit(solution)/shard_map/sweep_amplitudes/pallas_call | solution.py:413
  125.3 3.6 %collective-permute-start.18 = (bf16[8,256,256]{2,1,0:T(8,128)(2,1)S(1)}, bf16[8,256,256]{2,1,0:T(8,128)(2,1)S(1)}, u32[]{:S(2)}, u32[]{:S(2)}) collective-permute-start(bf16[8,256,256]{2,1,0:T(8,128)(2,1)S(1)} %sweep_amplitudes.2.refs_0_), channel_id=1, source_target_pairs={{1,4},{4,1},{5,8},{8,5},{9,12},{12,9},{3,6},{6,3},{7,10},{10,7},{1... | collective-permute-start | bytes 3145736 | tf_op jit(solution)/shard_map/ppermute | solution.py:27
  128.9 12.5 %collective-permute-done.18.refs_2_ = bf16[8,256,256]{2,1,0:T(8,128)(2,1)S(1)} collective-permute-done((bf16[8,256,256]{2,1,0:T(8,128)(2,1)S(1)}, bf16[8,256,256]{2,1,0:T(8,128)(2,1)S(1)}, u32[]{:S(2)}, u32[]{:S(2)}) %collective-permute-start.18) | collective-permute-done | bytes 1048608 | tf_op jit(solution)/shard_map/ppermute | solution.py:27
  141.4 4.3 %sweep_amplitudes.3 = bf16[8,256,256]{2,1,0:T(8,128)(2,1)} custom-call(s32[32]{0:T(128)S(1)} %reshape.63.at_ref, f32[32]{0:T(128)S(1)} %reshape.64.weight_ref, bf16[8,256,256]{2,1,0:T(8,128)(2,1)S(1)} %sweep_amplitudes.2.refs_0_, bf16[8,256,256]{2,1,0:T(8,128)(2,1)S(1)} %collective-permute-done.17.refs_1_, ...), custom_call_target="tpu_custom_call" | custom-call | flops 2097152 | bytes 16384 | tf_op jit(solution)/shard_map/sweep_amplitudes/pallas_call | solution.py:413
  (109 shorter events, 30.5 us)
Async XLA Ops:
  0.0 22.7 %copy-start = (s32[24,256]{1,0:T(8,128)S(1)}, s32[24,256]{1,0:T(8,128)}, u32[]{:S(2)}) copy-start(s32[24,256]{1,0:T(8,128)} %param.11) | copy-start | bytes 73732
  2.5 20.2 %collective-permute-start = (bf16[5120,128]{1,0:T(8,128)(2,1)}, bf16[5120,128]{1,0:T(8,128)(2,1)}, u32[]{:S(2)}, u32[]{:S(2)}) collective-permute-start(bf16[5120,128]{1,0:T(8,128)(2,1)} %dynamic-slice_bitcast_fusion), channel_id=1, source_target_pairs={{1,4},{4,1},{5,8},{8,5},{9,12},{12,9},{3,6},{6,3},{7,10},{10,7},{1... | collective-permute-start | bytes 3932168 | tf_op jit(solution)/shard_map/ppermute | solution.py:27
  14.8 11.3 %collective-permute-start.1 = (bf16[5120,256]{1,0:T(8,128)(2,1)}, bf16[5120,256]{1,0:T(8,128)(2,1)S(1)}, u32[]{:S(2)}, u32[]{:S(2)}) collective-permute-start(bf16[5120,256]{1,0:T(8,128)(2,1)} %get-tuple-element.58), channel_id=1, source_target_pairs={{0,1},{1,0},{2,3},{3,2},{4,5},{5,4},{6,7},{7,6},{8,9},{9,8},{10,11... | collective-permute-start | bytes 7864328 | tf_op jit(solution)/shard_map/ppermute | solution.py:19
  14.8 36.1 %collective-permute-start.5 = (bf16[5120,256]{1,0:T(8,128)(2,1)}, bf16[5120,256]{1,0:T(8,128)(2,1)}, u32[]{:S(2)}, u32[]{:S(2)}) collective-permute-start(bf16[5120,256]{1,0:T(8,128)(2,1)} %get-tuple-element.58), channel_id=1, source_target_pairs={{1,4},{4,1},{5,8},{8,5},{9,12},{12,9},{3,6},{6,3},{7,10},{10,7},{1... | collective-permute-start | bytes 7864328 | tf_op jit(solution)/shard_map/ppermute | solution.py:27
  18.6 7.6 %collective-permute-start.2 = (bf16[5120,256]{1,0:T(8,128)(2,1)}, bf16[5120,256]{1,0:T(8,128)(2,1)}, u32[]{:S(2)}, u32[]{:S(2)}) collective-permute-start(bf16[5120,256]{1,0:T(8,128)(2,1)} %get-tuple-element.59), channel_id=1, source_target_pairs={{0,1},{1,0},{2,3},{3,2},{4,5},{5,4},{6,7},{7,6},{8,9},{9,8},{10,11... | collective-permute-start | bytes 7864328 | tf_op jit(solution)/shard_map/ppermute | solution.py:19
  18.7 9.0 %collective-permute-start.3 = (bf16[5120,256]{1,0:T(8,128)(2,1)}, bf16[5120,256]{1,0:T(8,128)(2,1)}, u32[]{:S(2)}, u32[]{:S(2)}) collective-permute-start(bf16[5120,256]{1,0:T(8,128)(2,1)} %get-tuple-element.60), channel_id=1, source_target_pairs={{0,1},{1,0},{2,3},{3,2},{4,5},{5,4},{6,7},{7,6},{8,9},{9,8},{10,11... | collective-permute-start | bytes 7864328 | tf_op jit(solution)/shard_map/ppermute | solution.py:19
  26.1 17.4 %copy-start.11 = (f32[24]{0:T(128)S(1)}, f32[24]{0:T(128)}, u32[]{:S(2)}) copy-start(f32[24]{0:T(128)} %param.14) | copy-start | bytes 292
  26.1 17.4 %copy-start.9 = (s32[8]{0:T(128)S(1)}, s32[8]{0:T(128)}, u32[]{:S(2)}) copy-start(s32[8]{0:T(128)} %param.10) | copy-start | bytes 100
  39.6 5.3 %collective-permute-start.4 = (bf16[3,768,256]{2,1,0:T(8,128)(2,1)}, bf16[3,768,256]{2,1,0:T(8,128)(2,1)S(1)}, u32[]{:S(2)}, u32[]{:S(2)}) collective-permute-start(bf16[3,768,256]{2,1,0:T(8,128)(2,1)} %get-tuple-element.62.sent_ref), channel_id=1, source_target_pairs={{0,1},{1,0},{2,3},{3,2},{4,5},{5,4},{6,7},{7,6},{8,9},{9,8},{10,11... | collective-permute-start | bytes 3538952 | tf_op jit(solution)/shard_map/ppermute | solution.py:19
  39.8 39.2 %collective-permute-start.7 = (bf16[5120,256]{1,0:T(8,128)(2,1)}, bf16[5120,256]{1,0:T(8,128)(2,1)}, u32[]{:S(2)}, u32[]{:S(2)}) collective-permute-start(bf16[5120,256]{1,0:T(8,128)(2,1)} %get-tuple-element.59), channel_id=1, source_target_pairs={{1,4},{4,1},{5,8},{8,5},{9,12},{12,9},{3,6},{6,3},{7,10},{10,7},{1... | collective-permute-start | bytes 7864328 | tf_op jit(solution)/shard_map/ppermute | solution.py:27
  47.0 32.0 %collective-permute-start.6 = (bf16[8,256,256]{2,1,0:T(8,128)(2,1)S(1)}, bf16[8,256,256]{2,1,0:T(8,128)(2,1)S(1)}, u32[]{:S(2)}, u32[]{:S(2)}) collective-permute-start(bf16[8,256,256]{2,1,0:T(8,128)(2,1)S(1)} %local_integrals.1.part_ref), channel_id=1, source_target_pairs={{0,2},{2,0},{1,3},{3,1},{4,6},{6,4},{5,7},{7,5},{8,10},{10,8},{9,1... | collective-permute-start | bytes 3145736 | tf_op jit(solution)/shard_map/ppermute | solution.py:34
  67.1 26.0 %slice-start = ((s8[7864320]{0:T(1024)(128)(4,1)}), s8[4194304]{0:T(1024)(128)(4,1)S(1)}, s32[]{:S(2)}) async-start(s8[7864320]{0:T(1024)(128)(4,1)} %bitcast.41), calls=%async_computation | async-start | bytes 8388608
  67.1 26.0 %slice-start.1 = ((s8[7864320]{0:T(1024)(128)(4,1)}), s8[3670016]{0:T(1024)(128)(4,1)S(1)}, s32[]{:S(2)}) async-start(s8[7864320]{0:T(1024)(128)(4,1)} %bitcast.41), calls=%async_computation.1 | async-start | bytes 7340032
  67.1 26.0 %collective-permute-start.8 = (bf16[5120,128]{1,0:T(8,128)(2,1)S(1)}, bf16[5120,128]{1,0:T(8,128)(2,1)S(1)}, u32[]{:S(2)}, u32[]{:S(2)}) collective-permute-start(bf16[5120,128]{1,0:T(8,128)(2,1)S(1)} %copy-done.5), channel_id=1, source_target_pairs={{1,4},{4,1},{5,8},{8,5},{9,12},{12,9},{3,6},{6,3},{7,10},{10,7},{1... | collective-permute-start | bytes 3932168 | tf_op jit(solution)/shard_map/ppermute | solution.py:27
  70.8 15.5 %collective-permute-start.9 = (bf16[3,384,256]{2,1,0:T(8,128)(2,1)S(1)}, bf16[3,384,256]{2,1,0:T(8,128)(2,1)S(1)}, u32[]{:S(2)}, u32[]{:S(2)}) collective-permute-start(bf16[3,384,256]{2,1,0:T(8,128)(2,1)S(1)} %line_products.3.refs_0_), channel_id=1, source_target_pairs={{0,2},{2,0},{1,3},{3,1},{4,6},{6,4},{5,7},{7,5},{8,10},{10,8},{9,1... | collective-permute-start | bytes 1769480 | tf_op jit(solution)/shard_map/ppermute | solution.py:34
  83.3 13.1 %collective-permute-start.10 = (bf16[3,256,256]{2,1,0:T(8,128)(2,1)S(1)}, bf16[3,256,256]{2,1,0:T(8,128)(2,1)S(1)}, u32[]{:S(2)}, u32[]{:S(2)}) collective-permute-start(bf16[3,256,256]{2,1,0:T(8,128)(2,1)S(1)} %line_products.4.refs_1_), channel_id=1, source_target_pairs={{0,2},{2,0},{1,3},{3,1},{4,6},{6,4},{5,7},{7,5},{8,10},{10,8},{9,1... | collective-permute-start | bytes 1179656 | tf_op jit(solution)/shard_map/ppermute | solution.py:34
  86.5 13.7 %collective-permute-start.12 = (bf16[3,384,256]{2,1,0:T(8,128)(2,1)S(1)}, bf16[3,384,256]{2,1,0:T(8,128)(2,1)S(1)}, u32[]{:S(2)}, u32[]{:S(2)}) collective-permute-start(bf16[3,384,256]{2,1,0:T(8,128)(2,1)S(1)} %add_convert_fusion), channel_id=1, source_target_pairs={{1,4},{4,1},{5,8},{8,5},{9,12},{12,9},{3,6},{6,3},{7,10},{10,7},{1... | collective-permute-start | bytes 1769480 | tf_op jit(solution)/shard_map/ppermute | solution.py:27
  95.1 5.0 %collective-permute-start.11 = (bf16[3,128,256]{2,1,0:T(8,128)(2,1)S(1)}, bf16[3,128,256]{2,1,0:T(8,128)(2,1)S(1)}, u32[]{:S(2)}, u32[]{:S(2)}) collective-permute-start(bf16[3,128,256]{2,1,0:T(8,128)(2,1)S(1)} %line_products.5.refs_2_), channel_id=1, source_target_pairs={{0,2},{2,0},{1,3},{3,1},{4,6},{6,4},{5,7},{7,5},{8,10},{10,8},{9,1... | collective-permute-start | bytes 589832 | tf_op jit(solution)/shard_map/ppermute | solution.py:34
  96.5 12.5 %collective-permute-start.13 = (bf16[3,256,256]{2,1,0:T(8,128)(2,1)S(1)}, bf16[3,256,256]{2,1,0:T(8,128)(2,1)S(1)}, u32[]{:S(2)}, u32[]{:S(2)}) collective-permute-start(bf16[3,256,256]{2,1,0:T(8,128)(2,1)S(1)} %add_convert_fusion.1), channel_id=1, source_target_pairs={{1,4},{4,1},{5,8},{8,5},{9,12},{12,9},{3,6},{6,3},{7,10},{10,7},{1... | collective-permute-start | bytes 1179656 | tf_op jit(solution)/shard_map/ppermute | solution.py:27
  100.2 8.8 %collective-permute-start.14 = (bf16[3,128,256]{2,1,0:T(8,128)(2,1)S(1)}, bf16[3,128,256]{2,1,0:T(8,128)(2,1)S(1)}, u32[]{:S(2)}, u32[]{:S(2)}) collective-permute-start(bf16[3,128,256]{2,1,0:T(8,128)(2,1)S(1)} %add_convert_fusion.2), channel_id=1, source_target_pairs={{1,4},{4,1},{5,8},{8,5},{9,12},{12,9},{3,6},{6,3},{7,10},{10,7},{1... | collective-permute-start | bytes 589832 | tf_op jit(solution)/shard_map/ppermute | solution.py:27
  105.6 16.1 %collective-permute-start.16 = (bf16[8,256,256]{2,1,0:T(8,128)(2,1)S(1)}, bf16[8,256,256]{2,1,0:T(8,128)(2,1)S(1)}, u32[]{:S(2)}, u32[]{:S(2)}) collective-permute-start(bf16[8,256,256]{2,1,0:T(8,128)(2,1)S(1)} %multiply_convert_fusion), channel_id=1, source_target_pairs={{1,4},{4,1},{5,8},{8,5},{9,12},{12,9},{3,6},{6,3},{7,10},{10,7},{1... | collective-permute-start | bytes 3145736 | tf_op jit(solution)/shard_map/ppermute | solution.py:27
  110.7 11.1 %collective-permute-start.15 = (bf16[8,256,256]{2,1,0:T(8,128)(2,1)S(1)}, bf16[8,256,256]{2,1,0:T(8,128)(2,1)S(1)}, u32[]{:S(2)}, u32[]{:S(2)}) collective-permute-start(bf16[8,256,256]{2,1,0:T(8,128)(2,1)S(1)} %get-tuple-element.86.refs_2_), channel_id=1, source_target_pairs={{0,1},{1,0},{2,3},{3,2},{4,5},{5,4},{6,7},{7,6},{8,9},{9,8},{10,11... | collective-permute-start | bytes 3145736 | tf_op jit(solution)/shard_map/ppermute | solution.py:19
  125.2 3.7 %collective-permute-start.17 = (bf16[8,256,256]{2,1,0:T(8,128)(2,1)S(1)}, bf16[8,256,256]{2,1,0:T(8,128)(2,1)S(1)}, u32[]{:S(2)}, u32[]{:S(2)}) collective-permute-start(bf16[8,256,256]{2,1,0:T(8,128)(2,1)S(1)} %sweep_amplitudes.2.refs_0_), channel_id=1, source_target_pairs={{0,1},{1,0},{2,3},{3,2},{4,5},{5,4},{6,7},{7,6},{8,9},{9,8},{10,11... | collective-permute-start | bytes 3145736 | tf_op jit(solution)/shard_map/ppermute | solution.py:19
  125.3 16.1 %collective-permute-start.18 = (bf16[8,256,256]{2,1,0:T(8,128)(2,1)S(1)}, bf16[8,256,256]{2,1,0:T(8,128)(2,1)S(1)}, u32[]{:S(2)}, u32[]{:S(2)}) collective-permute-start(bf16[8,256,256]{2,1,0:T(8,128)(2,1)S(1)} %sweep_amplitudes.2.refs_0_), channel_id=1, source_target_pairs={{1,4},{4,1},{5,8},{8,5},{9,12},{12,9},{3,6},{6,3},{7,10},{10,7},{1... | collective-permute-start | bytes 3145736 | tf_op jit(solution)/shard_map/ppermute | solution.py:27
  (9 other events, 59.0 us)

commit v6 on v5

--- a/solution.py
+++ b/solution.py
@@ -378,48 +378,93 @@
     )(energies, dom)
 
 
-def sweep_kernel(patched, at_ref, weight_ref, *refs):
-    if patched:
-        patch_at_ref, patch_ref, *refs = refs
-    own_ref, chip_ref, line_ref, rows_ref, cols_ref, inverse_ref, base_ref, out_ref, held_ref = refs
+def near_kernel(at_ref, weight_ref, *refs):
+    *parts, rows_ref, cols_ref, inverse_ref, base_ref, out_ref, held_ref = refs
     slots, neighbours = rows_ref.shape[:2]
-
-    held_ref[:slots] = own_ref[...]
-    held_ref[slots : 2 * slots] = chip_ref[...]
-    held_ref[2 * slots :] = line_ref[...]
-    if patched:
-
-        def patch(slot, carry):
-            @pl.when(patch_at_ref[3 * slots + slot] == 1)
-            def _():
-                held_ref[2 * slots + slot] = patch_ref[slot]
-
-            return carry
-
-        lax.fori_loop(0, slots, patch, 0)
+    at = 0
+    for part in parts:
+        held_ref[at : at + part.shape[0]] = part[...]
+        at += part.shape[0]
     for slot in range(slots):
         total = None
         for n in range(neighbours):
-            source = held_ref[at_ref[slot * neighbours + n]]
+            at = at_ref[slot * neighbours + n]
+            near = at < 2 * slots
+            source = held_ref[jnp.where(near, at, 0)]
+            weight = jnp.where(near, weight_ref[slot * neighbours + n], 0.0)
             selected = jnp.dot(rows_ref[slot, n], source, preferred_element_type=F32).astype(BF16)
-            term = weight_ref[slot * neighbours + n] * jnp.dot(selected, cols_ref[slot, n], preferred_element_type=F32)
+            term = weight * jnp.dot(selected, cols_ref[slot, n], preferred_element_type=F32)
             total = term if total is None else total + term
-        out_ref[slot] = (base_ref[slot] + total * inverse_ref[slot]).astype(out_ref.dtype)
-
-
-def sweep_amplitudes(at, weights, own, chip, line, row_match, col_match, base, inverse, patch=()):
-    slots, width, _ = own.shape
+        out_ref[slot] = base_ref[slot] + total * inverse_ref[slot]
+
+
+def near_sweep(at, weights, parts, row_match, col_match, base, inverse):
+    slots, width, _ = base.shape
     neighbours = row_match.shape[1]
     return pl.pallas_call(
-        functools.partial(sweep_kernel, bool(patch)),
-        in_specs=in_smem(2 + len(patch[:1])) + in_vmem(7 + len(patch[1:])),
+        near_kernel,
+        in_specs=in_smem(2) + in_vmem(4 + len(parts)),
+        out_specs=in_vmem(1)[0],
+        out_shape=jax.ShapeDtypeStruct((slots, width, width), F32),
+        scratch_shapes=[pltpu.VMEM((2 * slots, width, width), BF16)],
+        compiler_params=params(8),
+        cost_estimate=cost(4 * slots * neighbours * width**3, 16 * MIB),
+        name="near_sweep",
+    )(at, weights, *parts, row_match, col_match, inverse, base)
+
+
+GROUP = 4
+
+
+def far_kernel(patched, at_ref, weight_ref, *refs):
+    if patched:
+        patch_at_ref, patch_ref, *refs = refs
+    line_ref, rows_ref, cols_ref, inverse_ref, start_ref, out_ref, total_ref, list_ref = refs
+    slots, neighbours = rows_ref.shape[:2]
+    total_ref[...] = start_ref[...]
+
+    def enlist(k, found):
+        list_ref[found] = k
+        return found + jnp.where(at_ref[k] >= 2 * slots, 1, 0)
+
+    found = lax.fori_loop(0, slots * neighbours, enlist, 0)
+
+    def product(k):
+        slot, n = k // neighbours, k % neighbours
+        mate_slot = at_ref[k] - 2 * slots
+        source = line_ref[mate_slot]
+        if patched:
+            source = jnp.where(patch_at_ref[3 * slots + mate_slot] == 1, patch_ref[mate_slot], source)
+        selected = jnp.dot(rows_ref[slot, n], source, preferred_element_type=F32).astype(BF16)
+        return jnp.dot(selected, cols_ref[slot, n], preferred_element_type=F32)
+
+    def body(step, carry):
+        first = step * GROUP
+        listed = [list_ref[jnp.minimum(first + g, found - 1)] for g in range(GROUP)]
+        products = [product(k) for k in listed]
+        for g, k in enumerate(listed):
+            slot = k // neighbours
+            weight = jnp.where(first + g < found, weight_ref[k], 0.0)
+            total_ref[slot] += weight * products[g] * inverse_ref[slot]
+        return carry
+
+    lax.fori_loop(0, (found + GROUP - 1) // GROUP, body, 0)
+    out_ref[...] = total_ref[...].astype(out_ref.dtype)
+
+
+def far_sweep(at, weights, line, row_match, col_match, inverse, start, patch):
+    slots, width, _ = line.shape
+    neighbours = row_match.shape[1]
+    return pl.pallas_call(
+        functools.partial(far_kernel, bool(patch)),
+        in_specs=in_smem(2 + len(patch[:1])) + in_vmem(5 + len(patch[1:])),
         out_specs=in_vmem(1)[0],
         out_shape=jax.ShapeDtypeStruct((slots, width, width), BF16),
-        scratch_shapes=[pltpu.VMEM((3 * slots, width, width), BF16)],
+        scratch_shapes=[pltpu.VMEM((slots, width, width), F32), pltpu.SMEM((slots * neighbours + 1,), jnp.int32)],
         compiler_params=params(8),
         cost_estimate=cost(4 * slots * neighbours * width**3, 16 * MIB),
-        name="sweep_amplitudes",
-    )(at, weights, *patch, own, chip, line, row_match, col_match, inverse, base)
+        name="far_sweep",
+    )(at, weights, *patch, line, row_match, col_match, inverse, start)
 
 
 def on_device(three_index, pair_orbs, live_pairs, domains, coupled, fock_coupling_weight, occ_energy, virt_energy):
@@ -518,10 +563,11 @@
     row_match = (row_dom[:, None, :, None] == source_rows[:, :, None, :]).astype(BF16)
     col_match = (source_cols[:, :, :, None] == col_dom[:, None, None, :]).astype(BF16)
     for sweep in range(ITERS):
-        from_line, patches = (line_mate(rounded), ()) if sweep else (from_mate, (slot_at, patch))
-        rounded = sweep_amplitudes(
-            at, weights, rounded, chip_mate(rounded), from_line, row_match, col_match, base, inverse, patches
-        )
+        from_mate, patches = (line_mate(rounded), ()) if sweep else (from_mate, (slot_at, patch))
+        cuts = (0, slots // 2, slots)
+        chip = [chip_mate(rounded[i:j]) for i, j in zip(cuts[:-1], cuts[1:])]
+        near = near_sweep(at, weights, [rounded, *chip], row_match, col_match, base, inverse)
+        rounded = far_sweep(at, weights, after(from_mate, near), row_match, col_match, inverse, near, patches)
     return rounded
 
 

time: 146 us -> 145 us (level)
  waiting for transfers between devices: 41.9 us -> 34.6 us
  Pallas kernels: 44 us -> 49.9 us
    ppermute x9, waiting for transfers between devices: 38.7 us -> 29.3 us  [line_mate(): return lax.ppermute(value, LINE, pairs)]
    pallas_call x2 -> x4, Pallas kernels: 7.71 us -> 13.1 us  [the longest x2 6.57 us: near_sweep(): pl.pallas_call(near_kernel, in_specs=in_smem(2) + in_vmem(4 + len(parts))...]
    ppermute x6 -> x8, waiting for transfers between devices: 1.5 us -> 3.65 us  [chip_mate(): return lax.ppermute(value, 'occ', [(0, 1), (1, 0)])]
  transfers between devices with their start and end apart: 19 -> 21, of which waited for: 9 -> 11; matrix products, arithmetic and copies ran while one was open for 8% -> 8% of each run, Pallas kernels for 25% -> 30%
where the time goes in v6:
time: 145 us; the launch traced here: 144 us
  Pallas kernels  49.9 us (34%)
  starting transfers between devices  39.4 us (27%)
  waiting for transfers between devices  34.6 us (24%)
  local copies, waits for them, and re-layouts  14.9 us (10%)
  other arithmetic  5 us (3%)
    ppermute x9, starting transfers between devices, line_mate(): return lax.ppermute(value, LINE, pairs)  32.4 us
    ppermute x9, waiting for transfers between devices, line_mate(): return lax.ppermute(value, LINE, pairs)  29.3 us
    pallas_call x1, Pallas kernels, chip_products(): pl.pallas_call(functools.partial(chip_kernel, n), in_specs=in_smem(1) + [...  11.9 us
    pallas_call x3, Pallas kernels, line_products(): pl.pallas_call(functools.partial(line_kernel, n), in_specs=in_vmem(1) + [...  11.5 us
    pallas_call x2, Pallas kernels, near_sweep(): pl.pallas_call(near_kernel, in_specs=in_smem(2) + in_vmem(4 + len(parts))...  6.57 us
    pallas_call x2, Pallas kernels, far_sweep(): pl.pallas_call(functools.partial(far_kernel, bool(patch)), in_specs=in_sm...  6.48 us
    pallas_call x1, Pallas kernels, send_blocks(): pl.pallas_call(send_kernel, in_specs=in_smem(1) + [anywhere], out_specs=[...  5.73 us
    unnamed x28, local copies, waits for them, and re-layouts  5.24 us
  transfers between devices with their start and end apart: 21, of which 11 were waited for; matrix products, arithmetic and copies ran while one was open for 8% of the time, Pallas kernels for 30%

profile of v6, /device:TPU:1, one launch (start us, length us, event | category | flops | bytes accessed | tf_op | source)
XLA Modules:
  0.0 144.4 jit_solution(12564045208534509468)
XLA Ops:
  2.5 4.6 %collective-permute-start = (bf16[5120,128]{1,0:T(8,128)(2,1)}, bf16[5120,128]{1,0:T(8,128)(2,1)}, u32[]{:S(2)}, u32[]{:S(2)}) collective-permute-start(bf16[5120,128]{1,0:T(8,128)(2,1)} %dynamic-slice_bitcast_fusion), channel_id=1, source_target_pairs={{1,4},{4,1},{5,8},{8,5},{9,12},{12,9},{3,6},{6,3},{7,10},{10,7},{1... | collective-permute-start | bytes 3932168 | tf_op jit(solution)/shard_map/ppermute | solution.py:27
  7.1 5.7 %send_blocks.1 = (bf16[5120,256]{1,0:T(8,128)(2,1)}, bf16[5120,256]{1,0:T(8,128)(2,1)}, bf16[5120,256]{1,0:T(8,128)(2,1)}, bf16[5120,128]{1,0:T(8,128)(2,1)S(1)}, f32[3,256,256]{2,1,0:T(8,128)S(1)}) custom-call(s32[1]{0:T(128)S(6)} %sub.53.half_ref, bf16[3,10240,256]{2,1,0:T(8,128)(2,1)} %blocks_ref.1), custom_call_target="tpu_custom_call" | custom-call | flops 1966080 | bytes 15360 | tf_op jit(solution)/shard_map/send_blocks/pallas_call | solution.py:122
  14.8 3.8 %collective-permute-start.5 = (bf16[5120,256]{1,0:T(8,128)(2,1)}, bf16[5120,256]{1,0:T(8,128)(2,1)}, u32[]{:S(2)}, u32[]{:S(2)}) collective-permute-start(bf16[5120,256]{1,0:T(8,128)(2,1)} %get-tuple-element.60), channel_id=1, source_target_pairs={{1,4},{4,1},{5,8},{8,5},{9,12},{12,9},{3,6},{6,3},{7,10},{10,7},{1... | collective-permute-start | bytes 7864328 | tf_op jit(solution)/shard_map/ppermute | solution.py:27
  19.2 3.5 %collective-permute-done.refs_0_ = bf16[5120,128]{1,0:T(8,128)(2,1)} collective-permute-done((bf16[5120,128]{1,0:T(8,128)(2,1)}, bf16[5120,128]{1,0:T(8,128)(2,1)}, u32[]{:S(2)}, u32[]{:S(2)}) %collective-permute-start) | collective-permute-done | bytes 1310752 | tf_op jit(solution)/shard_map/ppermute | solution.py:27
  22.9 3.2 %energies_of.1 = f32[9,256]{1,0:T(8,128)S(1)} custom-call(f32[1792]{0:T(1024)S(1)} %copy-done.6, s32[9,256]{1,0:T(8,128)S(1)} %constant_dynamic-slice_fusion.3.dom_ref), custom_call_target="tpu_custom_call" | custom-call | flops 60000002048 | tf_op jit(solution)/shard_map/energies_of/pallas_call | solution.py:370
  27.7 11.9 %chip_products.1 = (bf16[3,768,256]{2,1,0:T(8,128)(2,1)}, f32[3,256,256]{2,1,0:T(8,128)S(1)}, bf16[3,5120,256]{2,1,0:T(8,128)(2,1)}) custom-call(s32[1]{0:T(128)} %bitcast.half_ref, bf16[3,10240,256]{2,1,0:T(8,128)(2,1)} %blocks_ref.1, bf16[5120,256]{1,0:T(8,128)(2,1)S(1)} %collective-permute-done.1.refs_0_, ...), custom_call_target="tpu_custom_call" | custom-call | flops 5898240 | bytes 15360 | tf_op jit(solution)/shard_map/chip_products/pallas_call | solution.py:174
  39.8 3.7 %collective-permute-start.7 = (bf16[5120,256]{1,0:T(8,128)(2,1)}, bf16[5120,256]{1,0:T(8,128)(2,1)}, u32[]{:S(2)}, u32[]{:S(2)}) collective-permute-start(bf16[5120,256]{1,0:T(8,128)(2,1)} %get-tuple-element.61), channel_id=1, source_target_pairs={{1,4},{4,1},{5,8},{8,5},{9,12},{12,9},{3,6},{6,3},{7,10},{10,7},{1... | collective-permute-start | bytes 7864328 | tf_op jit(solution)/shard_map/ppermute | solution.py:27
  48.0 2.9 %collective-permute-done.5.refs_1_ = bf16[5120,256]{1,0:T(8,128)(2,1)} collective-permute-done((bf16[5120,256]{1,0:T(8,128)(2,1)}, bf16[5120,256]{1,0:T(8,128)(2,1)}, u32[]{:S(2)}, u32[]{:S(2)}) %collective-permute-start.5) | collective-permute-done | bytes 2621472 | tf_op jit(solution)/shard_map/ppermute | solution.py:27
  58.5 3.2 %copy-done.1 = bf16[3,5120,256]{2,1,0:T(8,128)(2,1)S(1)} copy-done((bf16[3,5120,256]{2,1,0:T(8,128)(2,1)S(1)}, bf16[3,5120,256]{2,1,0:T(8,128)(2,1)}, u32[]{:S(2)}) %copy-start.1) | copy-done | bytes 7864344
  61.7 5.3 %line_products.3.refs_0_ = bf16[3,384,256]{2,1,0:T(8,128)(2,1)S(1)} custom-call(bf16[3,5120,256]{2,1,0:T(8,128)(2,1)S(1)} %copy-done.1, bf16[5120,128]{1,0:T(8,128)(2,1)} %collective-permute-done.refs_0_, bf16[5120,256]{1,0:T(8,128)(2,1)} %collective-permute-done.5.refs_1_), custom_call_target="tpu_custom_call" | custom-call | flops 2949120 | bytes 11520 | tf_op jit(solution)/shard_map/line_products/pallas_call | solution.py:223
  67.0 3.7 %collective-permute-start.8 = (bf16[5120,128]{1,0:T(8,128)(2,1)S(1)}, bf16[5120,128]{1,0:T(8,128)(2,1)S(1)}, u32[]{:S(2)}, u32[]{:S(2)}) collective-permute-start(bf16[5120,128]{1,0:T(8,128)(2,1)S(1)} %copy-done.5), channel_id=1, source_target_pairs={{1,4},{4,1},{5,8},{8,5},{9,12},{12,9},{3,6},{6,3},{7,10},{10,7},{1... | collective-permute-start | bytes 3932168 | tf_op jit(solution)/shard_map/ppermute | solution.py:27
  72.0 7.0 %collective-permute-done.7.refs_0_ = bf16[5120,256]{1,0:T(8,128)(2,1)} collective-permute-done((bf16[5120,256]{1,0:T(8,128)(2,1)}, bf16[5120,256]{1,0:T(8,128)(2,1)}, u32[]{:S(2)}, u32[]{:S(2)}) %collective-permute-start.7) | collective-permute-done | bytes 2621472 | tf_op jit(solution)/shard_map/ppermute | solution.py:27
  79.0 4.3 %line_products.4.refs_1_ = bf16[3,256,256]{2,1,0:T(8,128)(2,1)S(1)} custom-call(bf16[3,5120,256]{2,1,0:T(8,128)(2,1)S(1)} %copy-done.1, bf16[5120,256]{1,0:T(8,128)(2,1)} %collective-permute-done.7.refs_0_), custom_call_target="tpu_custom_call" | custom-call | flops 1966080 | bytes 10240 | tf_op jit(solution)/shard_map/line_products/pallas_call | solution.py:223
  86.4 2.7 %collective-permute-start.12 = (bf16[3,384,256]{2,1,0:T(8,128)(2,1)S(1)}, bf16[3,384,256]{2,1,0:T(8,128)(2,1)S(1)}, u32[]{:S(2)}, u32[]{:S(2)}) collective-permute-start(bf16[3,384,256]{2,1,0:T(8,128)(2,1)S(1)} %add_convert_fusion), channel_id=1, source_target_pairs={{1,4},{4,1},{5,8},{8,5},{9,12},{12,9},{3,6},{6,3},{7,10},{10,7},{1... | collective-permute-start | bytes 1769480 | tf_op jit(solution)/shard_map/ppermute | solution.py:27
  89.7 3.3 %collective-permute-done.8.refs_0_ = bf16[5120,128]{1,0:T(8,128)(2,1)S(1)} collective-permute-done((bf16[5120,128]{1,0:T(8,128)(2,1)S(1)}, bf16[5120,128]{1,0:T(8,128)(2,1)S(1)}, u32[]{:S(2)}, u32[]{:S(2)}) %collective-permute-start.8) | collective-permute-done | bytes 1310752 | tf_op jit(solution)/shard_map/ppermute | solution.py:27
  96.5 3.6 %collective-permute-start.13 = (bf16[3,256,256]{2,1,0:T(8,128)(2,1)S(1)}, bf16[3,256,256]{2,1,0:T(8,128)(2,1)S(1)}, u32[]{:S(2)}, u32[]{:S(2)}) collective-permute-start(bf16[3,256,256]{2,1,0:T(8,128)(2,1)S(1)} %add_convert_fusion.1), channel_id=1, source_target_pairs={{1,4},{4,1},{5,8},{8,5},{9,12},{12,9},{3,6},{6,3},{7,10},{10,7},{1... | collective-permute-start | bytes 1179656 | tf_op jit(solution)/shard_map/ppermute | solution.py:27
  100.2 5.4 %collective-permute-start.14 = (bf16[3,128,256]{2,1,0:T(8,128)(2,1)S(1)}, bf16[3,128,256]{2,1,0:T(8,128)(2,1)S(1)}, u32[]{:S(2)}, u32[]{:S(2)}) collective-permute-start(bf16[3,128,256]{2,1,0:T(8,128)(2,1)S(1)} %add_convert_fusion.2), channel_id=1, source_target_pairs={{1,4},{4,1},{5,8},{8,5},{9,12},{12,9},{3,6},{6,3},{7,10},{10,7},{1... | collective-permute-start | bytes 589832 | tf_op jit(solution)/shard_map/ppermute | solution.py:27
  114.4 3.3 %near_sweep.2.refs_6_ = f32[8,256,256]{2,1,0:T(8,128)S(1)} custom-call(s32[32]{0:T(128)S(1)} %reshape.63.at_ref, f32[32]{0:T(128)S(1)} %reshape.64.weight_ref, bf16[8,256,256]{2,1,0:T(8,128)(2,1)S(1)} %get-tuple-element.89.refs_0_, bf16[4,256,256]{2,1,0:T(8,128)(2,1)S(1)} %collective-permute-done.16.refs_1_, ...), custom_call_target="tpu_custom_call" | custom-call | flops 2097152 | bytes 16384 | tf_op jit(solution)/shard_map/near_sweep/pallas_call | solution.py:404
  117.7 4.0 %collective-permute-done.15.refs_2_ = bf16[8,256,256]{2,1,0:T(8,128)(2,1)S(1)} collective-permute-done((bf16[8,256,256]{2,1,0:T(8,128)(2,1)S(1)}, bf16[8,256,256]{2,1,0:T(8,128)(2,1)S(1)}, u32[]{:S(2)}, u32[]{:S(2)}) %collective-permute-start.15) | collective-permute-done | bytes 1048608 | tf_op jit(solution)/shard_map/ppermute | solution.py:27
  121.8 2.8 %far_sweep.2.refs_0_ = bf16[8,256,256]{2,1,0:T(8,128)(2,1)S(1)} custom-call(s32[32]{0:T(128)S(1)} %reshape.63.at_ref, f32[32]{0:T(128)S(1)} %reshape.64.weight_ref, s32[48]{0:T(128)S(1)} %concatenate.14.at_ref.refs_0_, bf16[8,256,256]{2,1,0:T(8,128)(2,1)S(1)} %get-tuple-element.87.refs_1_, bf16[8,256,256]{2,1,0:T(8,128)(2,1)S(1)} %collective-permute-done.15.refs_2_, ...), custom_call_target="tpu_custom_call" | custom-call | flops 2097152 | bytes 16384 | tf_op jit(solution)/shard_map/far_sweep/pallas_call | solution.py:458
  124.6 2.7 %collective-permute-start.18 = (bf16[8,256,256]{2,1,0:T(8,128)(2,1)S(1)}, bf16[8,256,256]{2,1,0:T(8,128)(2,1)S(1)}, u32[]{:S(2)}, u32[]{:S(2)}) collective-permute-start(bf16[8,256,256]{2,1,0:T(8,128)(2,1)S(1)} %far_sweep.2.refs_0_), channel_id=1, source_target_pairs={{1,4},{4,1},{5,8},{8,5},{9,12},{12,9},{3,6},{6,3},{7,10},{10,7},{1... | collective-permute-start | bytes 3145736 | tf_op jit(solution)/shard_map/ppermute | solution.py:27
  130.1 3.3 %near_sweep.3.refs_4_ = f32[8,256,256]{2,1,0:T(8,128)S(1)} custom-call(s32[32]{0:T(128)S(1)} %reshape.63.at_ref, f32[32]{0:T(128)S(1)} %reshape.64.weight_ref, bf16[8,256,256]{2,1,0:T(8,128)(2,1)S(1)} %far_sweep.2.refs_0_, bf16[4,256,256]{2,1,0:T(8,128)(2,1)S(1)} %collective-permute-done.19.refs_1_, ...), custom_call_target="tpu_custom_call" | custom-call | flops 2097152 | bytes 16384 | tf_op jit(solution)/shard_map/near_sweep/pallas_call | solution.py:404
  133.4 7.3 %collective-permute-done.18.refs_0_ = bf16[8,256,256]{2,1,0:T(8,128)(2,1)S(1)} collective-permute-done((bf16[8,256,256]{2,1,0:T(8,128)(2,1)S(1)}, bf16[8,256,256]{2,1,0:T(8,128)(2,1)S(1)}, u32[]{:S(2)}, u32[]{:S(2)}) %collective-permute-start.18) | collective-permute-done | bytes 1048608 | tf_op jit(solution)/shard_map/ppermute | solution.py:27
  140.7 3.7 %far_sweep.3 = bf16[8,256,256]{2,1,0:T(8,128)(2,1)} custom-call(s32[32]{0:T(128)S(1)} %reshape.63.at_ref, f32[32]{0:T(128)S(1)} %reshape.64.weight_ref, bf16[8,256,256]{2,1,0:T(8,128)(2,1)S(1)} %collective-permute-done.18.refs_0_, bf16[8,4,256,256]{3,2,1,0:T(8,128)(2,1)S(1)} %compare_convert_fusion.1.refs_3_.refs_1_, ...), custom_call_target="tpu_custom_call" | custom-call | flops 2097152 | bytes 16384 | tf_op jit(solution)/shard_map/far_sweep/pallas_call | solution.py:458
  (117 shorter events, 38.7 us)
Async XLA Ops:
  0.0 22.7 %copy-start = (s32[24,256]{1,0:T(8,128)S(1)}, s32[24,256]{1,0:T(8,128)}, u32[]{:S(2)}) copy-start(s32[24,256]{1,0:T(8,128)} %param.11) | copy-start | bytes 73732
  2.5 20.2 %collective-permute-start = (bf16[5120,128]{1,0:T(8,128)(2,1)}, bf16[5120,128]{1,0:T(8,128)(2,1)}, u32[]{:S(2)}, u32[]{:S(2)}) collective-permute-start(bf16[5120,128]{1,0:T(8,128)(2,1)} %dynamic-slice_bitcast_fusion), channel_id=1, source_target_pairs={{1,4},{4,1},{5,8},{8,5},{9,12},{12,9},{3,6},{6,3},{7,10},{10,7},{1... | collective-permute-start | bytes 3932168 | tf_op jit(solution)/shard_map/ppermute | solution.py:27
  14.8 11.3 %collective-permute-start.1 = (bf16[5120,256]{1,0:T(8,128)(2,1)}, bf16[5120,256]{1,0:T(8,128)(2,1)S(1)}, u32[]{:S(2)}, u32[]{:S(2)}) collective-permute-start(bf16[5120,256]{1,0:T(8,128)(2,1)} %get-tuple-element.60), channel_id=1, source_target_pairs={{0,1},{1,0},{2,3},{3,2},{4,5},{5,4},{6,7},{7,6},{8,9},{9,8},{10,11... | collective-permute-start | bytes 7864328 | tf_op jit(solution)/shard_map/ppermute | solution.py:19
  14.8 36.1 %collective-permute-start.5 = (bf16[5120,256]{1,0:T(8,128)(2,1)}, bf16[5120,256]{1,0:T(8,128)(2,1)}, u32[]{:S(2)}, u32[]{:S(2)}) collective-permute-start(bf16[5120,256]{1,0:T(8,128)(2,1)} %get-tuple-element.60), channel_id=1, source_target_pairs={{1,4},{4,1},{5,8},{8,5},{9,12},{12,9},{3,6},{6,3},{7,10},{10,7},{1... | collective-permute-start | bytes 7864328 | tf_op jit(solution)/shard_map/ppermute | solution.py:27
  18.6 7.6 %collective-permute-start.2 = (bf16[5120,256]{1,0:T(8,128)(2,1)}, bf16[5120,256]{1,0:T(8,128)(2,1)}, u32[]{:S(2)}, u32[]{:S(2)}) collective-permute-start(bf16[5120,256]{1,0:T(8,128)(2,1)} %get-tuple-element.61), channel_id=1, source_target_pairs={{0,1},{1,0},{2,3},{3,2},{4,5},{5,4},{6,7},{7,6},{8,9},{9,8},{10,11... | collective-permute-start | bytes 7864328 | tf_op jit(solution)/shard_map/ppermute | solution.py:19
  18.7 9.0 %collective-permute-start.3 = (bf16[5120,256]{1,0:T(8,128)(2,1)}, bf16[5120,256]{1,0:T(8,128)(2,1)}, u32[]{:S(2)}, u32[]{:S(2)}) collective-permute-start(bf16[5120,256]{1,0:T(8,128)(2,1)} %get-tuple-element.62), channel_id=1, source_target_pairs={{0,1},{1,0},{2,3},{3,2},{4,5},{5,4},{6,7},{7,6},{8,9},{9,8},{10,11... | collective-permute-start | bytes 7864328 | tf_op jit(solution)/shard_map/ppermute | solution.py:19
  39.6 5.2 %collective-permute-start.4 = (bf16[3,768,256]{2,1,0:T(8,128)(2,1)}, bf16[3,768,256]{2,1,0:T(8,128)(2,1)S(1)}, u32[]{:S(2)}, u32[]{:S(2)}) collective-permute-start(bf16[3,768,256]{2,1,0:T(8,128)(2,1)} %get-tuple-element.64.sent_ref), channel_id=1, source_target_pairs={{0,1},{1,0},{2,3},{3,2},{4,5},{5,4},{6,7},{7,6},{8,9},{9,8},{10,11... | collective-permute-start | bytes 3538952 | tf_op jit(solution)/shard_map/ppermute | solution.py:19
  39.8 39.2 %collective-permute-start.7 = (bf16[5120,256]{1,0:T(8,128)(2,1)}, bf16[5120,256]{1,0:T(8,128)(2,1)}, u32[]{:S(2)}, u32[]{:S(2)}) collective-permute-start(bf16[5120,256]{1,0:T(8,128)(2,1)} %get-tuple-element.61), channel_id=1, source_target_pairs={{1,4},{4,1},{5,8},{8,5},{9,12},{12,9},{3,6},{6,3},{7,10},{10,7},{1... | collective-permute-start | bytes 7864328 | tf_op jit(solution)/shard_map/ppermute | solution.py:27
  46.8 32.3 %collective-permute-start.6 = (bf16[8,256,256]{2,1,0:T(8,128)(2,1)S(1)}, bf16[8,256,256]{2,1,0:T(8,128)(2,1)S(1)}, u32[]{:S(2)}, u32[]{:S(2)}) collective-permute-start(bf16[8,256,256]{2,1,0:T(8,128)(2,1)S(1)} %local_integrals.1.part_ref), channel_id=1, source_target_pairs={{0,2},{2,0},{1,3},{3,1},{4,6},{6,4},{5,7},{7,5},{8,10},{10,8},{9,1... | collective-permute-start | bytes 3145736 | tf_op jit(solution)/shard_map/ppermute | solution.py:34
  67.0 26.1 %slice-start = ((s8[7864320]{0:T(1024)(128)(4,1)}), s8[4194304]{0:T(1024)(128)(4,1)S(1)}, s32[]{:S(2)}) async-start(s8[7864320]{0:T(1024)(128)(4,1)} %bitcast.41), calls=%async_computation | async-start | bytes 8388608
  67.0 26.1 %slice-start.1 = ((s8[7864320]{0:T(1024)(128)(4,1)}), s8[3670016]{0:T(1024)(128)(4,1)S(1)}, s32[]{:S(2)}) async-start(s8[7864320]{0:T(1024)(128)(4,1)} %bitcast.41), calls=%async_computation.1 | async-start | bytes 7340032
  67.0 26.1 %collective-permute-start.8 = (bf16[5120,128]{1,0:T(8,128)(2,1)S(1)}, bf16[5120,128]{1,0:T(8,128)(2,1)S(1)}, u32[]{:S(2)}, u32[]{:S(2)}) collective-permute-start(bf16[5120,128]{1,0:T(8,128)(2,1)S(1)} %copy-done.5), channel_id=1, source_target_pairs={{1,4},{4,1},{5,8},{8,5},{9,12},{12,9},{3,6},{6,3},{7,10},{10,7},{1... | collective-permute-start | bytes 3932168 | tf_op jit(solution)/shard_map/ppermute | solution.py:27
  70.7 15.5 %collective-permute-start.9 = (bf16[3,384,256]{2,1,0:T(8,128)(2,1)S(1)}, bf16[3,384,256]{2,1,0:T(8,128)(2,1)S(1)}, u32[]{:S(2)}, u32[]{:S(2)}) collective-permute-start(bf16[3,384,256]{2,1,0:T(8,128)(2,1)S(1)} %line_products.3.refs_0_), channel_id=1, source_target_pairs={{0,2},{2,0},{1,3},{3,1},{4,6},{6,4},{5,7},{7,5},{8,10},{10,8},{9,1... | collective-permute-start | bytes 1769480 | tf_op jit(solution)/shard_map/ppermute | solution.py:34
  83.3 13.1 %collective-permute-start.10 = (bf16[3,256,256]{2,1,0:T(8,128)(2,1)S(1)}, bf16[3,256,256]{2,1,0:T(8,128)(2,1)S(1)}, u32[]{:S(2)}, u32[]{:S(2)}) collective-permute-start(bf16[3,256,256]{2,1,0:T(8,128)(2,1)S(1)} %line_products.4.refs_1_), channel_id=1, source_target_pairs={{0,2},{2,0},{1,3},{3,1},{4,6},{6,4},{5,7},{7,5},{8,10},{10,8},{9,1... | collective-permute-start | bytes 1179656 | tf_op jit(solution)/shard_map/ppermute | solution.py:34
  86.4 13.8 %collective-permute-start.12 = (bf16[3,384,256]{2,1,0:T(8,128)(2,1)S(1)}, bf16[3,384,256]{2,1,0:T(8,128)(2,1)S(1)}, u32[]{:S(2)}, u32[]{:S(2)}) collective-permute-start(bf16[3,384,256]{2,1,0:T(8,128)(2,1)S(1)} %add_convert_fusion), channel_id=1, source_target_pairs={{1,4},{4,1},{5,8},{8,5},{9,12},{12,9},{3,6},{6,3},{7,10},{10,7},{1... | collective-permute-start | bytes 1769480 | tf_op jit(solution)/shard_map/ppermute | solution.py:27
  95.1 5.0 %collective-permute-start.11 = (bf16[3,128,256]{2,1,0:T(8,128)(2,1)S(1)}, bf16[3,128,256]{2,1,0:T(8,128)(2,1)S(1)}, u32[]{:S(2)}, u32[]{:S(2)}) collective-permute-start(bf16[3,128,256]{2,1,0:T(8,128)(2,1)S(1)} %line_products.5.refs_2_), channel_id=1, source_target_pairs={{0,2},{2,0},{1,3},{3,1},{4,6},{6,4},{5,7},{7,5},{8,10},{10,8},{9,1... | collective-permute-start | bytes 589832 | tf_op jit(solution)/shard_map/ppermute | solution.py:34
  96.5 12.5 %collective-permute-start.13 = (bf16[3,256,256]{2,1,0:T(8,128)(2,1)S(1)}, bf16[3,256,256]{2,1,0:T(8,128)(2,1)S(1)}, u32[]{:S(2)}, u32[]{:S(2)}) collective-permute-start(bf16[3,256,256]{2,1,0:T(8,128)(2,1)S(1)} %add_convert_fusion.1), channel_id=1, source_target_pairs={{1,4},{4,1},{5,8},{8,5},{9,12},{12,9},{3,6},{6,3},{7,10},{10,7},{1... | collective-permute-start | bytes 1179656 | tf_op jit(solution)/shard_map/ppermute | solution.py:27
  100.2 8.8 %collective-permute-start.14 = (bf16[3,128,256]{2,1,0:T(8,128)(2,1)S(1)}, bf16[3,128,256]{2,1,0:T(8,128)(2,1)S(1)}, u32[]{:S(2)}, u32[]{:S(2)}) collective-permute-start(bf16[3,128,256]{2,1,0:T(8,128)(2,1)S(1)} %add_convert_fusion.2), channel_id=1, source_target_pairs={{1,4},{4,1},{5,8},{8,5},{9,12},{12,9},{3,6},{6,3},{7,10},{10,7},{1... | collective-permute-start | bytes 589832 | tf_op jit(solution)/shard_map/ppermute | solution.py:27
  105.6 16.1 %collective-permute-start.15 = (bf16[8,256,256]{2,1,0:T(8,128)(2,1)S(1)}, bf16[8,256,256]{2,1,0:T(8,128)(2,1)S(1)}, u32[]{:S(2)}, u32[]{:S(2)}) collective-permute-start(bf16[8,256,256]{2,1,0:T(8,128)(2,1)S(1)} %multiply_convert_fusion), channel_id=1, source_target_pairs={{1,4},{4,1},{5,8},{8,5},{9,12},{12,9},{3,6},{6,3},{7,10},{10,7},{1... | collective-permute-start | bytes 3145736 | tf_op jit(solution)/shard_map/ppermute | solution.py:27
  111.5 2.9 %collective-permute-start.16 = (bf16[4,256,256]{2,1,0:T(8,128)(2,1)S(1)}, bf16[4,256,256]{2,1,0:T(8,128)(2,1)S(1)}, u32[]{:S(2)}, u32[]{:S(2)}) collective-permute-start(bf16[4,256,256]{2,1,0:T(8,128)(2,1)S(1)} %get-tuple-element.100), channel_id=1, source_target_pairs={{0,1},{1,0},{2,3},{3,2},{4,5},{5,4},{6,7},{7,6},{8,9},{9,8},{10,11... | collective-permute-start | bytes 1572872 | tf_op jit(solution)/shard_map/ppermute | solution.py:19
  111.6 2.8 %collective-permute-start.17 = (bf16[4,256,256]{2,1,0:T(8,128)(2,1)S(1)}, bf16[4,256,256]{2,1,0:T(8,128)(2,1)S(1)}, u32[]{:S(2)}, u32[]{:S(2)}) collective-permute-start(bf16[4,256,256]{2,1,0:T(8,128)(2,1)S(1)} %get-tuple-element.99), channel_id=1, source_target_pairs={{0,1},{1,0},{2,3},{3,2},{4,5},{5,4},{6,7},{7,6},{8,9},{9,8},{10,11... | collective-permute-start | bytes 1572872 | tf_op jit(solution)/shard_map/ppermute | solution.py:19
  124.6 16.1 %collective-permute-start.18 = (bf16[8,256,256]{2,1,0:T(8,128)(2,1)S(1)}, bf16[8,256,256]{2,1,0:T(8,128)(2,1)S(1)}, u32[]{:S(2)}, u32[]{:S(2)}) collective-permute-start(bf16[8,256,256]{2,1,0:T(8,128)(2,1)S(1)} %far_sweep.2.refs_0_), channel_id=1, source_target_pairs={{1,4},{4,1},{5,8},{8,5},{9,12},{12,9},{3,6},{6,3},{7,10},{10,7},{1... | collective-permute-start | bytes 3145736 | tf_op jit(solution)/shard_map/ppermute | solution.py:27
  127.3 2.0 %collective-permute-start.19 = (bf16[4,256,256]{2,1,0:T(8,128)(2,1)S(1)}, bf16[4,256,256]{2,1,0:T(8,128)(2,1)S(1)}, u32[]{:S(2)}, u32[]{:S(2)}) collective-permute-start(bf16[4,256,256]{2,1,0:T(8,128)(2,1)S(1)} %get-tuple-element.98), channel_id=1, source_target_pairs={{0,1},{1,0},{2,3},{3,2},{4,5},{5,4},{6,7},{7,6},{8,9},{9,8},{10,11... | collective-permute-start | bytes 1572872 | tf_op jit(solution)/shard_map/ppermute | solution.py:19
  127.4 2.6 %collective-permute-start.20 = (bf16[4,256,256]{2,1,0:T(8,128)(2,1)S(1)}, bf16[4,256,256]{2,1,0:T(8,128)(2,1)S(1)}, u32[]{:S(2)}, u32[]{:S(2)}) collective-permute-start(bf16[4,256,256]{2,1,0:T(8,128)(2,1)S(1)} %get-tuple-element.97), channel_id=1, source_target_pairs={{0,1},{1,0},{2,3},{3,2},{4,5},{5,4},{6,7},{7,6},{8,9},{9,8},{10,11... | collective-permute-start | bytes 1572872 | tf_op jit(solution)/shard_map/ppermute | solution.py:19
  (11 other events, 93.9 us)

commit v7 on v6

--- a/solution.py
+++ b/solution.py
@@ -427,7 +427,7 @@
         list_ref[found] = k
         return found + jnp.where(at_ref[k] >= 2 * slots, 1, 0)
 
-    found = lax.fori_loop(0, slots * neighbours, enlist, 0)
+    found = lax.fori_loop(0, slots * neighbours, enlist, 0, unroll=True)
 
     def product(k):
         slot, n = k // neighbours, k % neighbours

time: 145 us -> 145 us (level)
  no operation moved by 1% of the time
where the time goes in v7:
time: 145 us; the launch traced here: 144 us
  Pallas kernels  49 us (34%)
  starting transfers between devices  38.8 us (27%)
  waiting for transfers between devices  35.6 us (25%)
  local copies, waits for them, and re-layouts  14.9 us (10%)
  other arithmetic  5 us (3%)
    ppermute x9, starting transfers between devices, line_mate(): return lax.ppermute(value, LINE, pairs)  31.8 us
    ppermute x9, waiting for transfers between devices, line_mate(): return lax.ppermute(value, LINE, pairs)  30.3 us
    pallas_call x1, Pallas kernels, chip_products(): pl.pallas_call(functools.partial(chip_kernel, n), in_specs=in_smem(1) + [...  11.9 us
    pallas_call x3, Pallas kernels, line_products(): pl.pallas_call(functools.partial(line_kernel, n), in_specs=in_vmem(1) + [...  11.5 us
    pallas_call x2, Pallas kernels, near_sweep(): pl.pallas_call(near_kernel, in_specs=in_smem(2) + in_vmem(4 + len(parts))...  6.57 us
    pallas_call x2, Pallas kernels, far_sweep(): pl.pallas_call(functools.partial(far_kernel, bool(patch)), in_specs=in_sm...  6.03 us
    pallas_call x1, Pallas kernels, send_blocks(): pl.pallas_call(send_kernel, in_specs=in_smem(1) + [anywhere], out_specs=[...  5.73 us
    unnamed x28, local copies, waits for them, and re-layouts  5.24 us
  transfers between devices with their start and end apart: 21, of which 11 were waited for; matrix products, arithmetic and copies ran while one was open for 8% of the time, Pallas kernels for 30%

profile of v7, /device:TPU:1, one launch (start us, length us, event | category | flops | bytes accessed | tf_op | source)
XLA Modules:
  0.0 143.9 jit_solution(4559893488565021385)
XLA Ops:
  0.0 2.5 %dynamic-slice_bitcast_fusion = bf16[5120,128]{1,0:T(8,128)(2,1)} fusion(bf16[3,10240,256]{2,1,0:T(8,128)(2,1)} %blocks_ref.1, s32[]{:T(128)S(6)} %select_n.116), kind=kLoop, calls=%fused_computation.12 | loop fusion | bytes 2621444 | tf_op jit(solution)/shard_map/squeeze | solution.py:482
  2.5 4.6 %collective-permute-start = (bf16[5120,128]{1,0:T(8,128)(2,1)}, bf16[5120,128]{1,0:T(8,128)(2,1)}, u32[]{:S(2)}, u32[]{:S(2)}) collective-permute-start(bf16[5120,128]{1,0:T(8,128)(2,1)} %dynamic-slice_bitcast_fusion), channel_id=1, source_target_pairs={{1,4},{4,1},{5,8},{8,5},{9,12},{12,9},{3,6},{6,3},{7,10},{10,7},{1... | collective-permute-start | bytes 3932168 | tf_op jit(solution)/shard_map/ppermute | solution.py:27
  7.1 5.7 %send_blocks.1 = (bf16[5120,256]{1,0:T(8,128)(2,1)}, bf16[5120,256]{1,0:T(8,128)(2,1)}, bf16[5120,256]{1,0:T(8,128)(2,1)}, bf16[5120,128]{1,0:T(8,128)(2,1)S(1)}, f32[3,256,256]{2,1,0:T(8,128)S(1)}) custom-call(s32[1]{0:T(128)S(6)} %sub.53.half_ref, bf16[3,10240,256]{2,1,0:T(8,128)(2,1)} %blocks_ref.1), custom_call_target="tpu_custom_call" | custom-call | flops 1966080 | bytes 15360 | tf_op jit(solution)/shard_map/send_blocks/pallas_call | solution.py:122
  14.8 3.8 %collective-permute-start.5 = (bf16[5120,256]{1,0:T(8,128)(2,1)}, bf16[5120,256]{1,0:T(8,128)(2,1)}, u32[]{:S(2)}, u32[]{:S(2)}) collective-permute-start(bf16[5120,256]{1,0:T(8,128)(2,1)} %get-tuple-element.60), channel_id=1, source_target_pairs={{1,4},{4,1},{5,8},{8,5},{9,12},{12,9},{3,6},{6,3},{7,10},{10,7},{1... | collective-permute-start | bytes 7864328 | tf_op jit(solution)/shard_map/ppermute | solution.py:27
  19.2 3.5 %collective-permute-done.refs_0_ = bf16[5120,128]{1,0:T(8,128)(2,1)} collective-permute-done((bf16[5120,128]{1,0:T(8,128)(2,1)}, bf16[5120,128]{1,0:T(8,128)(2,1)}, u32[]{:S(2)}, u32[]{:S(2)}) %collective-permute-start) | collective-permute-done | bytes 1310752 | tf_op jit(solution)/shard_map/ppermute | solution.py:27
  22.9 3.2 %energies_of.1 = f32[9,256]{1,0:T(8,128)S(1)} custom-call(f32[1792]{0:T(1024)S(1)} %copy-done.6, s32[9,256]{1,0:T(8,128)S(1)} %constant_dynamic-slice_fusion.3.dom_ref), custom_call_target="tpu_custom_call" | custom-call | flops 60000002048 | tf_op jit(solution)/shard_map/energies_of/pallas_call | solution.py:370
  27.7 11.9 %chip_products.1 = (bf16[3,768,256]{2,1,0:T(8,128)(2,1)}, f32[3,256,256]{2,1,0:T(8,128)S(1)}, bf16[3,5120,256]{2,1,0:T(8,128)(2,1)}) custom-call(s32[1]{0:T(128)} %bitcast.half_ref, bf16[3,10240,256]{2,1,0:T(8,128)(2,1)} %blocks_ref.1, bf16[5120,256]{1,0:T(8,128)(2,1)S(1)} %collective-permute-done.1.refs_0_, ...), custom_call_target="tpu_custom_call" | custom-call | flops 5898240 | bytes 15360 | tf_op jit(solution)/shard_map/chip_products/pallas_call | solution.py:174
  39.8 3.7 %collective-permute-start.7 = (bf16[5120,256]{1,0:T(8,128)(2,1)}, bf16[5120,256]{1,0:T(8,128)(2,1)}, u32[]{:S(2)}, u32[]{:S(2)}) collective-permute-start(bf16[5120,256]{1,0:T(8,128)(2,1)} %get-tuple-element.61), channel_id=1, source_target_pairs={{1,4},{4,1},{5,8},{8,5},{9,12},{12,9},{3,6},{6,3},{7,10},{10,7},{1... | collective-permute-start | bytes 7864328 | tf_op jit(solution)/shard_map/ppermute | solution.py:27
  48.2 2.8 %collective-permute-done.5.refs_1_ = bf16[5120,256]{1,0:T(8,128)(2,1)} collective-permute-done((bf16[5120,256]{1,0:T(8,128)(2,1)}, bf16[5120,256]{1,0:T(8,128)(2,1)}, u32[]{:S(2)}, u32[]{:S(2)}) %collective-permute-start.5) | collective-permute-done | bytes 2621472 | tf_op jit(solution)/shard_map/ppermute | solution.py:27
  58.5 3.2 %copy-done.1 = bf16[3,5120,256]{2,1,0:T(8,128)(2,1)S(1)} copy-done((bf16[3,5120,256]{2,1,0:T(8,128)(2,1)S(1)}, bf16[3,5120,256]{2,1,0:T(8,128)(2,1)}, u32[]{:S(2)}) %copy-start.1) | copy-done | bytes 7864344
  61.7 5.3 %line_products.3.refs_0_ = bf16[3,384,256]{2,1,0:T(8,128)(2,1)S(1)} custom-call(bf16[3,5120,256]{2,1,0:T(8,128)(2,1)S(1)} %copy-done.1, bf16[5120,128]{1,0:T(8,128)(2,1)} %collective-permute-done.refs_0_, bf16[5120,256]{1,0:T(8,128)(2,1)} %collective-permute-done.5.refs_1_), custom_call_target="tpu_custom_call" | custom-call | flops 2949120 | bytes 11520 | tf_op jit(solution)/shard_map/line_products/pallas_call | solution.py:223
  67.0 3.7 %collective-permute-start.8 = (bf16[5120,128]{1,0:T(8,128)(2,1)S(1)}, bf16[5120,128]{1,0:T(8,128)(2,1)S(1)}, u32[]{:S(2)}, u32[]{:S(2)}) collective-permute-start(bf16[5120,128]{1,0:T(8,128)(2,1)S(1)} %copy-done.5), channel_id=1, source_target_pairs={{1,4},{4,1},{5,8},{8,5},{9,12},{12,9},{3,6},{6,3},{7,10},{10,7},{1... | collective-permute-start | bytes 3932168 | tf_op jit(solution)/shard_map/ppermute | solution.py:27
  72.0 7.0 %collective-permute-done.7.refs_0_ = bf16[5120,256]{1,0:T(8,128)(2,1)} collective-permute-done((bf16[5120,256]{1,0:T(8,128)(2,1)}, bf16[5120,256]{1,0:T(8,128)(2,1)}, u32[]{:S(2)}, u32[]{:S(2)}) %collective-permute-start.7) | collective-permute-done | bytes 2621472 | tf_op jit(solution)/shard_map/ppermute | solution.py:27
  79.0 4.3 %line_products.4.refs_1_ = bf16[3,256,256]{2,1,0:T(8,128)(2,1)S(1)} custom-call(bf16[3,5120,256]{2,1,0:T(8,128)(2,1)S(1)} %copy-done.1, bf16[5120,256]{1,0:T(8,128)(2,1)} %collective-permute-done.7.refs_0_), custom_call_target="tpu_custom_call" | custom-call | flops 1966080 | bytes 10240 | tf_op jit(solution)/shard_map/line_products/pallas_call | solution.py:223
  86.4 2.7 %collective-permute-start.12 = (bf16[3,384,256]{2,1,0:T(8,128)(2,1)S(1)}, bf16[3,384,256]{2,1,0:T(8,128)(2,1)S(1)}, u32[]{:S(2)}, u32[]{:S(2)}) collective-permute-start(bf16[3,384,256]{2,1,0:T(8,128)(2,1)S(1)} %add_convert_fusion), channel_id=1, source_target_pairs={{1,4},{4,1},{5,8},{8,5},{9,12},{12,9},{3,6},{6,3},{7,10},{10,7},{1... | collective-permute-start | bytes 1769480 | tf_op jit(solution)/shard_map/ppermute | solution.py:27
  89.7 3.3 %collective-permute-done.8.refs_0_ = bf16[5120,128]{1,0:T(8,128)(2,1)S(1)} collective-permute-done((bf16[5120,128]{1,0:T(8,128)(2,1)S(1)}, bf16[5120,128]{1,0:T(8,128)(2,1)S(1)}, u32[]{:S(2)}, u32[]{:S(2)}) %collective-permute-start.8) | collective-permute-done | bytes 1310752 | tf_op jit(solution)/shard_map/ppermute | solution.py:27
  96.5 3.6 %collective-permute-start.13 = (bf16[3,256,256]{2,1,0:T(8,128)(2,1)S(1)}, bf16[3,256,256]{2,1,0:T(8,128)(2,1)S(1)}, u32[]{:S(2)}, u32[]{:S(2)}) collective-permute-start(bf16[3,256,256]{2,1,0:T(8,128)(2,1)S(1)} %add_convert_fusion.1), channel_id=1, source_target_pairs={{1,4},{4,1},{5,8},{8,5},{9,12},{12,9},{3,6},{6,3},{7,10},{10,7},{1... | collective-permute-start | bytes 1179656 | tf_op jit(solution)/shard_map/ppermute | solution.py:27
  100.2 5.4 %collective-permute-start.14 = (bf16[3,128,256]{2,1,0:T(8,128)(2,1)S(1)}, bf16[3,128,256]{2,1,0:T(8,128)(2,1)S(1)}, u32[]{:S(2)}, u32[]{:S(2)}) collective-permute-start(bf16[3,128,256]{2,1,0:T(8,128)(2,1)S(1)} %add_convert_fusion.2), channel_id=1, source_target_pairs={{1,4},{4,1},{5,8},{8,5},{9,12},{12,9},{3,6},{6,3},{7,10},{10,7},{1... | collective-permute-start | bytes 589832 | tf_op jit(solution)/shard_map/ppermute | solution.py:27
  113.9 3.3 %near_sweep.2.refs_6_ = f32[8,256,256]{2,1,0:T(8,128)S(1)} custom-call(s32[32]{0:T(128)S(1)} %reshape.63.at_ref, f32[32]{0:T(128)S(1)} %reshape.64.weight_ref, bf16[8,256,256]{2,1,0:T(8,128)(2,1)S(1)} %get-tuple-element.89.refs_0_, bf16[4,256,256]{2,1,0:T(8,128)(2,1)S(1)} %collective-permute-done.16.refs_1_, ...), custom_call_target="tpu_custom_call" | custom-call | flops 2097152 | bytes 16384 | tf_op jit(solution)/shard_map/near_sweep/pallas_call | solution.py:404
  117.2 4.6 %collective-permute-done.15.refs_2_ = bf16[8,256,256]{2,1,0:T(8,128)(2,1)S(1)} collective-permute-done((bf16[8,256,256]{2,1,0:T(8,128)(2,1)S(1)}, bf16[8,256,256]{2,1,0:T(8,128)(2,1)S(1)}, u32[]{:S(2)}, u32[]{:S(2)}) %collective-permute-start.15) | collective-permute-done | bytes 1048608 | tf_op jit(solution)/shard_map/ppermute | solution.py:27
  121.8 2.6 %far_sweep.2.refs_0_ = bf16[8,256,256]{2,1,0:T(8,128)(2,1)S(1)} custom-call(s32[32]{0:T(128)S(1)} %reshape.63.at_ref, f32[32]{0:T(128)S(1)} %reshape.64.weight_ref, s32[48]{0:T(128)S(1)} %concatenate.14.at_ref.refs_0_, bf16[8,256,256]{2,1,0:T(8,128)(2,1)S(1)} %get-tuple-element.87.refs_1_, bf16[8,256,256]{2,1,0:T(8,128)(2,1)S(1)} %collective-permute-done.15.refs_2_, ...), custom_call_target="tpu_custom_call" | custom-call | flops 2097152 | bytes 16384 | tf_op jit(solution)/shard_map/far_sweep/pallas_call | solution.py:458
  129.2 3.3 %near_sweep.3.refs_4_ = f32[8,256,256]{2,1,0:T(8,128)S(1)} custom-call(s32[32]{0:T(128)S(1)} %reshape.63.at_ref, f32[32]{0:T(128)S(1)} %reshape.64.weight_ref, bf16[8,256,256]{2,1,0:T(8,128)(2,1)S(1)} %far_sweep.2.refs_0_, bf16[4,256,256]{2,1,0:T(8,128)(2,1)S(1)} %collective-permute-done.19.refs_1_, ...), custom_call_target="tpu_custom_call" | custom-call | flops 2097152 | bytes 16384 | tf_op jit(solution)/shard_map/near_sweep/pallas_call | solution.py:404
  132.5 7.9 %collective-permute-done.18.refs_0_ = bf16[8,256,256]{2,1,0:T(8,128)(2,1)S(1)} collective-permute-done((bf16[8,256,256]{2,1,0:T(8,128)(2,1)S(1)}, bf16[8,256,256]{2,1,0:T(8,128)(2,1)S(1)}, u32[]{:S(2)}, u32[]{:S(2)}) %collective-permute-start.18) | collective-permute-done | bytes 1048608 | tf_op jit(solution)/shard_map/ppermute | solution.py:27
  140.5 3.5 %far_sweep.3 = bf16[8,256,256]{2,1,0:T(8,128)(2,1)} custom-call(s32[32]{0:T(128)S(1)} %reshape.63.at_ref, f32[32]{0:T(128)S(1)} %reshape.64.weight_ref, bf16[8,256,256]{2,1,0:T(8,128)(2,1)S(1)} %collective-permute-done.18.refs_0_, bf16[8,4,256,256]{3,2,1,0:T(8,128)(2,1)S(1)} %compare_convert_fusion.1.refs_3_.refs_1_, ...), custom_call_target="tpu_custom_call" | custom-call | flops 2097152 | bytes 16384 | tf_op jit(solution)/shard_map/far_sweep/pallas_call | solution.py:458
  (117 shorter events, 37.9 us)
Async XLA Ops:
  0.0 22.7 %copy-start = (s32[24,256]{1,0:T(8,128)S(1)}, s32[24,256]{1,0:T(8,128)}, u32[]{:S(2)}) copy-start(s32[24,256]{1,0:T(8,128)} %param.11) | copy-start | bytes 73732
  2.5 20.2 %collective-permute-start = (bf16[5120,128]{1,0:T(8,128)(2,1)}, bf16[5120,128]{1,0:T(8,128)(2,1)}, u32[]{:S(2)}, u32[]{:S(2)}) collective-permute-start(bf16[5120,128]{1,0:T(8,128)(2,1)} %dynamic-slice_bitcast_fusion), channel_id=1, source_target_pairs={{1,4},{4,1},{5,8},{8,5},{9,12},{12,9},{3,6},{6,3},{7,10},{10,7},{1... | collective-permute-start | bytes 3932168 | tf_op jit(solution)/shard_map/ppermute | solution.py:27
  14.8 11.3 %collective-permute-start.1 = (bf16[5120,256]{1,0:T(8,128)(2,1)}, bf16[5120,256]{1,0:T(8,128)(2,1)S(1)}, u32[]{:S(2)}, u32[]{:S(2)}) collective-permute-start(bf16[5120,256]{1,0:T(8,128)(2,1)} %get-tuple-element.60), channel_id=1, source_target_pairs={{0,1},{1,0},{2,3},{3,2},{4,5},{5,4},{6,7},{7,6},{8,9},{9,8},{10,11... | collective-permute-start | bytes 7864328 | tf_op jit(solution)/shard_map/ppermute | solution.py:19
  14.8 36.1 %collective-permute-start.5 = (bf16[5120,256]{1,0:T(8,128)(2,1)}, bf16[5120,256]{1,0:T(8,128)(2,1)}, u32[]{:S(2)}, u32[]{:S(2)}) collective-permute-start(bf16[5120,256]{1,0:T(8,128)(2,1)} %get-tuple-element.60), channel_id=1, source_target_pairs={{1,4},{4,1},{5,8},{8,5},{9,12},{12,9},{3,6},{6,3},{7,10},{10,7},{1... | collective-permute-start | bytes 7864328 | tf_op jit(solution)/shard_map/ppermute | solution.py:27
  18.6 7.6 %collective-permute-start.2 = (bf16[5120,256]{1,0:T(8,128)(2,1)}, bf16[5120,256]{1,0:T(8,128)(2,1)}, u32[]{:S(2)}, u32[]{:S(2)}) collective-permute-start(bf16[5120,256]{1,0:T(8,128)(2,1)} %get-tuple-element.61), channel_id=1, source_target_pairs={{0,1},{1,0},{2,3},{3,2},{4,5},{5,4},{6,7},{7,6},{8,9},{9,8},{10,11... | collective-permute-start | bytes 7864328 | tf_op jit(solution)/shard_map/ppermute | solution.py:19
  18.7 9.0 %collective-permute-start.3 = (bf16[5120,256]{1,0:T(8,128)(2,1)}, bf16[5120,256]{1,0:T(8,128)(2,1)}, u32[]{:S(2)}, u32[]{:S(2)}) collective-permute-start(bf16[5120,256]{1,0:T(8,128)(2,1)} %get-tuple-element.62), channel_id=1, source_target_pairs={{0,1},{1,0},{2,3},{3,2},{4,5},{5,4},{6,7},{7,6},{8,9},{9,8},{10,11... | collective-permute-start | bytes 7864328 | tf_op jit(solution)/shard_map/ppermute | solution.py:19
  39.6 5.2 %collective-permute-start.4 = (bf16[3,768,256]{2,1,0:T(8,128)(2,1)}, bf16[3,768,256]{2,1,0:T(8,128)(2,1)S(1)}, u32[]{:S(2)}, u32[]{:S(2)}) collective-permute-start(bf16[3,768,256]{2,1,0:T(8,128)(2,1)} %get-tuple-element.64.sent_ref), channel_id=1, source_target_pairs={{0,1},{1,0},{2,3},{3,2},{4,5},{5,4},{6,7},{7,6},{8,9},{9,8},{10,11... | collective-permute-start | bytes 3538952 | tf_op jit(solution)/shard_map/ppermute | solution.py:19
  39.8 39.2 %collective-permute-start.7 = (bf16[5120,256]{1,0:T(8,128)(2,1)}, bf16[5120,256]{1,0:T(8,128)(2,1)}, u32[]{:S(2)}, u32[]{:S(2)}) collective-permute-start(bf16[5120,256]{1,0:T(8,128)(2,1)} %get-tuple-element.61), channel_id=1, source_target_pairs={{1,4},{4,1},{5,8},{8,5},{9,12},{12,9},{3,6},{6,3},{7,10},{10,7},{1... | collective-permute-start | bytes 7864328 | tf_op jit(solution)/shard_map/ppermute | solution.py:27
  46.9 32.1 %collective-permute-start.6 = (bf16[8,256,256]{2,1,0:T(8,128)(2,1)S(1)}, bf16[8,256,256]{2,1,0:T(8,128)(2,1)S(1)}, u32[]{:S(2)}, u32[]{:S(2)}) collective-permute-start(bf16[8,256,256]{2,1,0:T(8,128)(2,1)S(1)} %local_integrals.1.part_ref), channel_id=1, source_target_pairs={{0,2},{2,0},{1,3},{3,1},{4,6},{6,4},{5,7},{7,5},{8,10},{10,8},{9,1... | collective-permute-start | bytes 3145736 | tf_op jit(solution)/shard_map/ppermute | solution.py:34
  67.0 26.1 %slice-start = ((s8[7864320]{0:T(1024)(128)(4,1)}), s8[4194304]{0:T(1024)(128)(4,1)S(1)}, s32[]{:S(2)}) async-start(s8[7864320]{0:T(1024)(128)(4,1)} %bitcast.41), calls=%async_computation | async-start | bytes 8388608
  67.0 26.1 %slice-start.1 = ((s8[7864320]{0:T(1024)(128)(4,1)}), s8[3670016]{0:T(1024)(128)(4,1)S(1)}, s32[]{:S(2)}) async-start(s8[7864320]{0:T(1024)(128)(4,1)} %bitcast.41), calls=%async_computation.1 | async-start | bytes 7340032
  67.0 26.1 %collective-permute-start.8 = (bf16[5120,128]{1,0:T(8,128)(2,1)S(1)}, bf16[5120,128]{1,0:T(8,128)(2,1)S(1)}, u32[]{:S(2)}, u32[]{:S(2)}) collective-permute-start(bf16[5120,128]{1,0:T(8,128)(2,1)S(1)} %copy-done.5), channel_id=1, source_target_pairs={{1,4},{4,1},{5,8},{8,5},{9,12},{12,9},{3,6},{6,3},{7,10},{10,7},{1... | collective-permute-start | bytes 3932168 | tf_op jit(solution)/shard_map/ppermute | solution.py:27
  70.7 15.5 %collective-permute-start.9 = (bf16[3,384,256]{2,1,0:T(8,128)(2,1)S(1)}, bf16[3,384,256]{2,1,0:T(8,128)(2,1)S(1)}, u32[]{:S(2)}, u32[]{:S(2)}) collective-permute-start(bf16[3,384,256]{2,1,0:T(8,128)(2,1)S(1)} %line_products.3.refs_0_), channel_id=1, source_target_pairs={{0,2},{2,0},{1,3},{3,1},{4,6},{6,4},{5,7},{7,5},{8,10},{10,8},{9,1... | collective-permute-start | bytes 1769480 | tf_op jit(solution)/shard_map/ppermute | solution.py:34
  83.3 13.1 %collective-permute-start.10 = (bf16[3,256,256]{2,1,0:T(8,128)(2,1)S(1)}, bf16[3,256,256]{2,1,0:T(8,128)(2,1)S(1)}, u32[]{:S(2)}, u32[]{:S(2)}) collective-permute-start(bf16[3,256,256]{2,1,0:T(8,128)(2,1)S(1)} %line_products.4.refs_1_), channel_id=1, source_target_pairs={{0,2},{2,0},{1,3},{3,1},{4,6},{6,4},{5,7},{7,5},{8,10},{10,8},{9,1... | collective-permute-start | bytes 1179656 | tf_op jit(solution)/shard_map/ppermute | solution.py:34
  86.4 13.8 %collective-permute-start.12 = (bf16[3,384,256]{2,1,0:T(8,128)(2,1)S(1)}, bf16[3,384,256]{2,1,0:T(8,128)(2,1)S(1)}, u32[]{:S(2)}, u32[]{:S(2)}) collective-permute-start(bf16[3,384,256]{2,1,0:T(8,128)(2,1)S(1)} %add_convert_fusion), channel_id=1, source_target_pairs={{1,4},{4,1},{5,8},{8,5},{9,12},{12,9},{3,6},{6,3},{7,10},{10,7},{1... | collective-permute-start | bytes 1769480 | tf_op jit(solution)/shard_map/ppermute | solution.py:27
  95.1 5.0 %collective-permute-start.11 = (bf16[3,128,256]{2,1,0:T(8,128)(2,1)S(1)}, bf16[3,128,256]{2,1,0:T(8,128)(2,1)S(1)}, u32[]{:S(2)}, u32[]{:S(2)}) collective-permute-start(bf16[3,128,256]{2,1,0:T(8,128)(2,1)S(1)} %line_products.5.refs_2_), channel_id=1, source_target_pairs={{0,2},{2,0},{1,3},{3,1},{4,6},{6,4},{5,7},{7,5},{8,10},{10,8},{9,1... | collective-permute-start | bytes 589832 | tf_op jit(solution)/shard_map/ppermute | solution.py:34
  96.5 12.5 %collective-permute-start.13 = (bf16[3,256,256]{2,1,0:T(8,128)(2,1)S(1)}, bf16[3,256,256]{2,1,0:T(8,128)(2,1)S(1)}, u32[]{:S(2)}, u32[]{:S(2)}) collective-permute-start(bf16[3,256,256]{2,1,0:T(8,128)(2,1)S(1)} %add_convert_fusion.1), channel_id=1, source_target_pairs={{1,4},{4,1},{5,8},{8,5},{9,12},{12,9},{3,6},{6,3},{7,10},{10,7},{1... | collective-permute-start | bytes 1179656 | tf_op jit(solution)/shard_map/ppermute | solution.py:27
  100.2 8.8 %collective-permute-start.14 = (bf16[3,128,256]{2,1,0:T(8,128)(2,1)S(1)}, bf16[3,128,256]{2,1,0:T(8,128)(2,1)S(1)}, u32[]{:S(2)}, u32[]{:S(2)}) collective-permute-start(bf16[3,128,256]{2,1,0:T(8,128)(2,1)S(1)} %add_convert_fusion.2), channel_id=1, source_target_pairs={{1,4},{4,1},{5,8},{8,5},{9,12},{12,9},{3,6},{6,3},{7,10},{10,7},{1... | collective-permute-start | bytes 589832 | tf_op jit(solution)/shard_map/ppermute | solution.py:27
  105.6 16.1 %collective-permute-start.15 = (bf16[8,256,256]{2,1,0:T(8,128)(2,1)S(1)}, bf16[8,256,256]{2,1,0:T(8,128)(2,1)S(1)}, u32[]{:S(2)}, u32[]{:S(2)}) collective-permute-start(bf16[8,256,256]{2,1,0:T(8,128)(2,1)S(1)} %multiply_convert_fusion), channel_id=1, source_target_pairs={{1,4},{4,1},{5,8},{8,5},{9,12},{12,9},{3,6},{6,3},{7,10},{10,7},{1... | collective-permute-start | bytes 3145736 | tf_op jit(solution)/shard_map/ppermute | solution.py:27
  111.0 2.9 %collective-permute-start.16 = (bf16[4,256,256]{2,1,0:T(8,128)(2,1)S(1)}, bf16[4,256,256]{2,1,0:T(8,128)(2,1)S(1)}, u32[]{:S(2)}, u32[]{:S(2)}) collective-permute-start(bf16[4,256,256]{2,1,0:T(8,128)(2,1)S(1)} %get-tuple-element.100), channel_id=1, source_target_pairs={{0,1},{1,0},{2,3},{3,2},{4,5},{5,4},{6,7},{7,6},{8,9},{9,8},{10,11... | collective-permute-start | bytes 1572872 | tf_op jit(solution)/shard_map/ppermute | solution.py:19
  111.1 2.8 %collective-permute-start.17 = (bf16[4,256,256]{2,1,0:T(8,128)(2,1)S(1)}, bf16[4,256,256]{2,1,0:T(8,128)(2,1)S(1)}, u32[]{:S(2)}, u32[]{:S(2)}) collective-permute-start(bf16[4,256,256]{2,1,0:T(8,128)(2,1)S(1)} %get-tuple-element.99), channel_id=1, source_target_pairs={{0,1},{1,0},{2,3},{3,2},{4,5},{5,4},{6,7},{7,6},{8,9},{9,8},{10,11... | collective-permute-start | bytes 1572872 | tf_op jit(solution)/shard_map/ppermute | solution.py:19
  124.3 16.1 %collective-permute-start.18 = (bf16[8,256,256]{2,1,0:T(8,128)(2,1)S(1)}, bf16[8,256,256]{2,1,0:T(8,128)(2,1)S(1)}, u32[]{:S(2)}, u32[]{:S(2)}) collective-permute-start(bf16[8,256,256]{2,1,0:T(8,128)(2,1)S(1)} %far_sweep.2.refs_0_), channel_id=1, source_target_pairs={{1,4},{4,1},{5,8},{8,5},{9,12},{12,9},{3,6},{6,3},{7,10},{10,7},{1... | collective-permute-start | bytes 3145736 | tf_op jit(solution)/shard_map/ppermute | solution.py:27
  126.5 2.0 %collective-permute-start.19 = (bf16[4,256,256]{2,1,0:T(8,128)(2,1)S(1)}, bf16[4,256,256]{2,1,0:T(8,128)(2,1)S(1)}, u32[]{:S(2)}, u32[]{:S(2)}) collective-permute-start(bf16[4,256,256]{2,1,0:T(8,128)(2,1)S(1)} %get-tuple-element.98), channel_id=1, source_target_pairs={{0,1},{1,0},{2,3},{3,2},{4,5},{5,4},{6,7},{7,6},{8,9},{9,8},{10,11... | collective-permute-start | bytes 1572872 | tf_op jit(solution)/shard_map/ppermute | solution.py:19
  126.6 2.6 %collective-permute-start.20 = (bf16[4,256,256]{2,1,0:T(8,128)(2,1)S(1)}, bf16[4,256,256]{2,1,0:T(8,128)(2,1)S(1)}, u32[]{:S(2)}, u32[]{:S(2)}) collective-permute-start(bf16[4,256,256]{2,1,0:T(8,128)(2,1)S(1)} %get-tuple-element.97), channel_id=1, source_target_pairs={{0,1},{1,0},{2,3},{3,2},{4,5},{5,4},{6,7},{7,6},{8,9},{9,8},{10,11... | collective-permute-start | bytes 1572872 | tf_op jit(solution)/shard_map/ppermute | solution.py:19
  (11 other events, 93.9 us)
